TPU v7x, 32 devices: a whole 2x2x4 slice. The times are simulated.
32 devices in a mesh: dp: 8 (over y, x, core), seq: 4 (over z).
Axes of the slice: x: 2, y: 2, z: 4, core: 2. Of those that a mesh axis runs over, the one named last changes fastest.
Arguments:
- layer_in: bfloat16 [32, 1024, 768], P('dp', 'seq'), may hold values from -6 to 6
- out_grad: bfloat16 [32, 1024, 768], P('dp', 'seq'), may hold values from -6 to 6
- norm_gain: float32 [768], P(('dp', 'seq')), may hold values from 0.1 to 1.9
- in_weight: float32 [768, 3352], P(('dp', 'seq')), may hold values from -0.21875 to 0.21875
- conv_params: float32 [5, 1792], P(None, ('dp', 'seq')), may hold values from -3 to 3
- gate_gain: float32 [1536], P(('dp', 'seq')), may hold values from 0.1 to 1.9
- out_weight: float32 [1536, 768], P(('dp', 'seq')), may hold values from -0.15625 to 0.15625
- head_params: float32 [3, 24], replicated, may hold values from -7 to 2.5, as said below
- norm_first: float32 [768], P(('dp', 'seq')), may hold values from -384 to 384
- norm_second: float32 [768], P(('dp', 'seq')), may hold values from 39321.6 to 163840
- in_first: float32 [768, 3352], P(('dp', 'seq')), may hold values from -192 to 192
- in_second: float32 [768, 3352], P(('dp', 'seq')), may hold values from 9830.4 to 40960
- conv_first: float32 [5, 1792], P(None, ('dp', 'seq')), may hold values from -192 to 192
- conv_second: float32 [5, 1792], P(None, ('dp', 'seq')), may hold values from 9830.4 to 40960
- gate_first: float32 [1536], P(('dp', 'seq')), may hold values from -256 to 256
- gate_second: float32 [1536], P(('dp', 'seq')), may hold values from 19660.8 to 81920
- out_first: float32 [1536, 768], P(('dp', 'seq')), may hold values from -384 to 384
- out_second: float32 [1536, 768], P(('dp', 'seq')), may hold values from 39321.6 to 163840
- head_first: float32 [3, 24], replicated, may hold values from -1280 to 1280
- head_second: float32 [3, 24], replicated, may hold values from 655360 to 2621440
- step_count: int32 [1], replicated, may hold values from 1 to 3
- hyper: float32 [4], replicated, may hold values from 0.01 to 0.8, as said below
Outputs:
- layer_out: bfloat16 [32, 1024, 768], P('dp', 'seq')
- in_grad: float32 [32, 1024, 768], P('dp', 'seq')
- norm_step: float32 [768], P(('dp', 'seq'))
- norm_first_new: float32 [768], P(('dp', 'seq'))
- norm_second_new: float32 [768], P(('dp', 'seq'))
- in_new: float32 [768, 3352], P(('dp', 'seq'))
- in_first_new: float32 [768, 3352], P(('dp', 'seq'))
- in_second_new: float32 [768, 3352], P(('dp', 'seq'))
- conv_step: float32 [5, 1792], P(None, ('dp', 'seq'))
- conv_first_new: float32 [5, 1792], P(None, ('dp', 'seq'))
- conv_second_new: float32 [5, 1792], P(None, ('dp', 'seq'))
- gate_step: float32 [1536], P(('dp', 'seq'))
- gate_first_new: float32 [1536], P(('dp', 'seq'))
- gate_second_new: float32 [1536], P(('dp', 'seq'))
- out_new: float32 [1536, 768], P(('dp', 'seq'))
- out_first_new: float32 [1536, 768], P(('dp', 'seq'))
- out_second_new: float32 [1536, 768], P(('dp', 'seq'))
- head_step: float32 [3, 24], replicated
- head_first_new: float32 [3, 24], replicated
- head_second_new: float32 [3, 24], replicated
- in_copy: bfloat16 [768, 3352], P(('dp', 'seq'))
- out_copy: bfloat16 [1536, 768], P(('dp', 'seq'))
Inputs may be any that keep to these rules, and one draw needn't show every extreme that they name: `head_params`: rows: step bias in -7 to -3, log of the decay rate in 0 to 2.5, skip gain in -1 to 1. `hyper`: learning rate 0.01 to 0.03, beta one 0.7 to 0.8, beta two 0.4 to 0.5, weight decay 0.05 to 0.2.
All inputs are finite; a program needn't handle non-finite values.
Results may differ from a plain program's by a relative error of at most 0.012.
The roundings to bfloat16 on the way count: a program that leaves them out, or rounds other values in their place, can miss the bound.
Values may be sent and summed in bfloat16 or wider, within the bound.
No kernel may reach another device: no remote copies, remote signals or barrier semaphores. Data moves between devices by JAX's collectives and lax.ppermute only.
A program may use at most 192 MiB of HBM per device.

v0:
```python
from functools import partial

import jax
import jax.numpy as jnp
from jax import lax
from jax.sharding import PartitionSpec as P

norm_eps = 1e-05
adam_eps = 1e-08
highest = lax.Precision.HIGHEST


def from_behind(block, axis, distance):
    devices = range(lax.axis_size(axis))
    route = [(i - distance, i) for i in devices if i - distance in devices]
    return lax.ppermute(block, axis, route)


def as_sent(shard):

    def short(part):
        return part.astype(jnp.bfloat16) if part.dtype == jnp.float32 else part

    return jax.tree.map(short, shard)


def exact_dot(left, right):
    return jnp.dot(left, right, precision=highest, preferred_element_type=jnp.float32)


def spread_heads(decay, width):
    return jnp.repeat(decay, width // decay.shape[-1], axis=-1)[..., None]


def conv_silu(extended, conv):
    tap_count = conv.shape[0] - 1
    out_rows = extended.shape[-2] - (tap_count - 1)
    summed = conv[tap_count]
    for offset in range(tap_count):
        summed = summed + conv[offset] * extended[..., offset : offset + out_rows, :]
    return jax.nn.silu(summed)


def group_local(mixed, dt_raw, head, inner_dim):
    state_dim = (mixed.shape[-1] - inner_dim) // 2
    value_rows = mixed[:, :inner_dim]
    key_rows = mixed[:, inner_dim : inner_dim + state_dim]
    query_rows = mixed[:, inner_dim + state_dim :]
    dt_steps = jax.nn.softplus(dt_raw + head[0])
    log_decay = dt_steps * -jnp.exp(head[1])
    length = mixed.shape[0]
    lower_mask = (jnp.arange(length)[:, None] >= jnp.arange(length)[None, :]).astype(jnp.float32)
    cum_decay = exact_dot(lower_mask, log_decay)
    return (value_rows, key_rows, query_rows, dt_steps, cum_decay)


def group_state(value_rows, key_rows, dt_steps, cum_decay):
    head_size = value_rows.shape[1] // dt_steps.shape[1]
    tail_weight = jnp.exp(cum_decay[-1][None, :] - cum_decay) * dt_steps
    weighted = value_rows * jnp.repeat(tail_weight, head_size, axis=1)
    state_loc = exact_dot(weighted.T, key_rows)
    return (state_loc, jnp.exp(cum_decay[-1]))


def group_tail(
    value_rows, key_rows, query_rows, dt_steps, cum_decay, state_in, gate_rows, head, gate_gain
):
    length, inner_dim = value_rows.shape
    head_count = dt_steps.shape[1]
    head_size = inner_dim // head_count
    scores = exact_dot(query_rows, key_rows.T)
    lower_mask = jnp.arange(length)[:, None] >= jnp.arange(length)[None, :]
    cum_heads = cum_decay.T
    decay_gaps = cum_heads[:, :, None] - cum_heads[:, None, :]
    zero_gap = jnp.zeros_like(decay_gaps)
    decays = jnp.where(lower_mask, jnp.exp(jnp.where(lower_mask, decay_gaps, zero_gap)), zero_gap)
    mixing = decays * scores[None] * dt_steps.T[:, None, :]
    per_head = value_rows.reshape(length, head_count, head_size)
    diag_out = jnp.einsum("hts,shp->thp", mixing, per_head, precision=highest).reshape(
        length, inner_dim
    )
    carried = exact_dot(query_rows, state_in.T) * jnp.repeat(jnp.exp(cum_decay), head_size, axis=1)
    skip_out = value_rows * jnp.repeat(head[2], head_size)
    mixed_out = diag_out + carried + skip_out
    gated_rows = mixed_out * jax.nn.silu(gate_rows)
    inv_rms = lax.rsqrt(jnp.mean(gated_rows * gated_rows, axis=-1, keepdims=True) + norm_eps)
    return gated_rows * inv_rms * gate_gain


def front_part(extended, dt_raw, conv, head, inner_dim):
    mixed = conv_silu(extended, conv)
    value_rows, key_rows, query_rows, dt_steps, cum_decay = group_local(
        mixed, dt_raw, head, inner_dim
    )
    state_loc, decay_tot = group_state(value_rows, key_rows, dt_steps, cum_decay)
    return (value_rows, key_rows, query_rows, dt_steps, cum_decay, state_loc, decay_tot)


def pre_norm(token_rows, gain):
    return (
        token_rows
        * lax.rsqrt(jnp.mean(token_rows * token_rows, axis=-1, keepdims=True) + norm_eps)
        * gain
    )


def adam_update(master, grad_sum, first_moment, second_moment, step_count, hyper):
    learn_rate, beta_one, beta_two, decay_rate = (hyper[0], hyper[1], hyper[2], hyper[3])
    step_float = step_count[0].astype(jnp.float32)
    new_first = beta_one * first_moment + (1.0 - beta_one) * grad_sum
    new_second = beta_two * second_moment + (1.0 - beta_two) * grad_sum * grad_sum
    first_hat = new_first / (1.0 - beta_one**step_float)
    second_hat = new_second / (1.0 - beta_two**step_float)
    change = -learn_rate * (first_hat / (jnp.sqrt(second_hat) + adam_eps) + decay_rate * master)
    return (master + change, change, new_first, new_second)


def local(
    layer_in,
    out_grad,
    norm_gain,
    in_weight,
    conv_params,
    gate_gain,
    out_weight,
    head_params,
    norm_first,
    norm_second,
    in_first,
    in_second,
    conv_first,
    conv_second,
    gate_first,
    gate_second,
    out_first,
    out_second,
    head_first,
    head_second,
    step_count,
    hyper,
):
    seq_count, length, width = layer_in.shape
    norm_low = norm_gain.astype(jnp.bfloat16)
    in_low = in_weight.astype(jnp.bfloat16)
    conv_low = conv_params.astype(jnp.bfloat16)
    gate_low = gate_gain.astype(jnp.bfloat16)
    out_low_w = out_weight.astype(jnp.bfloat16)
    gathered = (
        lax.all_gather(norm_low, ("dp", "seq"), axis=0, tiled=True),
        lax.all_gather(in_low, ("dp", "seq"), axis=0, tiled=True),
        lax.all_gather(conv_low, ("dp", "seq"), axis=1, tiled=True),
        lax.all_gather(gate_low, ("dp", "seq"), axis=0, tiled=True),
        lax.all_gather(out_low_w, ("dp", "seq"), axis=0, tiled=True),
    )
    norm_full, in_full, conv_full, gate_full, out_full = gathered
    inner_dim = gate_full.shape[0]
    conv_dim = conv_full.shape[1]
    tap_count = conv_full.shape[0] - 1
    edge_count = tap_count - 1
    rows_all = seq_count * length
    tokens = layer_in.reshape(rows_all, width).astype(jnp.float32)
    normed = pre_norm(tokens, norm_full.astype(jnp.float32)).astype(jnp.bfloat16)
    gate_part = jnp.dot(normed, in_full[:, :inner_dim], preferred_element_type=jnp.float32)
    conv_input = jnp.dot(
        normed, in_full[:, inner_dim : inner_dim + conv_dim], preferred_element_type=jnp.float32
    ).reshape(seq_count, length, conv_dim)
    dt_raw = jnp.dot(
        normed, in_full[:, inner_dim + conv_dim :], preferred_element_type=jnp.float32
    ).reshape(seq_count, length, -1)
    edge_rows = from_behind(
        conv_input[:, length - edge_count :, :].astype(jnp.bfloat16), "seq", 1
    ).astype(jnp.float32)
    extended = jnp.concatenate([edge_rows, conv_input], axis=1)
    front_batch = jax.vmap(partial(front_part, inner_dim=inner_dim), in_axes=(0, 0, None, None))
    value_rows, key_rows, query_rows, dt_steps, cum_decay, state_loc, decay_tot = front_batch(
        extended, dt_raw, conv_full.astype(jnp.float32), head_params
    )

    def relay_forward(turn, carried):
        return from_behind(
            (spread_heads(decay_tot, inner_dim) * carried + state_loc).astype(jnp.bfloat16),
            "seq",
            1,
        ).astype(jnp.float32)

    state_in = lax.fori_loop(0, lax.axis_size("seq") - 1, relay_forward, jnp.zeros_like(state_loc))
    gate_rows = gate_part.reshape(seq_count, length, inner_dim)
    gate_exact = gate_full.astype(jnp.float32)

    def tail_step(items):
        return group_tail(
            items[0],
            items[1],
            items[2],
            items[3],
            items[4],
            items[5],
            items[6],
            head_params,
            gate_exact,
        )

    normed_out = lax.map(
        tail_step, (value_rows, key_rows, query_rows, dt_steps, cum_decay, state_in, gate_rows)
    )
    out_rows = normed_out.reshape(rows_all, inner_dim).astype(jnp.bfloat16)
    layer_out = (
        (tokens + jnp.dot(out_rows, out_full, preferred_element_type=jnp.float32))
        .astype(jnp.bfloat16)
        .reshape(seq_count, length, width)
    )
    back_full = (
        lax.all_gather(norm_low, ("dp", "seq"), axis=0, tiled=True),
        lax.all_gather(in_low, ("dp", "seq"), axis=0, tiled=True),
        lax.all_gather(conv_low, ("dp", "seq"), axis=1, tiled=True),
        lax.all_gather(gate_low, ("dp", "seq"), axis=0, tiled=True),
        lax.all_gather(out_low_w, ("dp", "seq"), axis=0, tiled=True),
    )
    norm_back, in_back, conv_back, gate_back, out_back = back_full
    gate_back_exact = gate_back.astype(jnp.float32)
    cot_rows = out_grad.reshape(rows_all, width)
    d_out_weight = jnp.dot(out_rows.T, cot_rows, preferred_element_type=jnp.float32)
    d_normed_out = jnp.dot(cot_rows, out_back.T, preferred_element_type=jnp.float32).reshape(
        seq_count, length, inner_dim
    )

    def tail_grads(items):
        _, pull_tail = jax.vjp(
            group_tail,
            items[0],
            items[1],
            items[2],
            items[3],
            items[4],
            items[5],
            items[6],
            head_params,
            gate_back_exact,
        )
        return pull_tail(items[7])

    tail_out = lax.map(
        tail_grads,
        (value_rows, key_rows, query_rows, dt_steps, cum_decay, state_in, gate_rows, d_normed_out),
    )
    (
        d_values,
        d_keys,
        d_queries,
        d_dt_steps,
        d_cum,
        d_state_in,
        d_gate_rows,
        d_head_tail,
        d_gate_tail,
    ) = tail_out
    d_gate_gain = jnp.sum(d_gate_tail, axis=0)

    def relay_backward(turn, carried):
        return from_behind(
            (spread_heads(decay_tot, inner_dim) * carried + d_state_in).astype(jnp.bfloat16),
            "seq",
            -1,
        ).astype(jnp.float32)

    state_grad = lax.fori_loop(
        0, lax.axis_size("seq") - 1, relay_backward, jnp.zeros_like(d_state_in)
    )
    head_count = decay_tot.shape[1]
    d_decay = (
        jnp.sum(state_grad * state_in, axis=-1)
        .reshape(seq_count, head_count, inner_dim // head_count)
        .sum(axis=-1)
    )
    _, pull_front = jax.vjp(
        front_batch, extended, dt_raw, conv_back.astype(jnp.float32), head_params
    )
    d_extended, d_dt_raw, d_conv, d_head_front = pull_front(
        (d_values, d_keys, d_queries, d_dt_steps, d_cum, state_grad, d_decay)
    )
    incoming = from_behind(as_sent(d_extended[:, :edge_count, :]), "seq", -1)
    d_conv_own = d_extended[:, edge_count:, :]
    d_conv_input = jnp.concatenate(
        [
            d_conv_own[:, : length - edge_count, :],
            d_conv_own[:, length - edge_count :, :] + incoming,
        ],
        axis=1,
    )
    d_gate_low = d_gate_rows.reshape(rows_all, inner_dim).astype(jnp.bfloat16)
    d_conv_low = d_conv_input.reshape(rows_all, conv_dim).astype(jnp.bfloat16)
    d_dt_low = d_dt_raw.reshape(rows_all, -1).astype(jnp.bfloat16)
    d_normed = jnp.dot(d_gate_low, in_back[:, :inner_dim].T, preferred_element_type=jnp.float32)
    d_normed = d_normed + jnp.dot(
        d_conv_low,
        in_back[:, inner_dim : inner_dim + conv_dim].T,
        preferred_element_type=jnp.float32,
    )
    d_normed = d_normed + jnp.dot(
        d_dt_low, in_back[:, inner_dim + conv_dim :].T, preferred_element_type=jnp.float32
    )
    d_in_weight = jnp.concatenate(
        [
            jnp.dot(normed.T, d_gate_low, preferred_element_type=jnp.float32),
            jnp.dot(normed.T, d_conv_low, preferred_element_type=jnp.float32),
            jnp.dot(normed.T, d_dt_low, preferred_element_type=jnp.float32),
        ],
        axis=1,
    )
    _, pull_norm = jax.vjp(pre_norm, tokens, norm_back.astype(jnp.float32))
    d_tokens, d_norm_gain = pull_norm(d_normed)
    in_grad = (cot_rows.astype(jnp.float32) + d_tokens).reshape(seq_count, length, width)
    owned = (
        lax.psum_scatter(d_norm_gain, ("dp", "seq"), scatter_dimension=0, tiled=True),
        lax.psum_scatter(d_in_weight, ("dp", "seq"), scatter_dimension=0, tiled=True),
        lax.psum_scatter(d_conv, ("dp", "seq"), scatter_dimension=1, tiled=True),
        lax.psum_scatter(d_gate_gain, ("dp", "seq"), scatter_dimension=0, tiled=True),
        lax.psum_scatter(d_out_weight, ("dp", "seq"), scatter_dimension=0, tiled=True),
    )
    head_grad = lax.psum(jnp.sum(d_head_tail, axis=0) + d_head_front, ("dp", "seq"))
    norm_upd = adam_update(norm_gain, owned[0], norm_first, norm_second, step_count, hyper)
    in_upd = adam_update(in_weight, owned[1], in_first, in_second, step_count, hyper)
    conv_upd = adam_update(conv_params, owned[2], conv_first, conv_second, step_count, hyper)
    gate_upd = adam_update(gate_gain, owned[3], gate_first, gate_second, step_count, hyper)
    out_upd = adam_update(out_weight, owned[4], out_first, out_second, step_count, hyper)
    head_upd = adam_update(head_params, head_grad, head_first, head_second, step_count, hyper)
    return (
        layer_out,
        in_grad,
        norm_upd[1],
        norm_upd[2],
        norm_upd[3],
        in_upd[0],
        in_upd[2],
        in_upd[3],
        conv_upd[1],
        conv_upd[2],
        conv_upd[3],
        gate_upd[1],
        gate_upd[2],
        gate_upd[3],
        out_upd[0],
        out_upd[2],
        out_upd[3],
        head_upd[1],
        head_upd[2],
        head_upd[3],
        in_upd[0].astype(jnp.bfloat16),
        out_upd[0].astype(jnp.bfloat16),
    )


def solution(mesh):
    in_specs = (
        P("dp", "seq", None),
        P("dp", "seq", None),
        P(("dp", "seq")),
        P(("dp", "seq"), None),
        P(None, ("dp", "seq")),
        P(("dp", "seq")),
        P(("dp", "seq"), None),
        P(),
        P(("dp", "seq")),
        P(("dp", "seq")),
        P(("dp", "seq"), None),
        P(("dp", "seq"), None),
        P(None, ("dp", "seq")),
        P(None, ("dp", "seq")),
        P(("dp", "seq")),
        P(("dp", "seq")),
        P(("dp", "seq"), None),
        P(("dp", "seq"), None),
        P(),
        P(),
        P(),
        P(),
    )
    out_specs = (
        P("dp", "seq", None),
        P("dp", "seq", None),
        P(("dp", "seq")),
        P(("dp", "seq")),
        P(("dp", "seq")),
        P(("dp", "seq"), None),
        P(("dp", "seq"), None),
        P(("dp", "seq"), None),
        P(None, ("dp", "seq")),
        P(None, ("dp", "seq")),
        P(None, ("dp", "seq")),
        P(("dp", "seq")),
        P(("dp", "seq")),
        P(("dp", "seq")),
        P(("dp", "seq"), None),
        P(("dp", "seq"), None),
        P(("dp", "seq"), None),
        P(),
        P(),
        P(),
        P(("dp", "seq"), None),
        P(("dp", "seq"), None),
    )
    return jax.shard_map(local, mesh=mesh, in_specs=in_specs, out_specs=out_specs, check_vma=False)
```

profile of v0, /device:TPU:0, one launch (start us, length us, event | category | flops | bytes accessed | tf_op | source)
XLA Modules:
  0.0 1345.0 jit_solution(4135530470580273622)
XLA Ops:
  10.7 42.4 %all-reduce.24 = (bf16[768]{0:T(1024)(128)(2,1)S(1)}, bf16[1536]{0:T(1024)(128)(2,1)S(1)}) all-reduce(bf16[768]{0:T(1024)(128)(2,1)S(1)} %dynamic-update-slice, bf16[1536]{0:T(1024)(128)(2,1)S(1)} %dynamic-update-slice.1), channel_id=1, replica_groups=mesh['dp'=8,'seq'=4] {'dp','seq'}, use_global_device_ids=true, to_apply=%add.17 | all-reduce | flops 2304 | bytes 9216
  53.9 66.9 %all-gather = bf16[32,56,5]{1,2,0:T(8,128)(2,1)S(1)} all-gather(bf16[1,56,5]{1,2,0:T(8,128)(2,1)S(1)} %convert_bitcast_fusion), channel_id=1, replica_groups=mesh['dp'=8,'seq'=4] {'dp','seq'}, dimensions={0}, use_global_device_ids=true | all-gather | bytes 18480 | tf_op jit(solution)/shard_map/all_gather | solution.py:151
  156.6 15.0 %fusion.106 = (f32[4,256,1792]{2,1,0:T(8,128)S(1)}, f32[4,256,1792]{2,1,0:T(8,128)}) fusion(f32[4,256,1792]{2,1,0:T(8,128)} %copy-done.8, f32[1792]{0:T(1024)S(1)} %get-tuple-element.475, f32[4,3,1792]{2,1,0:T(4,128)S(1)} %convert_element_type.136, f32[1792]{0:T(1024)S(1)} %get-tuple-element.476, f32[1792]{0:T(1024)S(1)} %get-tuple-element.477, ...), kind=kLoop, calls=%fused_computation.162 | loop fusion | flops 27525120 | bytes 22141952 | tf_op jit(solution)/shard_map/vmap(jit(silu))/mul | solution.py:41
  178.9 10.1 fusion.166
  195.6 115.4 %while.60 = (s32[]{:T(128)}, f32[4,1536,128]{2,1,0:T(8,128)}, f32[4,24]{1,0:T(4,128)S(1)}, f32[4,1536,128]{2,1,0:T(8,128)S(1)}, s32[]{:T(128)}, /*index=5*/s32[]{:T(128)}) while((s32[]{:T(128)}, f32[4,1536,128]{2,1,0:T(8,128)}, f32[4,24]{1,0:T(4,128)S(1)}, f32[4,1536,128]{2,1,0:T(8,128)S(1)}, s32[]{:T(128)}, ...), condition=%wide.region_2.3_spmd.clone, body=%wide.region_1.2_spmd.clone.sunk | while | flops 3932163 | bytes 18973176 | solution.py:186
  200.2 28.5 %collective-permute-done = bf16[4,1536,128]{2,1,0:T(8,128)(2,1)} collective-permute-done((bf16[4,1536,128]{2,1,0:T(8,128)(2,1)}, bf16[4,1536,128]{2,1,0:T(8,128)(2,1)}, u32[]{:S(2)}, u32[]{:S(2)}) %collective-permute-start) | collective-permute-done | bytes 1572896 | tf_op jit(solution)/shard_map/while/body/eval_jaxpr/ppermute | solution.py:16
  241.0 27.6 %collective-permute-done = bf16[4,1536,128]{2,1,0:T(8,128)(2,1)} collective-permute-done((bf16[4,1536,128]{2,1,0:T(8,128)(2,1)}, bf16[4,1536,128]{2,1,0:T(8,128)(2,1)}, u32[]{:S(2)}, u32[]{:S(2)}) %collective-permute-start) | collective-permute-done | bytes 1572896 | tf_op jit(solution)/shard_map/while/body/eval_jaxpr/ppermute | solution.py:16
  281.0 26.7 %collective-permute-done = bf16[4,1536,128]{2,1,0:T(8,128)(2,1)} collective-permute-done((bf16[4,1536,128]{2,1,0:T(8,128)(2,1)}, bf16[4,1536,128]{2,1,0:T(8,128)(2,1)}, u32[]{:S(2)}, u32[]{:S(2)}) %collective-permute-start) | collective-permute-done | bytes 1572896 | tf_op jit(solution)/shard_map/while/body/eval_jaxpr/ppermute | solution.py:16
  311.6 105.8 %while.58 = (s32[]{:T(128)}, bf16[4,256,1536]{2,1,0:T(8,128)(2,1)}, f32[4,256,1536]{1,2,0:T(8,128)}, f32[4,256,24]{1,2,0:T(8,128)S(1)}, f32[4,256,128]{2,1,0:T(8...) while((s32[]{:T(128)}, bf16[4,256,1536]{2,1,0:T(8,128)(2,1)}, ...), condition=%wide.region_5.6_spmd, body=%wide.region_3.5_spmd.sunk | while | flops 1925644544 | bytes 56032312 | solution.py:203
  318.4 8.5 fusion.252
  429.2 110.4 %reduce-scatter.6.cloned.1.call-done = f32[48,768]{1,0:T(8,128)} async-done(((f32[1536,768]{1,0:T(8,128)}), f32[48,768]{1,0:T(8,128)}) %reduce-scatter.6.cloned.1.call-update) | async-done | bytes 147472 | tf_op jit(solution)/shard_map/reduce_scatter | solution.py:318
  543.4 56.5 %all-gather.6.cloned.1.call-done = bf16[1536,768]{1,0:T(8,128)(2,1)} async-done(((bf16[48,768]{1,0:T(8,128)(2,1)}), bf16[1536,768]{1,0:T(8,128)(2,1)}) %all-gather.6.cloned.1.call-update) | async-done | bytes 2359312 | tf_op jit(solution)/shard_map/all_gather | solution.py:153
  609.4 337.5 %while.59 = (s32[]{:T(128)}, f32[4,256,1536]{2,1,0:T(8,128)}, f32[4,256,128]{2,1,0:T(8,128)}, f32[4,256,128]{2,1,0:T(8,128)}, f32[4,256,24]{1,2,0:T(8,128)}, /*i...) while((s32[]{:T(128)}, f32[4,256,1536]{2,1,0:T(8,128)}, ...), condition=%wide.region_17.18_spmd, body=%wide.region_6.17_spmd.sunk | while | flops 5796823040 | bytes 128158408 | solution.py:242
  619.7 10.1 fusion.270
  660.8 12.0 fusion.276
  703.9 10.1 fusion.270
  745.0 12.0 fusion.276
  788.1 10.1 fusion.270
  829.3 12.0 fusion.276
  872.4 10.1 fusion.270
  913.5 12.0 fusion.276
  947.0 130.0 %while.61 = (s32[]{:T(128)}, f32[4,1536,128]{2,1,0:T(8,128)}, f32[4,24]{1,0:T(4,128)}, f32[4,1536,128]{2,1,0:T(8,128)}, s32[]{:T(128)}, /*index=5*/s32[]{:T(128)}) while((s32[]{:T(128)}, f32[4,1536,128]{2,1,0:T(8,128)}, f32[4,24]{1,0:T(4,128)}, f32[4,1536,128]{2,1,0:T(8,128)}, s32[]{:T(128)}, /*index=5*/s32[]{:T(128)}) %tuple.186), condition=%wide.region_19.20_spmd.clone, body=%wide.region_18.19_spmd.clone.sunk | while | flops 3932163 | bytes 18973176 | solution.py:266
  951.5 37.2 %collective-permute-done.1 = bf16[4,1536,128]{2,1,0:T(8,128)(2,1)S(1)} collective-permute-done((bf16[4,1536,128]{2,1,0:T(8,128)(2,1)S(1)}, bf16[4,1536,128]{2,1,0:T(8,128)(2,1)S(1)}, u32[]{:S(2)}, u32[]{:S(2)}) %collective-permute-start.1) | collective-permute-done | bytes 1572896 | tf_op jit(solution)/shard_map/while/body/eval_jaxpr/ppermute | solution.py:16
  996.0 36.3 %collective-permute-done.1 = bf16[4,1536,128]{2,1,0:T(8,128)(2,1)S(1)} collective-permute-done((bf16[4,1536,128]{2,1,0:T(8,128)(2,1)S(1)}, bf16[4,1536,128]{2,1,0:T(8,128)(2,1)S(1)}, u32[]{:S(2)}, u32[]{:S(2)}) %collective-permute-start.1) | collective-permute-done | bytes 1572896 | tf_op jit(solution)/shard_map/while/body/eval_jaxpr/ppermute | solution.py:16
  1039.7 35.4 %collective-permute-done.1 = bf16[4,1536,128]{2,1,0:T(8,128)(2,1)S(1)} collective-permute-done((bf16[4,1536,128]{2,1,0:T(8,128)(2,1)S(1)}, bf16[4,1536,128]{2,1,0:T(8,128)(2,1)S(1)}, u32[]{:S(2)}, u32[]{:S(2)}) %collective-permute-start.1) | collective-permute-done | bytes 1572896 | tf_op jit(solution)/shard_map/while/body/eval_jaxpr/ppermute | solution.py:16
  1080.8 10.6 convolution_add_fusion.1
  1091.5 11.1 multiply_add_fusion.2
  1129.2 17.8 %multiply_reduce_fusion.7 = (f32[1792]{0:T(1024)S(1)}, f32[1792]{0:T(1024)S(1)}, f32[1792]{0:T(1024)S(1)}, f32[1792]{0:T(1024)S(1)}, f32[1792]{0:T(1024)S(1)}, /*index=5*/f32[4,256,1792]{2,1,0:T(8,128)S(1)}) fusion(f32[4,256,1792]{2,1,0:T(8,128)} %copy-done.8, f32[4,3,1792]{2,1,0:T(4,128)S(1)} %copy-done.39, f32[4,256,1792]{2,1,0:T(8,128)} %get-tuple-element.592, ...), kind=kLoop, calls=%fused_computation.159 | loop fusion | flops 42196224 | bytes 29481984 | tf_op jit(solution)/shard_map/transpose(jvp(vmap()))/reduce_sum | solution.py:40
  1154.8 11.8 pad_add_fusion
  1183.7 8.7 pad_maximum_fusion
  1210.9 41.6 %all-reduce.23 = (f32[768]{0:T(1024)S(1)}, f32[5,1792]{1,0:T(8,128)S(1)}, f32[1536]{0:T(1024)S(1)}, f32[3,24]{1,0:T(4,128)S(1)}) all-reduce(f32[768]{0:T(1024)S(1)} %get-tuple-element.472, f32[5,1792]{1,0:T(8,128)S(1)} %pad_add_fusion.1, f32[1536]{0:T(1024)S(1)} %reduce_sum.285, ...), channel_id=2, replica_groups=mesh['dp'=8,'seq'=4] {'dp','seq'}, use_global_device_ids=true, to_apply=%region_26.27.clone | all-reduce | flops 11336 | bytes 90688
  1267.0 67.1 %reduce-scatter.8.cloned.1.call-done = f32[24,3352]{1,0:T(8,128)} async-done(((f32[768,3352]{1,0:T(8,128)}), f32[24,3352]{1,0:T(8,128)}) %reduce-scatter.8.cloned.1.call-update) | async-done | bytes 321808
  (672 shorter events, 565.1 us)
Async XLA Ops:
  7.2 118.6 %all-gather.4.cloned.1.call-start = ((), (), s32[]{:S(2)}) async-start(), calls=%async_computation.2 | async-start | bytes 5474304 | tf_op jit(solution)/shard_map/all_gather | solution.py:150
  8.9 530.7 %reduce-scatter.6.cloned.1.call-start = ((), (), s32[]{:S(2)}) async-start(), calls=%async_computation.4 | async-start | bytes 4866048 | tf_op jit(solution)/shard_map/reduce_scatter | solution.py:318
  53.2 85.3 %copy-start.40 = (f32[768]{0:T(1024)}, f32[768]{0:T(1024)S(1)}, u32[]{:S(2)}) copy-start(f32[768]{0:T(1024)S(1)} %convert_element_type.133) | copy-start | bytes 9220
  124.0 32.6 %copy-start.57 = (f32[1792]{0:T(1024)}, f32[1792]{0:T(1024)S(1)}, u32[]{:S(2)}) copy-start(f32[1792]{0:T(1024)S(1)} %get-tuple-element.475) | copy-start | bytes 21508
  135.5 20.3 %collective-permute-start.2 = (bf16[4,3,1792]{2,1,0:T(4,128)(2,1)S(1)}, bf16[4,3,1792]{2,1,0:T(4,128)(2,1)}, u32[]{:S(2)}, u32[]{:S(2)}) collective-permute-start(bf16[4,3,1792]{2,1,0:T(4,128)(2,1)S(1)} %slice.242), channel_id=1, source_target_pairs={{0,1},{1,2},{2,3},{4,5},{5,6},{6,7},{8,9},{9,10},{10,11},{12,13},{... | collective-permute-start | bytes 129032 | tf_op jit(solution)/shard_map/ppermute | solution.py:16
  197.6 31.1 %collective-permute-start = (bf16[4,1536,128]{2,1,0:T(8,128)(2,1)}, bf16[4,1536,128]{2,1,0:T(8,128)(2,1)}, u32[]{:S(2)}, u32[]{:S(2)}) collective-permute-start(bf16[4,1536,128]{2,1,0:T(8,128)(2,1)} %fusion.281), channel_id=1, source_target_pairs={{0,1},{1,2},{2,3},{4,5},{5,6},{6,7},{8,9},{9,10},{10,11},{12,13},{... | collective-permute-start | bytes 4718600 | tf_op jit(solution)/shard_map/while/body/eval_jaxpr/ppermute | solution.py:16
  235.4 33.2 %collective-permute-start = (bf16[4,1536,128]{2,1,0:T(8,128)(2,1)}, bf16[4,1536,128]{2,1,0:T(8,128)(2,1)}, u32[]{:S(2)}, u32[]{:S(2)}) collective-permute-start(bf16[4,1536,128]{2,1,0:T(8,128)(2,1)} %fusion.281), channel_id=1, source_target_pairs={{0,1},{1,2},{2,3},{4,5},{5,6},{6,7},{8,9},{9,10},{10,11},{12,13},{... | collective-permute-start | bytes 4718600 | tf_op jit(solution)/shard_map/while/body/eval_jaxpr/ppermute | solution.py:16
  275.4 32.3 %collective-permute-start = (bf16[4,1536,128]{2,1,0:T(8,128)(2,1)}, bf16[4,1536,128]{2,1,0:T(8,128)(2,1)}, u32[]{:S(2)}, u32[]{:S(2)}) collective-permute-start(bf16[4,1536,128]{2,1,0:T(8,128)(2,1)} %fusion.281), channel_id=1, source_target_pairs={{0,1},{1,2},{2,3},{4,5},{5,6},{6,7},{8,9},{9,10},{10,11},{12,13},{... | collective-permute-start | bytes 4718600 | tf_op jit(solution)/shard_map/while/body/eval_jaxpr/ppermute | solution.py:16
  424.5 115.1 %copy-start.52 = (f32[48,768]{1,0:T(8,128)S(1)}, f32[48,768]{1,0:T(8,128)}, u32[]{:S(2)}) copy-start(f32[48,768]{1,0:T(8,128)} %param.36) | copy-start | bytes 442372
  424.5 115.1 %copy-start.53 = (f32[48,768]{1,0:T(8,128)S(1)}, f32[48,768]{1,0:T(8,128)}, u32[]{:S(2)}) copy-start(f32[48,768]{1,0:T(8,128)} %param.47) | copy-start | bytes 442372
  424.5 115.1 %copy-start.54 = (f32[48,768]{1,0:T(8,128)S(1)}, f32[48,768]{1,0:T(8,128)}, u32[]{:S(2)}) copy-start(f32[48,768]{1,0:T(8,128)} %param.46) | copy-start | bytes 442372
  424.6 175.3 %copy-start.35 = (bf16[4,256,768]{2,1,0:T(8,128)(2,1)S(1)}, bf16[4,256,768]{2,1,0:T(8,128)(2,1)}, u32[]{:S(2)}) copy-start(bf16[4,256,768]{2,1,0:T(8,128)(2,1)} %param.31) | copy-start | bytes 4718596
  424.6 175.3 %all-gather.6.cloned.1.call-start = ((), (), s32[]{:S(2)}) async-start(), calls=%async_computation.3 | async-start | bytes 2433024 | tf_op jit(solution)/shard_map/all_gather | solution.py:153
  543.3 790.8 %reduce-scatter.8.cloned.1.call-start = ((), (), s32[]{:S(2)}) async-start(), calls=%async_computation.5 | async-start | bytes 10948608
  950.2 38.5 %collective-permute-start.1 = (bf16[4,1536,128]{2,1,0:T(8,128)(2,1)S(1)}, bf16[4,1536,128]{2,1,0:T(8,128)(2,1)S(1)}, u32[]{:S(2)}, u32[]{:S(2)}) collective-permute-start(bf16[4,1536,128]{2,1,0:T(8,128)(2,1)S(1)} %fusion.282), channel_id=1, source_target_pairs={{1,0},{2,1},{3,2},{5,4},{6,5},{7,6},{9,8},{10,9},{11,10},{13,12},{... | collective-permute-start | bytes 4718600 | tf_op jit(solution)/shard_map/while/body/eval_jaxpr/ppermute | solution.py:16
  994.7 37.6 %collective-permute-start.1 = (bf16[4,1536,128]{2,1,0:T(8,128)(2,1)S(1)}, bf16[4,1536,128]{2,1,0:T(8,128)(2,1)S(1)}, u32[]{:S(2)}, u32[]{:S(2)}) collective-permute-start(bf16[4,1536,128]{2,1,0:T(8,128)(2,1)S(1)} %fusion.282), channel_id=1, source_target_pairs={{1,0},{2,1},{3,2},{5,4},{6,5},{7,6},{9,8},{10,9},{11,10},{13,12},{... | collective-permute-start | bytes 4718600 | tf_op jit(solution)/shard_map/while/body/eval_jaxpr/ppermute | solution.py:16
  1038.4 36.7 %collective-permute-start.1 = (bf16[4,1536,128]{2,1,0:T(8,128)(2,1)S(1)}, bf16[4,1536,128]{2,1,0:T(8,128)(2,1)S(1)}, u32[]{:S(2)}, u32[]{:S(2)}) collective-permute-start(bf16[4,1536,128]{2,1,0:T(8,128)(2,1)S(1)} %fusion.282), channel_id=1, source_target_pairs={{1,0},{2,1},{3,2},{5,4},{6,5},{7,6},{9,8},{10,9},{11,10},{13,12},{... | collective-permute-start | bytes 4718600 | tf_op jit(solution)/shard_map/while/body/eval_jaxpr/ppermute | solution.py:16
  1167.5 8.0 collective-permute-start.3
  1205.4 47.1 %copy-start.80 = (f32[24]{0:T(128)S(1)}, f32[24]{0:T(128)}, u32[]{:S(2)}) copy-start(f32[24]{0:T(128)} %param.32) | copy-start | bytes 292
  1205.4 47.1 %copy-start.81 = (f32[24]{0:T(128)S(1)}, f32[24]{0:T(128)}, u32[]{:S(2)}) copy-start(f32[24]{0:T(128)} %param.39) | copy-start | bytes 292
  1205.4 47.1 %copy-start.82 = (f32[24]{0:T(128)S(1)}, f32[24]{0:T(128)}, u32[]{:S(2)}) copy-start(f32[24]{0:T(128)} %param.38) | copy-start | bytes 292
  1205.4 49.5 %copy-start.83 = (f32[48]{0:T(128)S(1)}, f32[48]{0:T(128)}, u32[]{:S(2)}) copy-start(f32[48]{0:T(128)} %param.35) | copy-start | bytes 580
  1205.4 49.5 %copy-start.84 = (f32[48]{0:T(128)S(1)}, f32[48]{0:T(128)}, u32[]{:S(2)}) copy-start(f32[48]{0:T(128)} %param.45) | copy-start | bytes 580
  1205.4 49.5 %copy-start.85 = (f32[48]{0:T(128)S(1)}, f32[48]{0:T(128)}, u32[]{:S(2)}) copy-start(f32[48]{0:T(128)} %param.44) | copy-start | bytes 580
  1205.4 52.0 %copy-start.78 = (f32[3,24]{1,0:T(4,128)S(1)}, f32[3,24]{1,0:T(4,128)}, u32[]{:S(2)}) copy-start(f32[3,24]{1,0:T(4,128)} %param.49) | copy-start | bytes 868
  1205.4 52.0 %copy-start.79 = (f32[3,24]{1,0:T(4,128)S(1)}, f32[3,24]{1,0:T(4,128)}, u32[]{:S(2)}) copy-start(f32[3,24]{1,0:T(4,128)} %param.48) | copy-start | bytes 868
  1205.5 54.4 %copy-start.71 = (f32[5,56]{1,0:T(8,128)S(1)}, f32[5,56]{1,0:T(8,128)}, u32[]{:S(2)}) copy-start(f32[5,56]{1,0:T(8,128)} %param.34) | copy-start | bytes 3364
  1205.5 54.4 %copy-start.76 = (f32[5,56]{1,0:T(8,128)S(1)}, f32[5,56]{1,0:T(8,128)}, u32[]{:S(2)}) copy-start(f32[5,56]{1,0:T(8,128)} %param.43) | copy-start | bytes 3364
  1205.5 54.4 %copy-start.77 = (f32[5,56]{1,0:T(8,128)S(1)}, f32[5,56]{1,0:T(8,128)}, u32[]{:S(2)}) copy-start(f32[5,56]{1,0:T(8,128)} %param.42) | copy-start | bytes 3364
  1205.5 56.9 %copy-start.14 = (bf16[4,256,768]{2,1,0:T(8,128)(2,1)S(1)}, bf16[4,256,768]{2,1,0:T(8,128)(2,1)}, u32[]{:S(2)}) copy-start(bf16[4,256,768]{2,1,0:T(8,128)(2,1)} %param.30) | copy-start | bytes 4718596
  1205.5 56.9 %copy-start.36 = (bf16[4,256,768]{2,1,0:T(8,128)(2,1)S(1)}, bf16[4,256,768]{2,1,0:T(8,128)(2,1)}, u32[]{:S(2)}) copy-start(bf16[4,256,768]{2,1,0:T(8,128)(2,1)} %param.31) | copy-start | bytes 4718596
  1262.4 71.7 %copy-start.37 = (f32[24,3352]{1,0:T(8,128)S(1)}, f32[24,3352]{1,0:T(8,128)}, u32[]{:S(2)}) copy-start(f32[24,3352]{1,0:T(8,128)} %param.33) | copy-start | bytes 965380
  (141 other events, 1099.6 us)
Sparse Core Ops, SparseCore 0:
  11.4 68.6 all-gather.3
  424.7 114.8 reduce-scatter.5
  543.4 56.4 all-gather.5
  1192.6 141.4 reduce-scatter.7
where the time goes:
time: 1360 us; the launch traced here: 1350 us
  waiting for transfers between devices  426 us (31%)
  matrix products  331 us (24%)
  other arithmetic  212 us (16%)
  local copies, waits for them, and re-layouts  182 us (13%)
  blocking collectives  151 us (11%)
  starting transfers between devices  22.1 us (2%)
  between operations  19 us (1%)
    ppermute x8, waiting for transfers between devices, from_behind(): return lax.ppermute(block, axis, route)  192 us
    dot_general x16, matrix products, group_tail(): jnp.einsum('hts,shp->thp', mixing, per_head, precision=highest)  150 us
    dot_general x36, matrix products, exact_dot(): jnp.dot(left, right, precision=highest, preferred_element_type=jnp.float32)  128 us
    reduce_scatter x1, waiting for transfers between devices, local(): lax.psum_scatter(d_out_weight, ('dp', 'seq'), scatter_dimension=0, tiled=...  110 us
    unnamed x2, blocking collectives  84 us
    unnamed x5, waiting for transfers between devices  67.2 us
    all_gather x1, blocking collectives, local(): lax.all_gather(conv_low, ('dp', 'seq'), axis=1, tiled=True)  66.9 us
    all_gather x1, waiting for transfers between devices, local(): lax.all_gather(out_low_w, ('dp', 'seq'), axis=0, tiled=True)  56.5 us
  transfers between devices with their start and end apart: 12, of which 9 were waited for; matrix products, arithmetic and copies ran while one was open for 5% of the time, Pallas kernels for 0%

commit v1 on v0

v1 whole, which is shorter than its diff:
```python
import math
from functools import partial

import jax
import jax.numpy as jnp
import numpy as np
from jax import lax
from jax.experimental import pallas as pl
from jax.experimental.pallas import tpu as pltpu
from jax.sharding import PartitionSpec as P

norm_eps = 1e-05
adam_eps = 1e-08
log2e = math.log2(math.e)
lanes = 128
vmem_bytes = 56 * 1024 * 1024
f32 = jnp.float32
bf16 = jnp.bfloat16


def dot(left, right, left_dim=1, right_dim=0):
    return lax.dot_general(
        left, right, (((left_dim,), (right_dim,)), ((), ())), preferred_element_type=f32
    )


def halves(value):
    high = value.astype(bf16)
    return high, (value - high.astype(f32)).astype(bf16)


def sigmoid(value):
    return 1.0 / (1.0 + jnp.exp(-value))


def column(ref_value, at, width):
    return jnp.broadcast_to(ref_value[:, at : at + 1], (ref_value.shape[0], width))


def pair_columns(value, pair, low_lane):
    rows = value.shape[0]
    first = column(value, 2 * pair, lanes)
    second = column(value, 2 * pair + 1, lanes)
    return jnp.where(low_lane, first, second), first, second


def tri_sum(mask, value, head_lane):
    high = value.astype(bf16).astype(f32)
    rest = value - high
    mid = rest.astype(bf16).astype(f32)
    low = rest - mid
    packed = high + pltpu.roll(mid, 32, 1) + pltpu.roll(low, 64, 1)
    summed = dot(mask, packed.astype(bf16))
    total = summed + pltpu.roll(summed, lanes - 32, 1) + pltpu.roll(summed, lanes - 64, 1)
    return jnp.where(head_lane, total, 0.0)


def conv_chunk(ext_ref, conv_ref, at, length, taps):
    summed = conv_ref[taps : taps + 1, at : at + lanes]
    base = 8 - (taps - 1)
    for tap in range(taps):
        summed = (
            summed
            + conv_ref[tap : tap + 1, at : at + lanes]
            * ext_ref[base + tap : base + tap + length, at : at + lanes]
        )
    return summed


def step_sizes(dt_raw, head_ref, head_lane):
    shifted = dt_raw + head_ref[0:1, :]
    steps = jnp.maximum(shifted, 0.0) + jnp.log1p(jnp.exp(-jnp.abs(shifted)))
    return jnp.where(head_lane, steps, 0.0), shifted


def fetch_weight(core_ref, own_ref, other_ref, whole_ref, sems):
    blocks, rows, _ = own_ref.shape
    core = core_ref[0]
    copies = []
    for block in range(blocks):
        for which, source in ((core, own_ref), (1 - core, other_ref)):
            at = pl.multiple_of((2 * block + which) * rows, rows)
            copies.append(
                pltpu.make_async_copy(
                    source.at[block], whole_ref.at[pl.ds(at, rows)], sems.at[len(copies)]
                )
            )
    for copy in copies:
        copy.start()
    return copies


def hand_out(core, total_ref, send_ref, keep_ref):
    blocks, rows, _ = send_ref.shape
    for block in range(blocks):
        at = pl.multiple_of((2 * block + 1 - core) * rows, rows)
        send_ref[block] = total_ref[pl.ds(at, rows), :].astype(bf16)
        at = pl.multiple_of((2 * block + core) * rows, rows)
        keep_ref[block] = total_ref[pl.ds(at, rows), :]


def add_product(total_ref, left_ref, right):
    for at in range(0, total_ref.shape[0], 2 * lanes):
        here = slice(at, at + 2 * lanes)
        total_ref[here, :] += dot(left_ref[:, here], right, 0, 0)


def mixer_forward_kernel(
    core_ref,
    x_ref,
    edge_ref,
    wa_own,
    wa_other,
    wb_own,
    wb_other,
    conv_ref,
    head_ref,
    skip_ref,
    start_ref,
    normed_ref,
    ext_ref,
    dtr_ref,
    cum_ref,
    y_ref,
    sin_ref,
    end_ref,
    tail_ref,
    state_ref,
    carried_ref,
    weighted_ref,
    wa_ref,
    wb_ref,
    wa_sems,
    wb_sems,
    *,
    heads,
    inner,
    taps,
    grouped,
):
    block = pl.program_id(1)
    length, width = x_ref.shape

    @pl.when(jnp.logical_and(pl.program_id(0) == 0, block == 0))
    def _():
        copies = fetch_weight(core_ref, wa_own, wa_other, wa_ref, wa_sems)
        copies += fetch_weight(core_ref, wb_own, wb_other, wb_ref, wb_sems)
        for copy in copies:
            copy.wait()

    half = length // 2
    wide_a = wa_ref.shape[1]
    conv_dim = conv_ref.shape[1]
    state_dim = (conv_dim - inner) // 2

    def norm_of(rows):
        rows = rows.astype(f32)
        scale = lax.rsqrt(jnp.mean(rows * rows, axis=-1, keepdims=True) + norm_eps)
        return (rows * scale * conv_ref[taps + 1 : taps + 2, :width]).astype(bf16)

    @pl.when(block == 0)
    def _():
        if grouped:
            state_ref[...] = start_ref[...]
            edge = norm_of(edge_ref[...])
            tail_ref[:, :wide_a] = dot(edge, wa_ref[...])
            tail_ref[:, wide_a:] = dot(edge, wb_ref[...])[:, : conv_dim - wide_a]
        else:
            state_ref[...] = jnp.zeros_like(state_ref)
            tail_ref[...] = jnp.zeros_like(tail_ref)

    normed = norm_of(x_ref[...])
    normed_ref[...] = normed
    ext_ref[0:8, :] = tail_ref[...]
    ext_ref[8 : 8 + length, :wide_a] = dot(normed, wa_ref[...])
    second = dot(normed, wb_ref[...])
    ext_ref[8 : 8 + length, wide_a:] = second[:, : conv_dim - wide_a]
    dt_raw = second[:, conv_dim - wide_a :]
    tail_ref[...] = ext_ref[length : length + 8, :]

    lane = lax.broadcasted_iota(jnp.int32, (length, lanes), 1)
    low_lane = lane < lanes // 2
    head_lane = lane < heads
    dtr_ref[...] = dt_raw
    steps, _ = step_sizes(dt_raw, head_ref, head_lane)
    log_decay = steps * (-log2e * jnp.exp(head_ref[1:2, :]))
    row = lax.broadcasted_iota(jnp.int32, (length, length), 0)
    col = lax.broadcasted_iota(jnp.int32, (length, length), 1)
    cum = tri_sum((row >= col).astype(bf16), log_decay, head_lane)
    cum_ref[...] = cum
    cum_rows = cum.T

    def mixed_chunk(at):
        summed = conv_chunk(ext_ref, conv_ref, at, length, taps)
        return summed * sigmoid(summed)

    keys = jnp.concatenate(
        [mixed_chunk(inner + at) for at in range(0, state_dim, lanes)], axis=1
    ).astype(bf16)
    queries = jnp.concatenate(
        [mixed_chunk(inner + state_dim + at) for at in range(0, state_dim, lanes)], axis=1
    ).astype(bf16)
    state_low = state_ref[...].astype(bf16)
    sin_ref[...] = state_low
    carried_ref[...] = dot(queries, state_low)
    square = (half, half)
    diag = lax.broadcasted_iota(jnp.int32, square, 0) >= lax.broadcasted_iota(
        jnp.int32, square, 1
    )
    scores_00 = jnp.where(diag, dot(queries[:half], keys[:half], 1, 1), 0.0)
    scores_10 = dot(queries[half:], keys[:half], 1, 1)
    scores_11 = jnp.where(diag, dot(queries[half:], keys[half:], 1, 1), 0.0)
    for pair in range(heads // 2):
        at = pair * lanes
        values = mixed_chunk(at)
        cum_rep, cum_0, cum_1 = pair_columns(cum, pair, low_lane)
        dt_rep, _, _ = pair_columns(steps, pair, low_lane)
        stepped = values * dt_rep
        last = cum_rep[length - 1 : length, :]
        weighted_ref[:, at : at + lanes] = (stepped * jnp.exp2(last - cum_rep)).astype(bf16)
        top = None
        bottom = None
        for which, cum_col in ((0, cum_0), (1, cum_1)):
            own = jnp.where(low_lane if which == 0 else jnp.logical_not(low_lane), stepped, 0.0)
            own = own.astype(bf16)
            head = 2 * pair + which
            early = cum_rows[head : head + 1, :half]
            late = cum_rows[head : head + 1, half:]
            mix_00 = jnp.exp2(jnp.minimum(cum_col[:half] - early, 0.0)) * scores_00
            mix_10 = jnp.exp2(jnp.minimum(cum_col[half:] - early, 0.0)) * scores_10
            mix_11 = jnp.exp2(jnp.minimum(cum_col[half:] - late, 0.0)) * scores_11
            part_top = dot(mix_00.astype(bf16), own[:half])
            part_bottom = dot(
                jnp.concatenate([mix_10.astype(bf16), mix_11.astype(bf16)], axis=1), own
            )
            top = part_top if top is None else top + part_top
            bottom = part_bottom if bottom is None else bottom + part_bottom
        rest = (
            jnp.exp2(cum_rep) * carried_ref[:, at : at + lanes]
            + skip_ref[0:1, at : at + lanes] * values
        )
        y_ref[0:half, at : at + lanes] = top + rest[:half]
        y_ref[half:length, at : at + lanes] = bottom + rest[half:]
        fresh = dot(keys, weighted_ref[:, at : at + lanes], 0, 0)
        state_ref[:, at : at + lanes] = jnp.exp2(last) * state_ref[:, at : at + lanes] + fresh

    @pl.when(block == pl.num_programs(1) - 1)
    def _():
        end_ref[...] = state_ref[...]


def gate_kernel(
    core_ref,
    normed_ref,
    x_ref,
    cot_ref,
    y_ref,
    wg_own,
    wg_other,
    wo_own,
    wo_other,
    small_ref,
    out_ref,
    dy_ref,
    dgate_ref,
    dgain_ref,
    out_send,
    out_keep,
    gate_send,
    gate_keep,
    gate_ref,
    dno_ref,
    low_ref,
    out_sum,
    gate_sum,
    wg_ref,
    wo_ref,
    wg_sems,
    wo_sems,
    *,
    gain_row,
):
    length, inner = y_ref.shape
    first = jnp.logical_and(pl.program_id(0) == 0, pl.program_id(1) == 0)

    @pl.when(first)
    def _():
        copies = fetch_weight(core_ref, wg_own, wg_other, wg_ref, wg_sems)
        copies += fetch_weight(core_ref, wo_own, wo_other, wo_ref, wo_sems)
        dgain_ref[...] = jnp.zeros_like(dgain_ref)
        out_sum[...] = jnp.zeros_like(out_sum)
        gate_sum[...] = jnp.zeros_like(gate_sum)
        for copy in copies:
            copy.wait()

    gate_ref[...] = dot(normed_ref[...], wg_ref[...])
    dno_ref[...] = dot(cot_ref[...], wo_ref[...], 1, 1)
    squares = jnp.zeros((length, lanes), f32)
    crosses = jnp.zeros((length, lanes), f32)
    for at in range(0, inner, lanes):
        here = slice(at, at + lanes)
        gate = gate_ref[:, here]
        gated = y_ref[:, here] * (gate * sigmoid(gate))
        squares = squares + gated * gated
        crosses = crosses + gated * (small_ref[gain_row : gain_row + 1, here] * dno_ref[:, here])
    scale = lax.rsqrt(jnp.sum(squares, axis=1, keepdims=True) * (1.0 / inner) + norm_eps)
    cross = scale * scale * scale * (jnp.sum(crosses, axis=1, keepdims=True) * (1.0 / inner))
    scale_b = jnp.broadcast_to(scale, (length, lanes))
    cross_b = jnp.broadcast_to(cross, (length, lanes))
    for at in range(0, inner, lanes):
        here = slice(at, at + lanes)
        gate = gate_ref[:, here]
        mixed_out = y_ref[:, here]
        sig = sigmoid(gate)
        silu = gate * sig
        gated = mixed_out * silu
        scaled = gated * scale_b
        d_out = dno_ref[:, here]
        low_ref[:, here] = (scaled * small_ref[gain_row : gain_row + 1, here]).astype(bf16)
        dgain_ref[0:1, here] += jnp.sum(scaled * d_out, axis=0, keepdims=True)
        d_gated = scale_b * (small_ref[gain_row : gain_row + 1, here] * d_out) - gated * cross_b
        dy_ref[:, here] = (d_gated * silu).astype(bf16)
        dgate_ref[:, here] = (d_gated * mixed_out * (sig * (1.0 + gate * (1.0 - sig)))).astype(
            bf16
        )
    out_ref[...] = (x_ref[...].astype(f32) + dot(low_ref[...], wo_ref[...])).astype(bf16)
    add_product(out_sum, low_ref, cot_ref[...])
    add_product(gate_sum, normed_ref, dgate_ref[...])
    last = jnp.logical_and(
        pl.program_id(0) == pl.num_programs(0) - 1, pl.program_id(1) == pl.num_programs(1) - 1
    )

    @pl.when(last)
    def _():
        hand_out(core_ref[0], out_sum, out_send, out_keep)
        hand_out(core_ref[0], gate_sum, gate_send, gate_keep)


def mixer_backward_kernel(
    ext_ref,
    dtr_ref,
    cum_ref,
    y_ref,
    sin_ref,
    dy_ref,
    conv_ref,
    head_ref,
    skip_ref,
    sum_ref,
    start_ref,
    next_ref,
    small_in_ref,
    dgain_ref,
    _,
    dproj_ref,
    dconv_ref,
    end_ref,
    lead_ref,
    grad_ref,
    dsx_ref,
    dwv_ref,
    dye_ref,
    weighted_ref,
    zhigh_ref,
    zlow_ref,
    direct_ref,
    rows_ref,
    *,
    heads,
    inner,
    taps,
    fresh,
):
    step = pl.program_id(1)
    length = dy_ref.shape[0]
    half = length // 2
    conv_dim = conv_ref.shape[1]
    state_dim = (conv_dim - inner) // 2
    first = jnp.logical_and(pl.program_id(0) == 0, step == 0)

    @pl.when(first)
    def _():
        if small_in_ref.shape == dconv_ref.shape:
            dconv_ref[...] = small_in_ref[...]
        else:
            dconv_ref[...] = jnp.zeros_like(dconv_ref)
            dconv_ref[taps + 2 : taps + 3, :inner] = dgain_ref[0:1, :]
        rows_ref[...] = jnp.zeros_like(rows_ref)

    @pl.when(step == 0)
    def _():
        if fresh:
            grad_ref[...] = jnp.zeros_like(grad_ref)
            dsx_ref[length : length + 8, :] = jnp.zeros((8, conv_dim), f32)
        else:
            grad_ref[...] = start_ref[...]
            dsx_ref[length : length + 8, :] = next_ref[...]

    @pl.when(step > 0)
    def _():
        dsx_ref[length : length + 8, :] = dsx_ref[0:8, :]

    lane = lax.broadcasted_iota(jnp.int32, (length, lanes), 1)
    low_lane = lane < lanes // 2
    head_lane = lane < heads
    steps, shifted = step_sizes(dtr_ref[...], head_ref, head_lane)
    cum = cum_ref[...]
    cum_rows = cum.T

    def slope_chunk(at):
        summed = conv_chunk(ext_ref, conv_ref, at, length, taps)
        sig = sigmoid(summed)
        return summed * sig, sig * (1.0 + summed * (1.0 - sig))

    def put_grad(at, d_summed):
        here = slice(at, at + lanes)
        dsx_ref[0:length, here] = d_summed
        total = None
        for tap in range(taps):
            base = 8 - (taps - 1) + tap
            dconv_ref[tap : tap + 1, here] += jnp.sum(
                d_summed * ext_ref[base : base + length, here], axis=0, keepdims=True
            )
            back = taps - 1 - tap
            term = conv_ref[tap : tap + 1, here] * dsx_ref[back : back + length, here]
            total = term if total is None else total + term
        dconv_ref[taps : taps + 1, here] += jnp.sum(d_summed, axis=0, keepdims=True)
        dproj_ref[:, here] = total.astype(bf16)

    parts = [slope_chunk(inner + at) for at in range(0, 2 * state_dim, lanes)]
    count = state_dim // lanes
    keys = jnp.concatenate([part[0] for part in parts[:count]], axis=1).astype(bf16)
    queries = jnp.concatenate([part[0] for part in parts[count:]], axis=1).astype(bf16)
    grad_low = grad_ref[...].astype(bf16)
    dwv_ref[...] = dot(keys, grad_low)
    square = (half, half)
    diag = lax.broadcasted_iota(jnp.int32, square, 0) <= lax.broadcasted_iota(
        jnp.int32, square, 1
    )
    scores_00 = jnp.where(diag, dot(keys[:half], queries[:half], 1, 1), 0.0)
    scores_01 = dot(keys[:half], queries[half:], 1, 1)
    scores_11 = jnp.where(diag, dot(keys[half:], queries[half:], 1, 1), 0.0)
    ds_00 = jnp.zeros(square, f32)
    ds_01 = jnp.zeros(square, f32)
    ds_11 = jnp.zeros(square, f32)
    for pair in range(heads // 2):
        at = pair * lanes
        here = slice(at, at + lanes)
        values, slope = slope_chunk(at)
        cum_rep, cum_0, cum_1 = pair_columns(cum, pair, low_lane)
        dt_rep, _, _ = pair_columns(steps, pair, low_lane)
        stepped = (values * dt_rep).astype(bf16)
        stepped_f = stepped.astype(f32)
        last = cum_rep[length - 1 : length, :]
        tail = jnp.exp2(last - cum_rep)
        d_y = dy_ref[:, here]
        d_yf = d_y.astype(f32)
        dye_ref[:, here] = (d_yf * jnp.exp2(cum_rep)).astype(bf16)
        top = None
        bottom = None
        for which, cum_col in ((0, cum_0), (1, cum_1)):
            own_lane = low_lane if which == 0 else jnp.logical_not(low_lane)
            own_dy = jnp.where(own_lane, d_yf, 0.0).astype(bf16)
            own_x = jnp.where(own_lane, stepped_f, 0.0).astype(bf16)
            head = 2 * pair + which
            early = cum_rows[head : head + 1, :half]
            late = cum_rows[head : head + 1, half:]
            decay_00 = jnp.exp2(jnp.minimum(early - cum_col[:half], 0.0))
            decay_01 = jnp.exp2(jnp.minimum(late - cum_col[:half], 0.0))
            decay_11 = jnp.exp2(jnp.minimum(late - cum_col[half:], 0.0))
            mix_0 = jnp.concatenate(
                [(decay_00 * scores_00).astype(bf16), (decay_01 * scores_01).astype(bf16)], axis=1
            )
            mix_1 = (decay_11 * scores_11).astype(bf16)
            part_top = dot(mix_0, own_dy)
            part_bottom = dot(mix_1, own_dy[half:])
            top = part_top if top is None else top + part_top
            bottom = part_bottom if bottom is None else bottom + part_bottom
            d_mix_0 = dot(own_x[:half], d_y, 1, 1)
            d_mix_1 = dot(own_x[half:], d_y[half:], 1, 1)
            ds_00 = ds_00 + decay_00 * d_mix_0[:, :half]
            ds_01 = ds_01 + decay_01 * d_mix_0[:, half:]
            ds_11 = ds_11 + decay_11 * d_mix_1
        d_diag = jnp.concatenate([top, bottom], axis=0)
        weighted = (stepped_f * tail).astype(bf16)
        weighted_ref[:, here] = weighted
        d_weighted = dwv_ref[:, here]
        through = weighted.astype(f32) * d_weighted
        d_stepped = d_diag + tail * d_weighted
        skip = skip_ref[0:1, here]
        z = d_yf * (y_ref[:, here] - skip * values) - stepped_f * d_diag - through
        z_high, z_low = halves(z)
        zhigh_ref[:, here] = z_high
        zlow_ref[:, here] = z_low
        direct_ref[:, here] = (d_stepped * values).astype(bf16)
        total_decay = jnp.exp2(last)
        rows_ref[0:1, here] = jnp.sum(through, axis=0, keepdims=True) + total_decay * jnp.sum(
            grad_ref[:, here] * sin_ref[:, here].astype(f32), axis=0, keepdims=True
        )
        rows_ref[1:2, here] = jnp.sum(d_yf * values, axis=0, keepdims=True)
        put_grad(at, (d_stepped * dt_rep + skip * d_yf) * slope)
        grad_ref[:, here] = total_decay * grad_ref[:, here] + dot(
            queries, dye_ref[:, here], 0, 0
        )

    ds_00 = jnp.where(diag, ds_00, 0.0).astype(bf16)
    ds_11 = jnp.where(diag, ds_11, 0.0).astype(bf16)
    ds_01 = ds_01.astype(bf16)
    d_queries = dot(dye_ref[...], sin_ref[...], 1, 1)
    d_keys = dot(weighted_ref[...], grad_low, 1, 1)
    d_queries = d_queries + jnp.concatenate(
        [
            dot(ds_00, keys[:half], 0, 0),
            dot(ds_01, keys[:half], 0, 0) + dot(ds_11, keys[half:], 0, 0),
        ],
        axis=0,
    )
    d_keys = d_keys + jnp.concatenate(
        [
            dot(ds_00, queries[:half]) + dot(ds_01, queries[half:]),
            dot(ds_11, queries[half:]),
        ],
        axis=0,
    )
    for at in range(0, state_dim, lanes):
        put_grad(inner + at, d_keys[:, at : at + lanes] * parts[at // lanes][1])
        put_grad(
            inner + state_dim + at,
            d_queries[:, at : at + lanes] * parts[count + at // lanes][1],
        )
    summing = sum_ref[...]
    rows_high, rows_low = halves(rows_ref[...])
    row_sums = dot(rows_high, summing) + dot(rows_low, summing)
    d_cum = dot(zhigh_ref[...], summing) + dot(zlow_ref[...], summing)
    at_last = lax.broadcasted_iota(jnp.int32, (length, lanes), 0) == length - 1
    d_cum = d_cum + jnp.where(at_last, row_sums[0:1, :], 0.0)
    row = lax.broadcasted_iota(jnp.int32, (length, length), 0)
    col = lax.broadcasted_iota(jnp.int32, (length, length), 1)
    d_log = tri_sum((row <= col).astype(bf16), d_cum, head_lane)
    rate = jnp.exp(head_ref[1:2, :])
    d_steps = dot(direct_ref[...], summing) - rate * d_log
    d_raw = jnp.where(head_lane, d_steps * sigmoid(shifted), 0.0)
    dproj_ref[:, conv_dim : conv_dim + lanes] = d_raw.astype(bf16)
    head_row = slice(taps + 3, taps + 4)
    dconv_ref[head_row, :lanes] += jnp.sum(d_raw, axis=0, keepdims=True)
    dconv_ref[head_row, lanes : 2 * lanes] += jnp.sum(d_log * steps, axis=0, keepdims=True) * (
        -rate
    )
    dconv_ref[head_row, 2 * lanes : 3 * lanes] += row_sums[1:2, :]

    @pl.when(step == pl.num_programs(1) - 1)
    def _():
        end_ref[...] = grad_ref[...]
        lead_ref[...] = dsx_ref[0:8, :]


def input_grad_kernel(
    core_ref,
    x_ref,
    dgate_ref,
    dproj_ref,
    small_ref,
    wg_own,
    wg_other,
    wa_own,
    wa_other,
    wb_own,
    wb_other,
    dx_ref,
    dsmall_ref,
    a_send,
    a_keep,
    b_send,
    b_keep,
    normed_ref,
    a_sum,
    b_sum,
    wg_ref,
    wa_ref,
    wb_ref,
    wg_sems,
    wa_sems,
    wb_sems,
    *,
    gain_row,
):
    first = jnp.logical_and(pl.program_id(0) == 0, pl.program_id(1) == 0)
    width = x_ref.shape[1]

    @pl.when(first)
    def _():
        copies = fetch_weight(core_ref, wg_own, wg_other, wg_ref, wg_sems)
        copies += fetch_weight(core_ref, wa_own, wa_other, wa_ref, wa_sems)
        copies += fetch_weight(core_ref, wb_own, wb_other, wb_ref, wb_sems)
        dsmall_ref[...] = jnp.zeros_like(dsmall_ref)
        a_sum[...] = jnp.zeros_like(a_sum)
        b_sum[...] = jnp.zeros_like(b_sum)
        for copy in copies:
            copy.wait()

    wide_a = wa_ref.shape[1]
    d_normed = (
        dot(dgate_ref[...], wg_ref[...], 1, 1)
        + dot(dproj_ref[:, :wide_a], wa_ref[...], 1, 1)
        + dot(dproj_ref[:, wide_a:], wb_ref[...], 1, 1)
    )
    rows = x_ref[...].astype(f32)
    scale = lax.rsqrt(jnp.mean(rows * rows, axis=-1, keepdims=True) + norm_eps)
    scaled = rows * scale
    dsmall_ref[0:1, :] += jnp.sum(scaled * d_normed, axis=0, keepdims=True)
    gain = small_ref[gain_row : gain_row + 1, :width]
    normed_ref[...] = (scaled * gain).astype(bf16)
    add_product(a_sum, normed_ref, dproj_ref[:, :wide_a])
    add_product(b_sum, normed_ref, dproj_ref[:, wide_a:])
    inner_grad = gain * d_normed
    cross = jnp.mean(scaled * inner_grad, axis=-1, keepdims=True)
    dx_ref[...] = (scale * (inner_grad - scaled * cross)).astype(bf16)
    last = jnp.logical_and(
        pl.program_id(0) == pl.num_programs(0) - 1, pl.program_id(1) == pl.num_programs(1) - 1
    )

    @pl.when(last)
    def _():
        hand_out(core_ref[0], a_sum, a_send, a_keep)
        hand_out(core_ref[0], b_sum, b_send, b_keep)


def adam_kernel(
    rates_ref,
    sums_ref,
    norm_ref,
    *refs,
    heads,
    taps,
    at_refs,
    arrivals,
):
    rest_refs, front_refs, refs = refs[:arrivals], refs[arrivals : 2 * arrivals], refs[2 * arrivals :]
    ins, outs = refs[:18], refs[18:]
    learn_rate, decay_rate = rates_ref[0], rates_ref[3]
    beta_one, beta_two = rates_ref[1], rates_ref[2]
    first_scale, second_scale = rates_ref[4], rates_ref[5]

    def update(which, grad, index):
        master, first, second = (ref[index] for ref in ins[3 * which : 3 * which + 3])
        new_first = beta_one * first + (1.0 - beta_one) * grad
        new_second = beta_two * second + (1.0 - beta_two) * grad * grad
        change = -learn_rate * (
            (new_first * first_scale) / (jnp.sqrt(new_second * second_scale) + adam_eps)
            + decay_rate * master
        )
        where = at_refs[which]
        outs[where][index] = master + change if which in (1, 4) else change
        outs[where + 1][index] = new_first
        outs[where + 2][index] = new_second
        if which in (1, 4):
            outs[-2 if which == 1 else -1][index] = (master + change).astype(bf16)

    everything = (slice(None), slice(None))
    rest, front = rest_refs[0][...], front_refs[0][...]
    inner = rest.shape[1] // 2
    for rest_ref, front_ref in zip(rest_refs[1:], front_refs[1:]):
        rest = rest + rest_ref[...].astype(f32)
        front = front + front_ref[...].astype(f32)
    proj = ins[3].shape[1]
    update(1, rest[:, :inner], (slice(None), slice(0, inner)))
    update(1, front[:, : proj - inner], (slice(None), slice(inner, proj)))
    rows = rest.shape[0]
    half = inner // 2
    update(4, rest[:, inner : inner + half], (slice(0, rows), slice(None)))
    update(4, rest[:, inner + half :], (slice(rows, 2 * rows), slice(None)))
    me = rates_ref[6].astype(jnp.int32)

    def own(sums, at, count):
        wide = sums.shape[1]
        shift = lax.rem(wide - me * count, wide)
        return pltpu.roll(sums[...], shift, 1)[at, :count]

    update(0, own(norm_ref, slice(0, 1), ins[0].shape[1]), everything)
    update(2, own(sums_ref, slice(0, taps + 1), ins[6].shape[1]), everything)
    update(3, own(sums_ref, slice(taps + 2, taps + 3), ins[9].shape[1]), everything)
    head_row = slice(taps + 3, taps + 4)
    for row in range(3):
        grad = sums_ref[head_row, row * lanes : row * lanes + heads]
        update(5, grad, (slice(row, row + 1), slice(None)))


def whole(shape):
    return pl.BlockSpec(shape, lambda p, b: (0,) * len(shape))


def by_block(shape, size, back=False):
    if back:
        return pl.BlockSpec(shape, lambda p, s: (p * size + (size - 1 - s), 0))
    return pl.BlockSpec(shape, lambda p, b: (p * size + b, 0))


def by_part(shape):
    return pl.BlockSpec(shape, lambda p, b: (p, 0))


def params():
    return pltpu.CompilerParams(
        dimension_semantics=("arbitrary", "arbitrary"), vmem_limit_bytes=vmem_bytes
    )


def cost(flops, moved, powers):
    return pl.CostEstimate(flops=flops, bytes_accessed=moved, transcendentals=powers)


ANY = pl.BlockSpec(memory_space=pl.ANY)
SMEM = pl.BlockSpec(memory_space=pltpu.SMEM)


def weight_scratch(*weights):
    wholes = [
        pltpu.VMEM((2 * own.shape[0] * own.shape[1], own.shape[2]), bf16) for own, _ in weights
    ]
    return wholes + [pltpu.SemaphoreType.DMA((2 * own.shape[0],)) for own, _ in weights]


def handed_out(rows, columns, blocks):
    shape = (blocks, rows // (2 * blocks), columns)
    return [jax.ShapeDtypeStruct(shape, bf16), jax.ShapeDtypeStruct(shape, f32)]


def mixer_forward(dims, core, tokens, wa, wb, small, head, skip, grouped, edge, start):
    part, size, piece, width, inner, heads, taps = dims
    conv_dim = small.shape[1]
    state_dim = (conv_dim - inner) // 2
    blocks = part * size
    rows = blocks * piece
    ext_rows = piece + 8
    return pl.pallas_call(
        partial(mixer_forward_kernel, heads=heads, inner=inner, taps=taps, grouped=grouped),
        grid=(part, size),
        in_specs=[
            SMEM,
            by_block((piece, width), size),
            by_part((8, width)) if grouped else ANY,
            ANY,
            ANY,
            ANY,
            ANY,
            whole(small.shape),
            whole(head.shape),
            whole(skip.shape),
            by_part((state_dim, inner)) if grouped else ANY,
        ],
        out_specs=[
            by_block((piece, width), size),
            by_block((ext_rows, conv_dim), size),
            by_block((piece, lanes), size),
            by_block((piece, lanes), size),
            by_block((piece, inner), size),
            by_block((state_dim, inner), size),
            by_part((state_dim, inner)),
        ],
        out_shape=[
            jax.ShapeDtypeStruct((rows, width), bf16),
            jax.ShapeDtypeStruct((blocks * ext_rows, conv_dim), f32),
            jax.ShapeDtypeStruct((rows, lanes), f32),
            jax.ShapeDtypeStruct((rows, lanes), f32),
            jax.ShapeDtypeStruct((rows, inner), f32),
            jax.ShapeDtypeStruct((blocks * state_dim, inner), bf16),
            jax.ShapeDtypeStruct((part * state_dim, inner), f32),
        ],
        scratch_shapes=[
            pltpu.VMEM((8, conv_dim), f32),
            pltpu.VMEM((state_dim, inner), f32),
            pltpu.VMEM((piece, inner), f32),
            pltpu.VMEM((piece, inner), bf16),
        ]
        + weight_scratch(wa, wb),
        compiler_params=params(),
        cost_estimate=cost(1, 1, 0),
    )(core, tokens, edge, *wa, *wb, small, head, skip, start)


def gate_step(dims, core, normed, tokens, cots, y, wg, wo, small):
    part, size, piece, width, inner, heads, taps = dims
    rows = part * size * piece
    blocks = wo[0].shape[0]
    handed = handed_out(inner, width, blocks) + handed_out(width, inner, blocks)
    return pl.pallas_call(
        partial(gate_kernel, gain_row=taps + 2),
        grid=(part, size),
        in_specs=[
            SMEM,
            by_block((piece, width), size),
            by_block((piece, width), size),
            by_block((piece, width), size),
            by_block((piece, inner), size),
            ANY,
            ANY,
            ANY,
            ANY,
            whole(small.shape),
        ],
        out_specs=[
            by_block((piece, width), size),
            by_block((piece, inner), size),
            by_block((piece, inner), size),
            whole((8, inner)),
        ]
        + [whole(array.shape) for array in handed],
        out_shape=[
            jax.ShapeDtypeStruct((rows, width), bf16),
            jax.ShapeDtypeStruct((rows, inner), bf16),
            jax.ShapeDtypeStruct((rows, inner), bf16),
            jax.ShapeDtypeStruct((8, inner), f32),
        ]
        + handed,
        scratch_shapes=[
            pltpu.VMEM((piece, inner), f32),
            pltpu.VMEM((piece, inner), f32),
            pltpu.VMEM((piece, inner), bf16),
            pltpu.VMEM((inner, width), f32),
            pltpu.VMEM((width, inner), f32),
        ]
        + weight_scratch(wg, wo),
        compiler_params=params(),
        cost_estimate=cost(1, 1, 0),
    )(core, normed, tokens, cots, y, *wg, *wo, small)


def mixer_backward(dims, saved, consts, carry, blocks, fresh):
    part, size, piece, width, inner, heads, taps = dims
    first, count = blocks
    small, head, skip, summing, dgain = consts
    conv_dim = small.shape[1]
    state_dim = (conv_dim - inner) // 2
    ext_rows = piece + 8
    wide = conv_dim + lanes
    dproj, dsmall, state, lead = carry

    def by_block(shape):
        return pl.BlockSpec(shape, lambda p, s: (p * size + (first + count - 1 - s), 0))

    return pl.pallas_call(
        partial(mixer_backward_kernel, heads=heads, inner=inner, taps=taps, fresh=fresh),
        grid=(part, count),
        in_specs=[
            by_block((ext_rows, conv_dim)),
            by_block((piece, lanes)),
            by_block((piece, lanes)),
            by_block((piece, inner)),
            by_block((state_dim, inner)),
            by_block((piece, inner)),
            whole(small.shape),
            whole(head.shape),
            whole(skip.shape),
            whole(summing.shape),
            ANY if fresh else by_part((state_dim, inner)),
            ANY if fresh else by_part((8, conv_dim)),
            whole(dsmall.shape),
            whole(dgain.shape),
            ANY,
        ],
        out_specs=[
            by_block((piece, wide)),
            whole((8, conv_dim)),
            by_part((state_dim, inner)),
            by_part((8, conv_dim)),
        ],
        out_shape=[
            jax.ShapeDtypeStruct((part * size * piece, wide), bf16),
            jax.ShapeDtypeStruct((8, conv_dim), f32),
            jax.ShapeDtypeStruct((part * state_dim, inner), f32),
            jax.ShapeDtypeStruct((part * 8, conv_dim), f32),
        ],
        scratch_shapes=[
            pltpu.VMEM((state_dim, inner), f32),
            pltpu.VMEM((piece + 8, conv_dim), f32),
            pltpu.VMEM((piece, inner), f32),
            pltpu.VMEM((piece, inner), bf16),
            pltpu.VMEM((piece, inner), bf16),
            pltpu.VMEM((piece, inner), bf16),
            pltpu.VMEM((piece, inner), bf16),
            pltpu.VMEM((piece, inner), bf16),
            pltpu.VMEM((8, inner), f32),
        ],
        input_output_aliases={14: 0} if dproj.shape[0] == part * size * piece else {},
        compiler_params=params(),
        cost_estimate=cost(1, 1, 0),
    )(*saved, small, head, skip, summing, state, lead, dsmall, dgain, dproj)


def input_grad(dims, core, tokens, dgate, dproj, small, wg, wa, wb):
    part, size, piece, width, inner, heads, taps = dims
    rows = part * size * piece
    blocks = wa[0].shape[0]
    wide_a, wide_b = wa[0].shape[2], wb[0].shape[2]
    handed = handed_out(width, wide_a, blocks) + handed_out(width, wide_b, blocks)
    return pl.pallas_call(
        partial(input_grad_kernel, gain_row=taps + 1),
        grid=(part, size),
        in_specs=[
            SMEM,
            by_block((piece, width), size),
            by_block((piece, inner), size),
            by_block((piece, dproj.shape[1]), size),
            whole(small.shape),
            ANY,
            ANY,
            ANY,
            ANY,
            ANY,
            ANY,
        ],
        out_specs=[by_block((piece, width), size), whole((8, width))]
        + [whole(array.shape) for array in handed],
        out_shape=[
            jax.ShapeDtypeStruct((rows, width), bf16),
            jax.ShapeDtypeStruct((8, width), f32),
        ]
        + handed,
        scratch_shapes=[
            pltpu.VMEM((piece, width), bf16),
            pltpu.VMEM((width, wide_a), f32),
            pltpu.VMEM((width, wide_b), f32),
        ]
        + weight_scratch(wg, wa, wb),
        compiler_params=params(),
        cost_estimate=cost(1, 1, 0),
    )(core, tokens, dgate, dproj, small, *wg, *wa, *wb)


def adam(rates, sums, norm_sums, gate_grads, front_grads, states, heads, taps):
    outs = []
    at_refs = []
    for which, (master, first, second) in enumerate(states):
        at_refs.append(len(outs))
        outs += [jax.ShapeDtypeStruct(master.shape, f32)] * 3
    outs.append(jax.ShapeDtypeStruct(states[1][0].shape, bf16))
    outs.append(jax.ShapeDtypeStruct(states[4][0].shape, bf16))
    flat = [array for state in states for array in state]
    vmem = pl.BlockSpec(memory_space=pltpu.VMEM)
    return pl.pallas_call(
        partial(
            adam_kernel, heads=heads, taps=taps, at_refs=at_refs, arrivals=len(gate_grads)
        ),
        in_specs=[SMEM] + [vmem] * (2 + 2 * len(gate_grads) + len(flat)),
        out_specs=[vmem] * len(outs),
        out_shape=outs,
        compiler_params=pltpu.CompilerParams(vmem_limit_bytes=vmem_bytes),
        cost_estimate=cost(1, 1, 0),
    )(rates, sums, norm_sums, *gate_grads, *front_grads, *flat)


def bit_count(extent):
    count = extent.bit_length() - 1
    if 1 << count != extent:
        raise ValueError(extent)
    return count


def swap(block, axis, bit):
    devices = range(lax.axis_size(axis))
    return lax.ppermute(block, axis, [(i, i ^ (1 << bit)) for i in devices])


def shifted_by(block, axis, distance):
    devices = range(lax.axis_size(axis))
    route = [(i, i + distance) for i in devices if i + distance in devices]
    return lax.ppermute(block, axis, route)


def pick(block, at, axis):
    return lax.dynamic_index_in_dim(block, at, axis, keepdims=False)


def gather_bit(block, axis, bit, at, *others):
    mine = (lax.axis_index(axis) >> bit) & 1
    other = swap(block, axis, bit)
    if others:
        other = after(other, *others)
    low = jnp.where(mine == 1, other, block)
    high = jnp.where(mine == 1, block, other)
    return jnp.stack([low, high], axis=at)


def gather_seq(shard):
    block = shard
    kept = []
    for done, bit in enumerate(reversed(range(bit_count(lax.axis_size("seq"))))):
        block = gather_bit(block, "seq", bit, done)
        kept.append(block)
    return block.reshape((-1,) + shard.shape), kept[0]


def dp_orders():
    bits = bit_count(lax.axis_size("dp"))
    return list(range(bits - 1, 0, -1)) + [0], list(range(1, bits)) + [0]


def gather_dp_bit(block, order, step, *others):
    at = sum(1 for b in order[:step] if b > order[step])
    return gather_bit(block, "dp", order[step], at, *others)


def give_half(block, axis, bit, at):
    mine = (lax.axis_index(axis) >> bit) & 1
    other = swap(pick(block, 1 - mine, at).astype(bf16), axis, bit)
    return pick(block, mine, at) + other.astype(f32)


def core_sums(send, keep):
    extent = lax.axis_size("seq")
    total = keep + swap(send, "dp", 0).astype(f32)
    bits = bit_count(lax.axis_size("dp")) - 1
    return total.reshape((2,) * bits + (extent, -1, send.shape[2]))


def scatter_dp_bit(block, order, step):
    bit = order[-1 - step]
    return give_half(block, "dp", bit, sum(1 for b in order[: len(order) - 1 - step] if b > bit))


def scatter_seq(block):
    extent = lax.axis_size("seq")
    place = lax.axis_index("seq")
    arrivals = [pick(block, place, 0)]
    for distance in range(1, extent):
        sent = pick(block, lax.rem(place + distance, extent), 0).astype(bf16)
        route = [(i, (i + distance) % extent) for i in range(extent)]
        arrivals.append(lax.ppermute(sent, "seq", route))
    return arrivals


def sum_over(block, axis):
    for bit in range(bit_count(lax.axis_size(axis))):
        block = block + swap(block, axis, bit)
    return block


def seq_groups(size):
    extent = lax.axis_size("seq")
    if size == extent:
        return None
    return [list(range(at, at + size)) for at in range(0, extent, size)]


def to_sequences(block, part, size):
    if size > 1:
        block = lax.all_to_all(
            block, "seq", 0, 0, axis_index_groups=seq_groups(size), tiled=True
        )
    piece, width = block.shape[1:]
    block = block.reshape(size, part, piece, width)
    if part > 1:
        block = block.transpose(1, 0, 2, 3)
    return block.reshape(-1, width)


def to_pieces(rows, part, size, piece):
    block = rows.reshape(part, size, piece, -1)
    if part > 1:
        block = block.transpose(1, 0, 2, 3)
    block = block.reshape(part * size, piece, -1)
    if size > 1:
        block = lax.all_to_all(
            block, "seq", 0, 0, axis_index_groups=seq_groups(size), tiled=True
        )
    return block


def after(value, *others):
    return lax.optimization_barrier((value,) + others)[0]


def padded(block, rows, columns):
    return jnp.pad(block, ((0, rows - block.shape[0]), (0, columns - block.shape[1])))


def summing_matrix(inner, heads):
    columns = np.zeros((inner, lanes), np.float32)
    columns[np.arange(inner), np.arange(inner) // (inner // heads)] = 1.0
    return jnp.asarray(columns, bf16)


def local(
    layer_in,
    out_grad,
    norm_gain,
    in_weight,
    conv_params,
    gate_gain,
    out_weight,
    head_params,
    norm_first,
    norm_second,
    in_first,
    in_second,
    conv_first,
    conv_second,
    gate_first,
    gate_second,
    out_first,
    out_second,
    head_first,
    head_second,
    step_count,
    hyper,
):
    seq_count, piece, width = layer_in.shape
    seq_extent = lax.axis_size("seq")
    me = lax.axis_index("dp") * seq_extent + lax.axis_index("seq")
    step_float = step_count[0].astype(f32)
    scales = 1.0 / (1.0 - hyper[1:3] ** step_float)
    rates = jnp.concatenate([hyper, scales, jnp.stack([me.astype(f32), jnp.zeros((), f32)])])
    core = (lax.axis_index("dp") & 1).astype(jnp.int32)[None]
    owners = lax.axis_size("dp") * seq_extent
    size = math.gcd(seq_extent, seq_count)
    part = seq_count // size
    groups = seq_extent // size
    inner = out_weight.shape[0] * owners
    heads = head_params.shape[1]
    tap_rows, conv_own = conv_params.shape
    taps = tap_rows - 1
    conv_dim = conv_own * owners
    state_dim = (conv_dim - inner) // 2
    own_rows = in_weight.shape[0]
    gate_own = gate_gain.shape[0]
    wide_a = min(1024, inner)
    dims = (part, size, piece, width, inner, heads, taps)

    small = jnp.zeros((8, conv_dim), bf16)
    for at, row, count in (
        (0, conv_params, conv_own),
        (tap_rows, norm_gain[None, :], own_rows),
        (tap_rows + 1, gate_gain[None, :], gate_own),
    ):
        small = lax.dynamic_update_slice(small, row.astype(bf16), (at, me * count))
    head = padded(head_params, 8, lanes)
    skip = jnp.repeat(head_params[2], inner // heads)[None, :]
    summing = summing_matrix(inner, heads)

    in_low = padded(in_weight.astype(bf16), own_rows, inner + conv_dim + lanes)
    out_low_own = out_weight.astype(bf16).reshape(2, own_rows, width)
    shard = jnp.concatenate([in_low, out_low_own[0], out_low_own[1]], axis=1)
    gathered, half_gathered = gather_seq(shard)
    small = sum_over(after(small, half_gathered), "seq")
    front_end = inner + conv_dim + lanes
    wg = gathered[:, :, :inner]
    wa = gathered[:, :, inner : inner + wide_a]
    wb = gathered[:, :, inner + wide_a : front_end]
    wo = jnp.stack(
        [gathered[:, :, front_end : front_end + width], gathered[:, :, front_end + width :]],
        axis=1,
    ).reshape(-1, 2 * own_rows, width)
    tokens = to_sequences(after(layer_in, head, skip, shard, rates), part, size)
    order_a, order_b = dp_orders()
    last = len(order_a) - 1
    for step in range(last):
        wa = gather_dp_bit(wa, order_a, step)
        wb = gather_dp_bit(wb, order_b, step)
    small = sum_over(small, "dp").astype(f32)
    wg, wo = after((wg, wo), wa, wb, small)

    def core_halves(block):
        block = block.reshape(owners // 2 // seq_extent, -1, block.shape[-1])
        return block, swap(block, "dp", 0)

    wb = core_halves(wb)
    wa = core_halves(wa)
    for step in range(last - 1):
        wg = gather_dp_bit(wg, order_a, step)
        wo = gather_dp_bit(wo, order_b, step)
    wg, wo, tokens = lax.optimization_barrier((wg, wo, after(tokens, wa, wb)))
    cots = to_sequences(after(out_grad, tokens), part, size)

    edge = core
    if groups > 1:
        edge = tokens.reshape(part, size * piece, width)[:, size * piece - 8 :, :]
        edge = shifted_by(edge, "seq", size).reshape(part * 8, width)

    def forward(start):
        return mixer_forward(
            dims, core, tokens, wa, wb, small, head, skip, groups > 1, edge, start
        )

    if groups > 1:
        first_out = forward(jnp.zeros((part * state_dim, inner), f32))
        cum_last = first_out[3].reshape(part, size, piece, lanes)[:, :, piece - 1, :heads]
        decay = jnp.exp2(jnp.sum(cum_last, axis=1))
        decay = jnp.repeat(decay, inner // heads, axis=1)[:, None, :]

        def relay(ends, distance):
            ends = ends.reshape(part, state_dim, inner)
            carried = jnp.zeros_like(ends)
            for _ in range(groups - 1):
                sent = (decay * carried + ends).astype(bf16)
                carried = shifted_by(sent, "seq", distance).astype(f32)
            return carried.reshape(part * state_dim, inner)

        start = relay(first_out[6], size)
    else:
        start = core
    normed, ext, dtr, cum, y, sin, _ = forward(start)

    wg = core_halves(gather_dp_bit(wg, order_a, last - 1, normed))
    wo = core_halves(gather_dp_bit(wo, order_b, last - 1, normed))
    layer_rows, dy, dgate, dgain, *handed = gate_step(
        dims, core, normed, tokens, cots, y, wg, wo, small
    )
    layer_out = to_pieces(layer_rows, part, size, piece)
    g_out = core_sums(*handed[:2])
    g_gate = core_sums(*handed[2:])
    dy = after(dy, g_out, g_gate)
    cut = size // 2
    saved = (ext, dtr, cum, y, sin, dy)
    consts = (small, head, skip, summing, dgain)

    def backward(state, lead):
        carry = (core, head, state, lead)
        return list(
            mixer_backward(dims, saved, consts, carry, (cut, size - cut), groups == 1)
        )

    if groups > 1:
        zeros = (jnp.zeros((part * state_dim, inner), f32), jnp.zeros((part * 8, conv_dim), f32))
        first_out = backward(*zeros)
        first_out = mixer_backward(dims, saved, consts, first_out, (0, cut), False)
        backward_out = backward(relay(first_out[2], -size), zeros[1])
    else:
        backward_out = backward(core, core)
    for step in range(1, last):
        g_out = scatter_dp_bit(g_out, order_a, step)
        g_gate = scatter_dp_bit(g_gate, order_b, step)
    backward_out[2], g_out, g_gate = lax.optimization_barrier((backward_out[2], g_out, g_gate))
    dproj, dsmall, _, lead = mixer_backward(dims, saved, consts, backward_out, (0, cut), False)
    g_out = scatter_dp_bit(g_out, order_a, last)
    g_gate = scatter_dp_bit(g_gate, order_b, last)
    if groups > 1:
        lead = shifted_by(lead.astype(bf16), "seq", -size).astype(f32)
        lead = lead.reshape(part, 8, conv_dim)
        fixes = []
        for row in range(taps - 1):
            terms = [small[tap] * lead[:, row - tap] for tap in range(row + 1)]
            fixes.append(sum(terms[1:], terms[0]))
        fix = jnp.pad(jnp.stack(fixes, axis=1), ((0, 0), (0, 0), (0, lanes)))
        dproj = dproj.reshape(part, size * piece, conv_dim + lanes)
        ends = dproj[:, size * piece - (taps - 1) :].astype(f32) + fix
        dproj = dproj.at[:, size * piece - (taps - 1) :].set(ends.astype(bf16))
        dproj = dproj.reshape(-1, conv_dim + lanes)
    g_rest = scatter_seq(
        jnp.concatenate([g_gate, g_out[:, :own_rows], g_out[:, own_rows:]], axis=2)
    )
    sums = sum_over(dsmall, "seq")
    tokens = after(tokens, layer_out, g_gate, g_out)
    dx, d_gain, *handed = input_grad(dims, core, tokens, dgate, dproj, small, wg, wa, wb)
    handed, dx, sums = after((handed, dx, sums), g_rest)
    g_a = core_sums(*handed[:2])
    g_b = core_sums(*handed[2:])
    sums, d_gain = after((sums, d_gain), g_a, g_b)
    for step in range(1, last + 1):
        g_a = scatter_dp_bit(g_a, order_a, step)
        g_b = scatter_dp_bit(g_b, order_b, step)
    g_front = scatter_seq(jnp.concatenate([g_a, g_b], axis=2))
    in_grad = out_grad.astype(f32) + to_pieces(dx, part, size, piece).astype(f32)
    sums = sum_over(sums, "dp")
    norm_sums = sum_over(sum_over(d_gain, "dp"), "seq")

    states = (
        (norm_gain[None, :], norm_first[None, :], norm_second[None, :]),
        (in_weight, in_first, in_second),
        (conv_params, conv_first, conv_second),
        (gate_gain[None, :], gate_first[None, :], gate_second[None, :]),
        (out_weight, out_first, out_second),
        (head_params, head_first, head_second),
    )
    new = adam(rates, sums, norm_sums, g_rest, g_front, states, heads, taps)
    new = [array[0] if array.shape[0] == 1 else array for array in new]
    return (layer_out, in_grad, *new)


def solution(mesh):
    in_specs = (
        P("dp", "seq", None),
        P("dp", "seq", None),
        P(("dp", "seq")),
        P(("dp", "seq"), None),
        P(None, ("dp", "seq")),
        P(("dp", "seq")),
        P(("dp", "seq"), None),
        P(),
        P(("dp", "seq")),
        P(("dp", "seq")),
        P(("dp", "seq"), None),
        P(("dp", "seq"), None),
        P(None, ("dp", "seq")),
        P(None, ("dp", "seq")),
        P(("dp", "seq")),
        P(("dp", "seq")),
        P(("dp", "seq"), None),
        P(("dp", "seq"), None),
        P(),
        P(),
        P(),
        P(),
    )
    out_specs = (
        P("dp", "seq", None),
        P("dp", "seq", None),
        P(("dp", "seq")),
        P(("dp", "seq")),
        P(("dp", "seq")),
        P(("dp", "seq"), None),
        P(("dp", "seq"), None),
        P(("dp", "seq"), None),
        P(None, ("dp", "seq")),
        P(None, ("dp", "seq")),
        P(None, ("dp", "seq")),
        P(("dp", "seq")),
        P(("dp", "seq")),
        P(("dp", "seq")),
        P(("dp", "seq"), None),
        P(("dp", "seq"), None),
        P(("dp", "seq"), None),
        P(),
        P(),
        P(),
        P(("dp", "seq"), None),
        P(("dp", "seq"), None),
    )
    return jax.shard_map(local, mesh=mesh, in_specs=in_specs, out_specs=out_specs, check_vma=False)
```

time: 1360 us -> 348 us (0.26)
  waiting for transfers between devices: 426 us -> 79.2 us
  matrix products: 331 us -> 0 us
  other arithmetic: 212 us -> 26.1 us
  local copies, waits for them, and re-layouts: 182 us -> 14.5 us
  blocking collectives: 151 us -> 0 us
  Pallas kernels: 0 us -> 148 us
  starting transfers between devices: 22.1 us -> 75.5 us
  between operations: 19 us -> 2.27 us
    dot_general x64 -> x0, matrix products: 331 us -> none  [the longest x16 150 us: group_tail(): jnp.einsum('hts,shp->thp', mixing, per_head, precision=highest)]
    pallas_call x0 -> x6, Pallas kernels: none -> 148 us  [the longest x2 57.7 us: mixer_backward(): pl.pallas_call(partial(mixer_backward_kernel, heads=heads, inner=inner, t...]
    ppermute x8 -> x47, waiting for transfers between devices: 192 us -> 77.8 us  [the longest x41 73.9 us: swap(): return lax.ppermute(block, axis, [(i, i ^ 1 << bit) for i in devices])]
    reduce_scatter x1 -> x0, waiting for transfers between devices: 110 us -> none  [local(): lax.psum_scatter(d_out_weight, ('dp', 'seq'), scatter_dimension=0, tiled=...]
    unnamed x2 -> x0, blocking collectives: 84 us -> none
    unnamed x5 -> x0, waiting for transfers between devices: 67.2 us -> none
    all_gather x1 -> x0, blocking collectives: 66.9 us -> none  [local(): lax.all_gather(conv_low, ('dp', 'seq'), axis=1, tiled=True)]
    reduce_sum x25 -> x0, other arithmetic: 60.1 us -> none  [the longest x1 17.8 us: conv_silu(): summed = summed + conv[offset] * extended[..., offset:offset + out_rows, :]]
  transfers between devices with their start and end apart: 12 -> 51, of which waited for: 9 -> 27; matrix products, arithmetic and copies ran while one was open for 5% -> 8% of each run, Pallas kernels for 0% -> 32%
where the time goes in v1:
time: 348 us; the launch traced here: 345 us
  Pallas kernels  148 us (43%)
  waiting for transfers between devices  79.2 us (23%)
  starting transfers between devices  75.5 us (22%)
  other arithmetic  26.1 us (8%)
  local copies, waits for them, and re-layouts  14.5 us (4%)
    ppermute x41, waiting for transfers between devices, swap(): return lax.ppermute(block, axis, [(i, i ^ 1 << bit) for i in devices])  73.9 us
    pallas_call x2, Pallas kernels, mixer_backward(): pl.pallas_call(partial(mixer_backward_kernel, heads=heads, inner=inner, t...  57.7 us
    ppermute x41, starting transfers between devices, swap(): return lax.ppermute(block, axis, [(i, i ^ 1 << bit) for i in devices])  50.7 us
    pallas_call x1, Pallas kernels, gate_step(): pl.pallas_call(partial(gate_kernel, gain_row=taps + 2), grid=(part, size)...  38.3 us
    pallas_call x1, Pallas kernels, mixer_forward(): pl.pallas_call(partial(mixer_forward_kernel, heads=heads, inner=inner, ta...  30.4 us
    pallas_call x1, Pallas kernels, input_grad(): pl.pallas_call(partial(input_grad_kernel, gain_row=taps + 1), grid=(part,...  17.6 us
    unnamed x47, local copies, waits for them, and re-layouts  9.52 us
    all_to_all x2, starting transfers between devices, to_pieces(): lax.all_to_all(block, 'seq', 0, 0, axis_index_groups=seq_groups(size), ti...  8.74 us
  transfers between devices with their start and end apart: 51, of which 27 were waited for; matrix products, arithmetic and copies ran while one was open for 8% of the time, Pallas kernels for 32%

profile of v1, /device:TPU:0, one launch (start us, length us, event | category | flops | bytes accessed | tf_op | source)
XLA Modules:
  0.0 345.2 jit_solution(7519221035432714229)
XLA Ops:
  2.7 4.1 %collective-permute-start = (bf16[24,4992]{1,0:T(8,128)(2,1)S(1)}, bf16[24,4992]{1,0:T(8,128)(2,1)S(1)}, u32[]{:S(2)}, u32[]{:S(2)}) collective-permute-start(bf16[24,4992]{1,0:T(8,128)(2,1)S(1)} %fusion.8), channel_id=1, source_target_pairs={{0,2},{1,3},{2,0},{3,1},{4,6},{5,7},{6,4},{7,5},{8,10},{9,11},{10,... | collective-permute-start | bytes 718856 | tf_op jit(solution)/shard_map/ppermute | solution.py:961
  9.3 8.4 %collective-permute-done = bf16[24,4992]{1,0:T(8,128)(2,1)S(1)} collective-permute-done((bf16[24,4992]{1,0:T(8,128)(2,1)S(1)}, bf16[24,4992]{1,0:T(8,128)(2,1)S(1)}, u32[]{:S(2)}, u32[]{:S(2)}) %collective-permute-start) | collective-permute-done | bytes 239648 | tf_op jit(solution)/shard_map/ppermute | solution.py:961
  18.7 3.1 collective-permute-done.6
  24.0 2.7 collective-permute-done.7
  35.5 4.8 %all-to-all-start = ((bf16[4,256,768]{2,1,0:T(8,128)(2,1)}), bf16[4,256,768]{2,1,0:T(8,128)(2,1)S(1)}, u32[]{:S(2)}, u32[]{:S(2)}) async-start(bf16[4,256,768]{2,1,0:T(8,128)(2,1)} %param.23), calls=%async_computation | async-start | bytes 3145728 | tf_op jit(solution)/shard_map/all_to_all | solution.py:1047
  40.9 2.5 collective-permute-done.1
  45.8 3.3 collective-permute-done.4
  53.6 3.2 collective-permute-done.5
  57.0 3.3 collective-permute-done.3
  60.4 2.4 collective-permute-start.12
  68.4 4.5 %collective-permute-done.11 = bf16[4,24,1536]{2,1,0:T(8,128)(2,1)S(1)} collective-permute-done((bf16[4,24,1536]{2,1,0:T(8,128)(2,1)S(1)}, bf16[4,24,1536]{2,1,0:T(8,128)(2,1)S(1)}, u32[]{:S(2)}, u32[]{:S(2)}) %collective-permute-start.11) | collective-permute-done | bytes 294944 | tf_op jit(solution)/shard_map/ppermute | solution.py:961
  78.1 3.6 %all-to-all-start.1 = ((bf16[4,256,768]{2,1,0:T(8,128)(2,1)}), bf16[4,256,768]{2,1,0:T(8,128)(2,1)S(1)}, u32[]{:S(2)}, u32[]{:S(2)}) async-start(bf16[4,256,768]{2,1,0:T(8,128)(2,1)} %param.24), calls=%async_computation.1 | async-start | bytes 3145728 | tf_op jit(solution)/shard_map/all_to_all | solution.py:1047
  81.7 30.4 %shard_map.390 = (bf16[1024,768]{1,0:T(8,128)(2,1)}, f32[1056,1792]{1,0:T(8,128)}, f32[1024,128]{1,0:T(8,128)}, f32[1024,128]{1,0:T(8,128)}, f32[1024,1536]{1,0:...) custom-call(s32[1]{0:T(128)} %bitcast.core_ref.edge_ref.start_ref.next_ref._, bf16[1024,768]{1,0:T(8,128)(2,1)} %bitcast.137, ...), custom_call_target="tpu_custom_call" | custom-call | flops 1 | bytes 1 | tf_op jit(solution)/shard_map/pallas_call | solution.py:735
  119.9 38.3 %shard_map.391 = (bf16[1024,768]{1,0:T(8,128)(2,1)}, bf16[1024,1536]{1,0:T(8,128)(2,1)}, bf16[1024,1536]{1,0:T(8,128)(2,1)}, f32[8,1536]{1,0:T(8,128)}, bf16[4,1...) custom-call(s32[1]{0:T(128)} %bitcast.core_ref.edge_ref.start_ref.next_ref, ...), custom_call_target="tpu_custom_call" | custom-call | flops 1 | bytes 1 | tf_op jit(solution)/shard_map/pallas_call | solution.py:786
  158.7 2.5 collective-permute-done.20
  162.3 2.3 convert_add_fusion.1
  171.8 5.0 %all-to-all-start.2 = ((bf16[4,256,768]{2,1,0:T(8,128)(2,1)}), bf16[4,256,768]{2,1,0:T(8,128)(2,1)}, u32[]{:S(2)}, u32[]{:S(2)}) async-start(bf16[4,256,768]{2,1,0:T(8,128)(2,1)} %bitcast.166), calls=%async_computation.2 | async-start | bytes 3145728 | tf_op jit(solution)/shard_map/all_to_all | solution.py:1063
  176.9 28.8 %shard_map.392 = (bf16[1024,1920]{1,0:T(8,128)(2,1)}, f32[8,1792]{1,0:T(8,128)}, f32[128,1536]{1,0:T(8,128)}, f32[8,1792]{1,0:T(8,128)}) custom-call(f32[1056,1792]{1,0:T(8,128)} %get-tuple-element.106.ext_ref, f32[1024,128]{1,0:T(8,128)} %get-tuple-element.107.dtr_ref, f32[1024,128]{1,0:T(8,128)} %get-tuple-element.108.cum_ref, ...), custom_call_target="tpu_custom_call" | custom-call | flops 1 | bytes 1 | tf_op jit(solution)/shard_map/pallas_call | solution.py:841
  210.0 29.0 %shard_map.393 = (bf16[1024,1920]{1,0:T(8,128)(2,1)}, f32[8,1792]{1,0:T(8,128)}, f32[128,1536]{1,0:T(8,128)}, f32[8,1792]{1,0:T(8,128)}) custom-call(f32[1056,1792]{1,0:T(8,128)} %get-tuple-element.106.ext_ref, f32[1024,128]{1,0:T(8,128)} %get-tuple-element.107.dtr_ref, f32[1024,128]{1,0:T(8,128)} %get-tuple-element.108.cum_ref, ...), custom_call_target="tpu_custom_call", output_to_operand_aliasing={{0}: (14, {})} | custom-call | flops 1 | bytes 1 | tf_op jit(solution)/shard_map/pallas_call | solution.py:841
  241.0 2.4 collective-permute-done.25
  244.2 2.9 collective-permute-start.26
  249.4 4.5 %collective-permute-done.23 = bf16[4,24,1536]{2,1,0:T(8,128)(2,1)S(1)} collective-permute-done((bf16[4,24,1536]{2,1,0:T(8,128)(2,1)S(1)}, bf16[4,24,1536]{2,1,0:T(8,128)(2,1)S(1)}, u32[]{:S(2)}, u32[]{:S(2)}) %collective-permute-start.23) | collective-permute-done | bytes 294944 | tf_op jit(solution)/shard_map/ppermute | solution.py:961
  258.9 17.6 %shard_map.394 = (bf16[1024,768]{1,0:T(8,128)(2,1)}, f32[8,768]{1,0:T(8,128)}, bf16[4,96,1024]{2,1,0:T(8,128)(2,1)}, f32[4,96,1024]{2,1,0:T(8,128)}, bf16[4,96,896]{2,1,0:T(8,128)(2,1)}, /*index=5*/f32[4,96,896]{2,1,0:T(8,128)}) custom-call(s32[1]{0:T(128)} %bitcast.core_ref.edge_ref.start_ref.next_ref._, bf16[1024,768]{1,0:T(8,128)(2,1)} %bitcast.139, ...), custom_call_target="tpu_custom_call" | custom-call | flops 1 | bytes 1 | tf_op jit(solution)/shard_map/pallas_call | solution.py:896
  277.2 3.7 %all-to-all-start.3 = ((bf16[4,256,768]{2,1,0:T(8,128)(2,1)}), bf16[4,256,768]{2,1,0:T(8,128)(2,1)S(1)}, u32[]{:S(2)}, u32[]{:S(2)}) async-start(bf16[4,256,768]{2,1,0:T(8,128)(2,1)} %bitcast.167), calls=%async_computation.3 | async-start | bytes 3145728 | tf_op jit(solution)/shard_map/all_to_all | solution.py:1063
  288.2 3.3 collective-permute-done.36
  292.0 3.3 collective-permute-done.37
  299.2 8.1 %collective-permute-done.38 = f32[8,768]{1,0:T(8,128)S(1)} collective-permute-done((f32[8,768]{1,0:T(8,128)S(1)}, f32[8,768]{1,0:T(8,128)S(1)}, u32[]{:S(2)}, u32[]{:S(2)}) %collective-permute-start.38) | collective-permute-done | bytes 24608 | tf_op jit(solution)/shard_map/ppermute | solution.py:961
  307.3 4.6 %collective-permute-start.39 = (f32[8,768]{1,0:T(8,128)S(1)}, f32[8,768]{1,0:T(8,128)S(1)}, u32[]{:S(2)}, u32[]{:S(2)}) collective-permute-start(f32[8,768]{1,0:T(8,128)S(1)} %add.201), channel_id=1, source_target_pairs={{0,2},{1,3},{2,0},{3,1},{4,6},{5,7},{6,4},{7,5},{8,10},{9,11},{10,... | collective-permute-start | bytes 73736 | tf_op jit(solution)/shard_map/ppermute | solution.py:961
  311.9 7.4 %collective-permute-done.39 = f32[8,768]{1,0:T(8,128)S(1)} collective-permute-done((f32[8,768]{1,0:T(8,128)S(1)}, f32[8,768]{1,0:T(8,128)S(1)}, u32[]{:S(2)}, u32[]{:S(2)}) %collective-permute-start.39) | collective-permute-done | bytes 24608 | tf_op jit(solution)/shard_map/ppermute | solution.py:961
  323.3 2.8 collective-permute-done.43
  336.8 3.6 %shard_map.395 = (f32[1,24]{1,0:T(1,128)}, f32[1,24]{1,0:T(1,128)}, f32[1,24]{1,0:T(1,128)}, f32[24,3352]{1,0:T(8,128)}, f32[24,3352]{1,0:T(8,128)}, /*index=5*/...) custom-call(f32[8]{0:T(128)} %pad_maximum_fusion.12.rates_ref, ...), custom_call_target="tpu_custom_call" | custom-call | flops 1 | bytes 1 | tf_op jit(solution)/shard_map/pallas_call | solution.py:940
  342.3 2.7 copy.62
  (210 shorter events, 94.0 us)
Async XLA Ops:
  2.7 15.1 %collective-permute-start = (bf16[24,4992]{1,0:T(8,128)(2,1)S(1)}, bf16[24,4992]{1,0:T(8,128)(2,1)S(1)}, u32[]{:S(2)}, u32[]{:S(2)}) collective-permute-start(bf16[24,4992]{1,0:T(8,128)(2,1)S(1)} %fusion.8), channel_id=1, source_target_pairs={{0,2},{1,3},{2,0},{3,1},{4,6},{5,7},{6,4},{7,5},{8,10},{9,11},{10,... | collective-permute-start | bytes 718856 | tf_op jit(solution)/shard_map/ppermute | solution.py:961
  29.6 13.7 %collective-permute-start.1 = (bf16[2,24,4992]{2,1,0:T(8,128)(2,1)S(1)}, bf16[2,24,4992]{2,1,0:T(8,128)(2,1)S(1)}, u32[]{:S(2)}, u32[]{:S(2)}) collective-permute-start(bf16[2,24,4992]{2,1,0:T(8,128)(2,1)S(1)} %pad_maximum_fusion.8), channel_id=1, source_target_pairs={{0,1},{1,0},{2,3},{3,2},{4,5},{5,4},{6,7},{7,6},{8,9},{9,8},{10,11... | collective-permute-start | bytes 1437704 | tf_op jit(solution)/shard_map/ppermute | solution.py:961
  31.9 8.3 %collective-permute-start.10 = (bf16[8,1792]{1,0:T(8,128)(2,1)S(1)}, bf16[8,1792]{1,0:T(8,128)(2,1)S(1)}, u32[]{:S(2)}, u32[]{:S(2)}) collective-permute-start(bf16[8,1792]{1,0:T(8,128)(2,1)S(1)} %add.171), channel_id=1, source_target_pairs={{0,16},{4,20},{8,24},{12,28},{16,0},{20,4},{24,8},{28,12},{1,17},{... | collective-permute-start | bytes 86024 | tf_op jit(solution)/shard_map/ppermute | solution.py:961
  35.5 40.6 %all-to-all-start = ((bf16[4,256,768]{2,1,0:T(8,128)(2,1)}), bf16[4,256,768]{2,1,0:T(8,128)(2,1)S(1)}, u32[]{:S(2)}, u32[]{:S(2)}) async-start(bf16[4,256,768]{2,1,0:T(8,128)(2,1)} %param.23), calls=%async_computation | async-start | bytes 3145728 | tf_op jit(solution)/shard_map/all_to_all | solution.py:1047
  43.7 7.4 %collective-permute-start.2 = (bf16[4,24,1024]{2,1,0:T(8,128)(2,1)S(1)}, bf16[4,24,1024]{2,1,0:T(8,128)(2,1)S(1)}, u32[]{:S(2)}, u32[]{:S(2)}) collective-permute-start(bf16[4,24,1024]{2,1,0:T(8,128)(2,1)S(1)} %slice.51), channel_id=1, source_target_pairs={{0,16},{4,20},{8,24},{12,28},{16,0},{20,4},{24,8},{28,12},{1,17},{... | collective-permute-start | bytes 589832 | tf_op jit(solution)/shard_map/ppermute | solution.py:961
  49.2 7.6 %collective-permute-start.5 = (bf16[2,4,24,896]{3,2,1,0:T(8,128)(2,1)S(1)}, bf16[2,4,24,896]{3,2,1,0:T(8,128)(2,1)S(1)}, u32[]{:S(2)}, u32[]{:S(2)}) collective-permute-start(bf16[2,4,24,896]{3,2,1,0:T(8,128)(2,1)S(1)} %pad_maximum_fusion.10), channel_id=1, source_target_pairs={{0,16},{4,20},{8,24},{12,28},{16,0},{20,4},{24,8},{28,12},{1,17},{... | collective-permute-start | bytes 1032200 | tf_op jit(solution)/shard_map/ppermute | solution.py:961
  51.2 9.1 %collective-permute-start.3 = (bf16[2,4,24,1024]{3,2,1,0:T(8,128)(2,1)S(1)}, bf16[2,4,24,1024]{3,2,1,0:T(8,128)(2,1)S(1)}, u32[]{:S(2)}, u32[]{:S(2)}) collective-permute-start(bf16[2,4,24,1024]{3,2,1,0:T(8,128)(2,1)S(1)} %pad_maximum_fusion.9), channel_id=1, source_target_pairs={{0,8},{4,12},{8,0},{12,4},{16,24},{20,28},{24,16},{28,20},{1,9},{5... | collective-permute-start | bytes 1179656 | tf_op jit(solution)/shard_map/ppermute | solution.py:961
  60.4 7.1 %collective-permute-start.12 = (bf16[4,48,768]{2,1,0:T(8,128)(2,1)S(1)}, bf16[4,48,768]{2,1,0:T(8,128)(2,1)S(1)}, u32[]{:S(2)}, u32[]{:S(2)}) collective-permute-start(bf16[4,48,768]{2,1,0:T(8,128)(2,1)S(1)} %bitcast.168), channel_id=1, source_target_pairs={{0,8},{4,12},{8,0},{12,4},{16,24},{20,28},{24,16},{28,20},{1,9},{5... | collective-permute-start | bytes 884744 | tf_op jit(solution)/shard_map/ppermute | solution.py:961
  62.8 11.0 %collective-permute-start.14 = (bf16[4,96,896]{2,1,0:T(8,128)(2,1)S(1)}, bf16[4,96,896]{2,1,0:T(8,128)(2,1)S(1)}, u32[]{:S(2)}, u32[]{:S(2)}) collective-permute-start(bf16[4,96,896]{2,1,0:T(8,128)(2,1)S(1)} %bitcast.151), channel_id=1, source_target_pairs={{0,4},{4,0},{8,12},{12,8},{16,20},{20,16},{24,28},{28,24},{1,5},{5... | collective-permute-start | bytes 2064392 | tf_op jit(solution)/shard_map/ppermute | solution.py:961
  62.9 11.8 %collective-permute-start.13 = (bf16[4,96,1024]{2,1,0:T(8,128)(2,1)S(1)}, bf16[4,96,1024]{2,1,0:T(8,128)(2,1)}, u32[]{:S(2)}, u32[]{:S(2)}) collective-permute-start(bf16[4,96,1024]{2,1,0:T(8,128)(2,1)S(1)} %bitcast.147), channel_id=1, source_target_pairs={{0,4},{4,0},{8,12},{12,8},{16,20},{20,16},{24,28},{28,24},{1,5},{5... | collective-permute-start | bytes 2359304 | tf_op jit(solution)/shard_map/ppermute | solution.py:961
  63.4 9.4 %collective-permute-start.11 = (bf16[4,24,1536]{2,1,0:T(8,128)(2,1)S(1)}, bf16[4,24,1536]{2,1,0:T(8,128)(2,1)S(1)}, u32[]{:S(2)}, u32[]{:S(2)}) collective-permute-start(bf16[4,24,1536]{2,1,0:T(8,128)(2,1)S(1)} %slice.48), channel_id=1, source_target_pairs={{0,16},{4,20},{8,24},{12,28},{16,0},{20,4},{24,8},{28,12},{1,17},{... | collective-permute-start | bytes 884744 | tf_op jit(solution)/shard_map/ppermute | solution.py:961
  76.1 36.0 %collective-permute-start.17 = (bf16[2,4,48,768]{3,2,1,0:T(8,128)(2,1)}, bf16[2,4,48,768]{3,2,1,0:T(8,128)(2,1)}, u32[]{:S(2)}, u32[]{:S(2)}) collective-permute-start(bf16[2,4,48,768]{3,2,1,0:T(8,128)(2,1)} %pad_maximum_fusion.7), channel_id=1, source_target_pairs={{0,16},{4,20},{8,24},{12,28},{16,0},{20,4},{24,8},{28,12},{1,17},{... | collective-permute-start | bytes 1769480 | tf_op jit(solution)/shard_map/ppermute | solution.py:961
  76.6 37.1 %collective-permute-start.15 = (bf16[2,4,24,1536]{3,2,1,0:T(8,128)(2,1)}, bf16[2,4,24,1536]{3,2,1,0:T(8,128)(2,1)}, u32[]{:S(2)}, u32[]{:S(2)}) collective-permute-start(bf16[2,4,24,1536]{3,2,1,0:T(8,128)(2,1)} %pad_maximum_fusion.6), channel_id=1, source_target_pairs={{0,8},{4,12},{8,0},{12,4},{16,24},{20,28},{24,16},{28,20},{1,9},{5... | collective-permute-start | bytes 1769480 | tf_op jit(solution)/shard_map/ppermute | solution.py:961
  78.1 40.5 %all-to-all-start.1 = ((bf16[4,256,768]{2,1,0:T(8,128)(2,1)}), bf16[4,256,768]{2,1,0:T(8,128)(2,1)S(1)}, u32[]{:S(2)}, u32[]{:S(2)}) async-start(bf16[4,256,768]{2,1,0:T(8,128)(2,1)} %param.24), calls=%async_computation.1 | async-start | bytes 3145728 | tf_op jit(solution)/shard_map/all_to_all | solution.py:1047
  158.4 8.7 %collective-permute-start.19 = (bf16[4,192,768]{2,1,0:T(8,128)(2,1)}, bf16[4,192,768]{2,1,0:T(8,128)(2,1)S(1)}, u32[]{:S(2)}, u32[]{:S(2)}) collective-permute-start(bf16[4,192,768]{2,1,0:T(8,128)(2,1)} %get-tuple-element.112), channel_id=1, source_target_pairs={{0,4},{4,0},{8,12},{12,8},{16,20},{20,16},{24,28},{28,24},{1,5},{5... | collective-permute-start | bytes 3538952 | tf_op jit(solution)/shard_map/ppermute | solution.py:961
  165.6 40.1 %collective-permute-start.22 = (bf16[2,4,24,1536]{3,2,1,0:T(8,128)(2,1)}, bf16[2,4,24,1536]{3,2,1,0:T(8,128)(2,1)}, u32[]{:S(2)}, u32[]{:S(2)}) collective-permute-start(bf16[2,4,24,1536]{3,2,1,0:T(8,128)(2,1)} %fusion), channel_id=1, source_target_pairs={{0,16},{4,20},{8,24},{12,28},{16,0},{20,4},{24,8},{28,12},{1,17},{... | collective-permute-start | bytes 1769480 | tf_op jit(solution)/shard_map/ppermute | solution.py:961
  171.3 35.7 %collective-permute-start.21 = (bf16[2,4,48,768]{3,2,1,0:T(8,128)(2,1)}, bf16[2,4,48,768]{3,2,1,0:T(8,128)(2,1)}, u32[]{:S(2)}, u32[]{:S(2)}) collective-permute-start(bf16[2,4,48,768]{3,2,1,0:T(8,128)(2,1)} %fusion.1), channel_id=1, source_target_pairs={{0,8},{4,12},{8,0},{12,4},{16,24},{20,28},{24,16},{28,20},{1,9},{5... | collective-permute-start | bytes 1769480 | tf_op jit(solution)/shard_map/ppermute | solution.py:961
  171.8 87.1 %all-to-all-start.2 = ((bf16[4,256,768]{2,1,0:T(8,128)(2,1)}), bf16[4,256,768]{2,1,0:T(8,128)(2,1)}, u32[]{:S(2)}, u32[]{:S(2)}) async-start(bf16[4,256,768]{2,1,0:T(8,128)(2,1)} %bitcast.166), calls=%async_computation.2 | async-start | bytes 3145728 | tf_op jit(solution)/shard_map/all_to_all | solution.py:1063
  208.7 40.6 %collective-permute-start.24 = (bf16[4,48,768]{2,1,0:T(8,128)(2,1)S(1)}, bf16[4,48,768]{2,1,0:T(8,128)(2,1)S(1)}, u32[]{:S(2)}, u32[]{:S(2)}) collective-permute-start(bf16[4,48,768]{2,1,0:T(8,128)(2,1)S(1)} %fusion.6), channel_id=1, source_target_pairs={{0,16},{4,20},{8,24},{12,28},{16,0},{20,4},{24,8},{28,12},{1,17},{... | collective-permute-start | bytes 884744 | tf_op jit(solution)/shard_map/ppermute | solution.py:961
  247.2 6.8 %collective-permute-start.23 = (bf16[4,24,1536]{2,1,0:T(8,128)(2,1)S(1)}, bf16[4,24,1536]{2,1,0:T(8,128)(2,1)S(1)}, u32[]{:S(2)}, u32[]{:S(2)}) collective-permute-start(bf16[4,24,1536]{2,1,0:T(8,128)(2,1)S(1)} %fusion.5), channel_id=1, source_target_pairs={{0,8},{4,12},{8,0},{12,4},{16,24},{20,28},{24,16},{28,20},{1,9},{5... | collective-permute-start | bytes 884744 | tf_op jit(solution)/shard_map/ppermute | solution.py:961
  254.2 22.3 %collective-permute-start.27 = (bf16[24,3072]{1,0:T(8,128)(2,1)S(1)}, bf16[24,3072]{1,0:T(8,128)(2,1)S(1)}, u32[]{:S(2)}, u32[]{:S(2)}) collective-permute-start(bf16[24,3072]{1,0:T(8,128)(2,1)S(1)} %get-tuple-element.164), channel_id=1, source_target_pairs={{0,1},{1,2},{2,3},{3,0},{4,5},{5,6},{6,7},{7,4},{8,9},{9,10},{10,1... | collective-permute-start | bytes 442376 | tf_op jit(solution)/shard_map/ppermute | solution.py:1028
  255.7 20.8 %collective-permute-start.28 = (bf16[24,3072]{1,0:T(8,128)(2,1)S(1)}, bf16[24,3072]{1,0:T(8,128)(2,1)S(1)}, u32[]{:S(2)}, u32[]{:S(2)}) collective-permute-start(bf16[24,3072]{1,0:T(8,128)(2,1)S(1)} %get-tuple-element.163), channel_id=1, source_target_pairs={{0,2},{1,3},{2,0},{3,1},{4,6},{5,7},{6,4},{7,5},{8,10},{9,11},{10,... | collective-permute-start | bytes 442376 | tf_op jit(solution)/shard_map/ppermute | solution.py:1028
  256.3 20.2 %collective-permute-start.29 = (bf16[24,3072]{1,0:T(8,128)(2,1)S(1)}, bf16[24,3072]{1,0:T(8,128)(2,1)S(1)}, u32[]{:S(2)}, u32[]{:S(2)}) collective-permute-start(bf16[24,3072]{1,0:T(8,128)(2,1)S(1)} %get-tuple-element.162), channel_id=1, source_target_pairs={{0,3},{1,0},{2,1},{3,2},{4,7},{5,4},{6,5},{7,6},{8,11},{9,8},{10,9... | collective-permute-start | bytes 442376 | tf_op jit(solution)/shard_map/ppermute | solution.py:1028
  276.6 6.7 %collective-permute-start.30 = (bf16[4,96,1024]{2,1,0:T(8,128)(2,1)}, bf16[4,96,1024]{2,1,0:T(8,128)(2,1)}, u32[]{:S(2)}, u32[]{:S(2)}) collective-permute-start(bf16[4,96,1024]{2,1,0:T(8,128)(2,1)} %get-tuple-element.137), channel_id=1, source_target_pairs={{0,4},{4,0},{8,12},{12,8},{16,20},{20,16},{24,28},{28,24},{1,5},{5... | collective-permute-start | bytes 2359304 | tf_op jit(solution)/shard_map/ppermute | solution.py:961
  277.2 63.1 %all-to-all-start.3 = ((bf16[4,256,768]{2,1,0:T(8,128)(2,1)}), bf16[4,256,768]{2,1,0:T(8,128)(2,1)S(1)}, u32[]{:S(2)}, u32[]{:S(2)}) async-start(bf16[4,256,768]{2,1,0:T(8,128)(2,1)} %bitcast.167), calls=%async_computation.3 | async-start | bytes 3145728 | tf_op jit(solution)/shard_map/all_to_all | solution.py:1063
  282.4 38.2 %collective-permute-start.42 = (bf16[2,4,24,896]{3,2,1,0:T(8,128)(2,1)S(1)}, bf16[2,4,24,896]{3,2,1,0:T(8,128)(2,1)S(1)}, u32[]{:S(2)}, u32[]{:S(2)}) collective-permute-start(bf16[2,4,24,896]{3,2,1,0:T(8,128)(2,1)S(1)} %fusion.4), channel_id=1, source_target_pairs={{0,16},{4,20},{8,24},{12,28},{16,0},{20,4},{24,8},{28,12},{1,17},{... | collective-permute-start | bytes 1032200 | tf_op jit(solution)/shard_map/ppermute | solution.py:961
  286.1 11.3 %collective-permute-start.33 = (f32[8,1792]{1,0:T(8,128)S(1)}, f32[8,1792]{1,0:T(8,128)S(1)}, u32[]{:S(2)}, u32[]{:S(2)}) collective-permute-start(f32[8,1792]{1,0:T(8,128)S(1)} %add.195), channel_id=1, source_target_pairs={{0,8},{4,12},{8,0},{12,4},{16,24},{20,28},{24,16},{28,20},{1,9},{5... | collective-permute-start | bytes 172040 | tf_op jit(solution)/shard_map/ppermute | solution.py:961
  295.4 12.0 %collective-permute-start.38 = (f32[8,768]{1,0:T(8,128)S(1)}, f32[8,768]{1,0:T(8,128)S(1)}, u32[]{:S(2)}, u32[]{:S(2)}) collective-permute-start(f32[8,768]{1,0:T(8,128)S(1)} %add.200), channel_id=1, source_target_pairs={{0,1},{1,0},{2,3},{3,2},{4,5},{5,4},{6,7},{7,6},{8,9},{9,8},{10,11... | collective-permute-start | bytes 73736 | tf_op jit(solution)/shard_map/ppermute | solution.py:961
  297.3 22.6 %collective-permute-start.34 = (f32[8,1792]{1,0:T(8,128)S(1)}, f32[8,1792]{1,0:T(8,128)S(1)}, u32[]{:S(2)}, u32[]{:S(2)}) collective-permute-start(f32[8,1792]{1,0:T(8,128)S(1)} %add.196), channel_id=1, source_target_pairs={{0,16},{4,20},{8,24},{12,28},{16,0},{20,4},{24,8},{28,12},{1,17},{... | collective-permute-start | bytes 172040 | tf_op jit(solution)/shard_map/ppermute | solution.py:961
  298.0 23.6 %collective-permute-start.40 = (bf16[2,4,24,1024]{3,2,1,0:T(8,128)(2,1)S(1)}, bf16[2,4,24,1024]{3,2,1,0:T(8,128)(2,1)S(1)}, u32[]{:S(2)}, u32[]{:S(2)}) collective-permute-start(bf16[2,4,24,1024]{3,2,1,0:T(8,128)(2,1)S(1)} %fusion.3), channel_id=1, source_target_pairs={{0,8},{4,12},{8,0},{12,4},{16,24},{20,28},{24,16},{28,20},{1,9},{5... | collective-permute-start | bytes 1179656 | tf_op jit(solution)/shard_map/ppermute | solution.py:961
  307.3 12.0 %collective-permute-start.39 = (f32[8,768]{1,0:T(8,128)S(1)}, f32[8,768]{1,0:T(8,128)S(1)}, u32[]{:S(2)}, u32[]{:S(2)}) collective-permute-start(f32[8,768]{1,0:T(8,128)S(1)} %add.201), channel_id=1, source_target_pairs={{0,2},{1,3},{2,0},{3,1},{4,6},{5,7},{6,4},{7,5},{8,10},{9,11},{10,... | collective-permute-start | bytes 73736 | tf_op jit(solution)/shard_map/ppermute | solution.py:961
  327.6 8.4 %collective-permute-start.45 = (bf16[24,1920]{1,0:T(8,128)(2,1)S(1)}, bf16[24,1920]{1,0:T(8,128)(2,1)S(1)}, u32[]{:S(2)}, u32[]{:S(2)}) collective-permute-start(bf16[24,1920]{1,0:T(8,128)(2,1)S(1)} %get-tuple-element.181), channel_id=1, source_target_pairs={{0,2},{1,3},{2,0},{3,1},{4,6},{5,7},{6,4},{7,5},{8,10},{9,11},{10,... | collective-permute-start | bytes 276488 | tf_op jit(solution)/shard_map/ppermute | solution.py:1028
  (42 other events, 184.3 us)

commit v2 on v1

--- a/solution.py
+++ b/solution.py
@@ -30,7 +30,7 @@
 
 
 def sigmoid(value):
-    return 1.0 / (1.0 + jnp.exp(-value))
+    return 0.5 * jnp.tanh(0.5 * value) + 0.5
 
 
 def column(ref_value, at, width):
@@ -62,9 +62,14 @@
         summed = (
             summed
             + conv_ref[tap : tap + 1, at : at + lanes]
-            * ext_ref[base + tap : base + tap + length, at : at + lanes]
+            * ext_ref[at // lanes, base + tap : base + tap + length, :]
         )
     return summed
+
+
+def put_columns(ext_ref, rows, values, chunk):
+    for at in range(0, values.shape[1], lanes):
+        ext_ref[chunk + at // lanes, rows, :] = values[:, at : at + lanes]
 
 
 def step_sizes(dt_raw, head_ref, head_lane):
@@ -117,27 +122,32 @@
     head_ref,
     skip_ref,
     start_ref,
-    normed_ref,
-    ext_ref,
-    dtr_ref,
-    cum_ref,
-    y_ref,
-    sin_ref,
-    end_ref,
-    tail_ref,
-    state_ref,
-    carried_ref,
-    weighted_ref,
-    wa_ref,
-    wb_ref,
-    wa_sems,
-    wb_sems,
-    *,
+    before_ref,
+    *refs,
     heads,
     inner,
     taps,
     grouped,
+    resumed,
 ):
+    (
+        normed_ref,
+        ext_ref,
+        dtr_ref,
+        cum_ref,
+        y_ref,
+        sin_ref,
+        end_ref,
+        after_ref,
+        tail_ref,
+        state_ref,
+        carried_ref,
+        weighted_ref,
+        wa_ref,
+        wb_ref,
+        wa_sems,
+        wb_sems,
+    ) = refs[6:] if resumed else refs
     block = pl.program_id(1)
     length, width = x_ref.shape
 
@@ -160,23 +170,30 @@
 
     @pl.when(block == 0)
     def _():
-        if grouped:
+        if resumed:
+            state_ref[...] = start_ref[...]
+            tail_ref[...] = before_ref[...]
+        elif grouped:
             state_ref[...] = start_ref[...]
             edge = norm_of(edge_ref[...])
-            tail_ref[:, :wide_a] = dot(edge, wa_ref[...])
-            tail_ref[:, wide_a:] = dot(edge, wb_ref[...])[:, : conv_dim - wide_a]
+            put_columns(tail_ref, slice(0, 8), dot(edge, wa_ref[...]), 0)
+            edge_b = dot(edge, wb_ref[...])[:, : conv_dim - wide_a]
+            put_columns(tail_ref, slice(0, 8), edge_b, wide_a // lanes)
         else:
             state_ref[...] = jnp.zeros_like(state_ref)
             tail_ref[...] = jnp.zeros_like(tail_ref)
 
     normed = norm_of(x_ref[...])
     normed_ref[...] = normed
-    ext_ref[0:8, :] = tail_ref[...]
-    ext_ref[8 : 8 + length, :wide_a] = dot(normed, wa_ref[...])
+    ext_ref[:, 0:8, :] = tail_ref[...]
+    own_rows = slice(8, 8 + length)
+    for at in range(0, wide_a, 2 * lanes):
+        product = dot(normed, wa_ref[:, at : at + 2 * lanes])
+        put_columns(ext_ref, own_rows, product, at // lanes)
     second = dot(normed, wb_ref[...])
-    ext_ref[8 : 8 + length, wide_a:] = second[:, : conv_dim - wide_a]
+    put_columns(ext_ref, own_rows, second[:, : conv_dim - wide_a], wide_a // lanes)
     dt_raw = second[:, conv_dim - wide_a :]
-    tail_ref[...] = ext_ref[length : length + 8, :]
+    tail_ref[...] = ext_ref[:, length : length + 8, :]
 
     lane = lax.broadcasted_iota(jnp.int32, (length, lanes), 1)
     low_lane = lane < lanes // 2
@@ -227,7 +244,7 @@
             early = cum_rows[head : head + 1, :half]
             late = cum_rows[head : head + 1, half:]
             mix_00 = jnp.exp2(jnp.minimum(cum_col[:half] - early, 0.0)) * scores_00
-            mix_10 = jnp.exp2(jnp.minimum(cum_col[half:] - early, 0.0)) * scores_10
+            mix_10 = jnp.exp2(cum_col[half:] - early) * scores_10
             mix_11 = jnp.exp2(jnp.minimum(cum_col[half:] - late, 0.0)) * scores_11
             part_top = dot(mix_00.astype(bf16), own[:half])
             part_bottom = dot(
@@ -241,19 +258,22 @@
         )
         y_ref[0:half, at : at + lanes] = top + rest[:half]
         y_ref[half:length, at : at + lanes] = bottom + rest[half:]
-        fresh = dot(keys, weighted_ref[:, at : at + lanes], 0, 0)
-        state_ref[:, at : at + lanes] = jnp.exp2(last) * state_ref[:, at : at + lanes] + fresh
+        state_ref[:, at : at + lanes] = jnp.exp2(last) * state_ref[:, at : at + lanes]
+
+    state_ref[...] += dot(keys, weighted_ref[...], 0, 0)
 
     @pl.when(block == pl.num_programs(1) - 1)
     def _():
         end_ref[...] = state_ref[...]
+        after_ref[...] = tail_ref[...]
 
 
 def gate_kernel(
     core_ref,
     normed_ref,
     x_ref,
-    cot_ref,
+    cot_a_ref,
+    cot_b_ref,
     y_ref,
     wg_own,
     wg_other,
@@ -271,6 +291,7 @@
     gate_ref,
     dno_ref,
     low_ref,
+    cot_ref,
     out_sum,
     gate_sum,
     wg_ref,
@@ -294,6 +315,8 @@
             copy.wait()
 
     gate_ref[...] = dot(normed_ref[...], wg_ref[...])
+    cot_ref[:, : cot_a_ref.shape[1]] = cot_a_ref[...]
+    cot_ref[:, cot_a_ref.shape[1] :] = cot_b_ref[...]
     dno_ref[...] = dot(cot_ref[...], wo_ref[...], 1, 1)
     squares = jnp.zeros((length, lanes), f32)
     crosses = jnp.zeros((length, lanes), f32)
@@ -391,14 +414,14 @@
     def _():
         if fresh:
             grad_ref[...] = jnp.zeros_like(grad_ref)
-            dsx_ref[length : length + 8, :] = jnp.zeros((8, conv_dim), f32)
+            dsx_ref[:, length : length + 8, :] = jnp.zeros((conv_dim // lanes, 8, lanes), f32)
         else:
             grad_ref[...] = start_ref[...]
-            dsx_ref[length : length + 8, :] = next_ref[...]
+            dsx_ref[:, length : length + 8, :] = next_ref[...]
 
     @pl.when(step > 0)
     def _():
-        dsx_ref[length : length + 8, :] = dsx_ref[0:8, :]
+        dsx_ref[:, length : length + 8, :] = dsx_ref[:, 0:8, :]
 
     lane = lax.broadcasted_iota(jnp.int32, (length, lanes), 1)
     low_lane = lane < lanes // 2
@@ -414,15 +437,16 @@
 
     def put_grad(at, d_summed):
         here = slice(at, at + lanes)
-        dsx_ref[0:length, here] = d_summed
+        chunk = at // lanes
+        dsx_ref[chunk, 0:length, :] = d_summed
         total = None
         for tap in range(taps):
             base = 8 - (taps - 1) + tap
             dconv_ref[tap : tap + 1, here] += jnp.sum(
-                d_summed * ext_ref[base : base + length, here], axis=0, keepdims=True
+                d_summed * ext_ref[chunk, base : base + length, :], axis=0, keepdims=True
             )
             back = taps - 1 - tap
-            term = conv_ref[tap : tap + 1, here] * dsx_ref[back : back + length, here]
+            term = conv_ref[tap : tap + 1, here] * dsx_ref[chunk, back : back + length, :]
             total = term if total is None else total + term
         dconv_ref[taps : taps + 1, here] += jnp.sum(d_summed, axis=0, keepdims=True)
         dproj_ref[:, here] = total.astype(bf16)
@@ -455,6 +479,7 @@
         tail = jnp.exp2(last - cum_rep)
         d_y = dy_ref[:, here]
         d_yf = d_y.astype(f32)
+        d_y_t = d_yf.T.astype(bf16)
         dye_ref[:, here] = (d_yf * jnp.exp2(cum_rep)).astype(bf16)
         top = None
         bottom = None
@@ -466,7 +491,7 @@
             early = cum_rows[head : head + 1, :half]
             late = cum_rows[head : head + 1, half:]
             decay_00 = jnp.exp2(jnp.minimum(early - cum_col[:half], 0.0))
-            decay_01 = jnp.exp2(jnp.minimum(late - cum_col[:half], 0.0))
+            decay_01 = jnp.exp2(late - cum_col[:half])
             decay_11 = jnp.exp2(jnp.minimum(late - cum_col[half:], 0.0))
             mix_0 = jnp.concatenate(
                 [(decay_00 * scores_00).astype(bf16), (decay_01 * scores_01).astype(bf16)], axis=1
@@ -476,8 +501,8 @@
             part_bottom = dot(mix_1, own_dy[half:])
             top = part_top if top is None else top + part_top
             bottom = part_bottom if bottom is None else bottom + part_bottom
-            d_mix_0 = dot(own_x[:half], d_y, 1, 1)
-            d_mix_1 = dot(own_x[half:], d_y[half:], 1, 1)
+            d_mix_0 = dot(own_x[:half], d_y_t)
+            d_mix_1 = dot(own_x[half:], d_y_t[:, half:])
             ds_00 = ds_00 + decay_00 * d_mix_0[:, :half]
             ds_01 = ds_01 + decay_01 * d_mix_0[:, half:]
             ds_11 = ds_11 + decay_11 * d_mix_1
@@ -499,10 +524,9 @@
         )
         rows_ref[1:2, here] = jnp.sum(d_yf * values, axis=0, keepdims=True)
         put_grad(at, (d_stepped * dt_rep + skip * d_yf) * slope)
-        grad_ref[:, here] = total_decay * grad_ref[:, here] + dot(
-            queries, dye_ref[:, here], 0, 0
-        )
-
+        grad_ref[:, here] = total_decay * grad_ref[:, here]
+
+    grad_ref[...] += dot(queries, dye_ref[...], 0, 0)
     ds_00 = jnp.where(diag, ds_00, 0.0).astype(bf16)
     ds_11 = jnp.where(diag, ds_11, 0.0).astype(bf16)
     ds_01 = ds_01.astype(bf16)
@@ -551,7 +575,7 @@
     @pl.when(step == pl.num_programs(1) - 1)
     def _():
         end_ref[...] = grad_ref[...]
-        lead_ref[...] = dsx_ref[0:8, :]
+        lead_ref[...] = dsx_ref[:, 0:8, :]
 
 
 def input_grad_kernel(
@@ -560,6 +584,7 @@
     dgate_ref,
     dproj_ref,
     small_ref,
+    dsmall_in_ref,
     wg_own,
     wg_other,
     wa_own,
@@ -592,7 +617,7 @@
         copies = fetch_weight(core_ref, wg_own, wg_other, wg_ref, wg_sems)
         copies += fetch_weight(core_ref, wa_own, wa_other, wa_ref, wa_sems)
         copies += fetch_weight(core_ref, wb_own, wb_other, wb_ref, wb_sems)
-        dsmall_ref[...] = jnp.zeros_like(dsmall_ref)
+        dsmall_ref[...] = dsmall_in_ref[...]
         a_sum[...] = jnp.zeros_like(a_sum)
         b_sum[...] = jnp.zeros_like(b_sum)
         for copy in copies:
@@ -607,7 +632,9 @@
     rows = x_ref[...].astype(f32)
     scale = lax.rsqrt(jnp.mean(rows * rows, axis=-1, keepdims=True) + norm_eps)
     scaled = rows * scale
-    dsmall_ref[0:1, :] += jnp.sum(scaled * d_normed, axis=0, keepdims=True)
+    dsmall_ref[gain_row : gain_row + 1, :width] += jnp.sum(
+        scaled * d_normed, axis=0, keepdims=True
+    )
     gain = small_ref[gain_row : gain_row + 1, :width]
     normed_ref[...] = (scaled * gain).astype(bf16)
     add_product(a_sum, normed_ref, dproj_ref[:, :wide_a])
@@ -627,14 +654,13 @@
 
 def adam_kernel(
     rates_ref,
-    sums_ref,
-    norm_ref,
     *refs,
     heads,
     taps,
     at_refs,
     arrivals,
 ):
+    sum_refs, refs = refs[:arrivals], refs[arrivals:]
     rest_refs, front_refs, refs = refs[:arrivals], refs[arrivals : 2 * arrivals], refs[2 * arrivals :]
     ins, outs = refs[:18], refs[18:]
     learn_rate, decay_rate = rates_ref[0], rates_ref[3]
@@ -671,17 +697,30 @@
     update(4, rest[:, inner + half :], (slice(rows, 2 * rows), slice(None)))
     me = rates_ref[6].astype(jnp.int32)
 
-    def own(sums, at, count):
+    place = rates_ref[7].astype(jnp.int32)
+    terms = [ref[...] for ref in sum_refs]
+    sums = terms[0]
+    for term in terms[1:]:
+        sums = sums + term
+
+    def own(at, count):
         wide = sums.shape[1]
         shift = lax.rem(wide - me * count, wide)
-        return pltpu.roll(sums[...], shift, 1)[at, :count]
-
-    update(0, own(norm_ref, slice(0, 1), ins[0].shape[1]), everything)
-    update(2, own(sums_ref, slice(0, taps + 1), ins[6].shape[1]), everything)
-    update(3, own(sums_ref, slice(taps + 2, taps + 3), ins[9].shape[1]), everything)
+        return pltpu.roll(sums, shift, 1)[at, :count]
+
+    update(0, own(slice(taps + 1, taps + 2), ins[0].shape[1]), everything)
+    update(2, own(slice(0, taps + 1), ins[6].shape[1]), everything)
+    update(3, own(slice(taps + 2, taps + 3), ins[9].shape[1]), everything)
+    sums = jnp.zeros_like(sums)
+    for source in range(arrivals):
+        distance = lax.rem(place + arrivals - source, arrivals)
+        term = terms[0]
+        for which in range(1, arrivals):
+            term = jnp.where(distance == which, terms[which], term)
+        sums = sums + term
     head_row = slice(taps + 3, taps + 4)
     for row in range(3):
-        grad = sums_ref[head_row, row * lanes : row * lanes + heads]
+        grad = sums[head_row, row * lanes : row * lanes + heads]
         update(5, grad, (slice(row, row + 1), slice(None)))
 
 
@@ -725,19 +764,39 @@
     return [jax.ShapeDtypeStruct(shape, bf16), jax.ShapeDtypeStruct(shape, f32)]
 
 
-def mixer_forward(dims, core, tokens, wa, wb, small, head, skip, grouped, edge, start):
+def mixer_forward(dims, core, tokens, wa, wb, small, head, skip, edge, start, grouped, kept, blocks):
     part, size, piece, width, inner, heads, taps = dims
+    first, count = blocks
     conv_dim = small.shape[1]
     state_dim = (conv_dim - inner) // 2
-    blocks = part * size
-    rows = blocks * piece
+    all_blocks = part * size
+    rows = all_blocks * piece
     ext_rows = piece + 8
+    chunks = conv_dim // lanes
+    resumed = kept is not None
+
+    def by_block(shape):
+        return pl.BlockSpec(shape, lambda p, b: (p * size + first + b, 0))
+
+    tail_block = pl.BlockSpec((chunks, 8, lanes), lambda p, b: (p, 0, 0))
+    before = core
+    if resumed:
+        *arrays, start, before = kept
+    else:
+        arrays = []
     return pl.pallas_call(
-        partial(mixer_forward_kernel, heads=heads, inner=inner, taps=taps, grouped=grouped),
-        grid=(part, size),
+        partial(
+            mixer_forward_kernel,
+            heads=heads,
+            inner=inner,
+            taps=taps,
+            grouped=grouped,
+            resumed=resumed,
+        ),
+        grid=(part, count),
         in_specs=[
             SMEM,
-            by_block((piece, width), size),
+            by_block((piece, width)),
             by_part((8, width)) if grouped else ANY,
             ANY,
             ANY,
@@ -746,43 +805,50 @@
             whole(small.shape),
             whole(head.shape),
             whole(skip.shape),
-            by_part((state_dim, inner)) if grouped else ANY,
-        ],
+            by_part((state_dim, inner)) if grouped or resumed else ANY,
+            tail_block if resumed else ANY,
+        ]
+        + [ANY] * len(arrays),
         out_specs=[
-            by_block((piece, width), size),
-            by_block((ext_rows, conv_dim), size),
-            by_block((piece, lanes), size),
-            by_block((piece, lanes), size),
-            by_block((piece, inner), size),
-            by_block((state_dim, inner), size),
+            by_block((piece, width)),
+            pl.BlockSpec((chunks, ext_rows, lanes), lambda p, b: (p * size + first + b, 0, 0)),
+            by_block((piece, lanes)),
+            by_block((piece, lanes)),
+            by_block((piece, inner)),
+            by_block((state_dim, inner)),
             by_part((state_dim, inner)),
+            tail_block,
         ],
         out_shape=[
             jax.ShapeDtypeStruct((rows, width), bf16),
-            jax.ShapeDtypeStruct((blocks * ext_rows, conv_dim), f32),
+            jax.ShapeDtypeStruct((all_blocks * chunks, ext_rows, lanes), f32),
             jax.ShapeDtypeStruct((rows, lanes), f32),
             jax.ShapeDtypeStruct((rows, lanes), f32),
             jax.ShapeDtypeStruct((rows, inner), f32),
-            jax.ShapeDtypeStruct((blocks * state_dim, inner), bf16),
+            jax.ShapeDtypeStruct((all_blocks * state_dim, inner), bf16),
             jax.ShapeDtypeStruct((part * state_dim, inner), f32),
+            jax.ShapeDtypeStruct((part * chunks, 8, lanes), f32),
         ],
         scratch_shapes=[
-            pltpu.VMEM((8, conv_dim), f32),
+            pltpu.VMEM((chunks, 8, lanes), f32),
             pltpu.VMEM((state_dim, inner), f32),
             pltpu.VMEM((piece, inner), f32),
             pltpu.VMEM((piece, inner), bf16),
         ]
         + weight_scratch(wa, wb),
+        input_output_aliases={12 + at: at for at in range(len(arrays))},
         compiler_params=params(),
         cost_estimate=cost(1, 1, 0),
-    )(core, tokens, edge, *wa, *wb, small, head, skip, start)
-
-
-def gate_step(dims, core, normed, tokens, cots, y, wg, wo, small):
+    )(core, tokens, edge, *wa, *wb, small, head, skip, start, before, *arrays)
+
+
+def gate_step(dims, core, normed, tokens, cots_b, y, wg, wo, small):
     part, size, piece, width, inner, heads, taps = dims
     rows = part * size * piece
     blocks = wo[0].shape[0]
     handed = handed_out(inner, width, blocks) + handed_out(width, inner, blocks)
+    wide_b = cots_b.shape[1]
+    at_a = width // (width - wide_b)
     return pl.pallas_call(
         partial(gate_kernel, gain_row=taps + 2),
         grid=(part, size),
@@ -790,7 +856,8 @@
             SMEM,
             by_block((piece, width), size),
             by_block((piece, width), size),
-            by_block((piece, width), size),
+            pl.BlockSpec((piece, width - wide_b), lambda p, b: (p * size + b, at_a)),
+            by_block((piece, wide_b), size),
             by_block((piece, inner), size),
             ANY,
             ANY,
@@ -816,13 +883,14 @@
             pltpu.VMEM((piece, inner), f32),
             pltpu.VMEM((piece, inner), f32),
             pltpu.VMEM((piece, inner), bf16),
+            pltpu.VMEM((piece, width), bf16),
             pltpu.VMEM((inner, width), f32),
             pltpu.VMEM((width, inner), f32),
         ]
         + weight_scratch(wg, wo),
         compiler_params=params(),
         cost_estimate=cost(1, 1, 0),
-    )(core, normed, tokens, cots, y, *wg, *wo, small)
+    )(core, normed, tokens, tokens, cots_b, y, *wg, *wo, small)
 
 
 def mixer_backward(dims, saved, consts, carry, blocks, fresh):
@@ -832,8 +900,10 @@
     conv_dim = small.shape[1]
     state_dim = (conv_dim - inner) // 2
     ext_rows = piece + 8
+    chunks = conv_dim // lanes
     wide = conv_dim + lanes
     dproj, dsmall, state, lead = carry
+    lead_block = pl.BlockSpec((chunks, 8, lanes), lambda p, s: (p, 0, 0))
 
     def by_block(shape):
         return pl.BlockSpec(shape, lambda p, s: (p * size + (first + count - 1 - s), 0))
@@ -842,7 +912,9 @@
         partial(mixer_backward_kernel, heads=heads, inner=inner, taps=taps, fresh=fresh),
         grid=(part, count),
         in_specs=[
-            by_block((ext_rows, conv_dim)),
+            pl.BlockSpec(
+                (chunks, ext_rows, lanes), lambda p, s: (p * size + (first + count - 1 - s), 0, 0)
+            ),
             by_block((piece, lanes)),
             by_block((piece, lanes)),
             by_block((piece, inner)),
@@ -853,7 +925,7 @@
             whole(skip.shape),
             whole(summing.shape),
             ANY if fresh else by_part((state_dim, inner)),
-            ANY if fresh else by_part((8, conv_dim)),
+            ANY if fresh else lead_block,
             whole(dsmall.shape),
             whole(dgain.shape),
             ANY,
@@ -862,17 +934,17 @@
             by_block((piece, wide)),
             whole((8, conv_dim)),
             by_part((state_dim, inner)),
-            by_part((8, conv_dim)),
+            lead_block,
         ],
         out_shape=[
             jax.ShapeDtypeStruct((part * size * piece, wide), bf16),
             jax.ShapeDtypeStruct((8, conv_dim), f32),
             jax.ShapeDtypeStruct((part * state_dim, inner), f32),
-            jax.ShapeDtypeStruct((part * 8, conv_dim), f32),
+            jax.ShapeDtypeStruct((part * chunks, 8, lanes), f32),
         ],
         scratch_shapes=[
             pltpu.VMEM((state_dim, inner), f32),
-            pltpu.VMEM((piece + 8, conv_dim), f32),
+            pltpu.VMEM((chunks, ext_rows, lanes), f32),
             pltpu.VMEM((piece, inner), f32),
             pltpu.VMEM((piece, inner), bf16),
             pltpu.VMEM((piece, inner), bf16),
@@ -887,7 +959,7 @@
     )(*saved, small, head, skip, summing, state, lead, dsmall, dgain, dproj)
 
 
-def input_grad(dims, core, tokens, dgate, dproj, small, wg, wa, wb):
+def input_grad(dims, core, tokens, dgate, dproj, small, dsmall, wg, wa, wb):
     part, size, piece, width, inner, heads, taps = dims
     rows = part * size * piece
     blocks = wa[0].shape[0]
@@ -902,6 +974,7 @@
             by_block((piece, inner), size),
             by_block((piece, dproj.shape[1]), size),
             whole(small.shape),
+            whole(dsmall.shape),
             ANY,
             ANY,
             ANY,
@@ -909,11 +982,11 @@
             ANY,
             ANY,
         ],
-        out_specs=[by_block((piece, width), size), whole((8, width))]
+        out_specs=[by_block((piece, width), size), whole(dsmall.shape)]
         + [whole(array.shape) for array in handed],
         out_shape=[
             jax.ShapeDtypeStruct((rows, width), bf16),
-            jax.ShapeDtypeStruct((8, width), f32),
+            jax.ShapeDtypeStruct(dsmall.shape, f32),
         ]
         + handed,
         scratch_shapes=[
@@ -924,10 +997,10 @@
         + weight_scratch(wg, wa, wb),
         compiler_params=params(),
         cost_estimate=cost(1, 1, 0),
-    )(core, tokens, dgate, dproj, small, *wg, *wa, *wb)
-
-
-def adam(rates, sums, norm_sums, gate_grads, front_grads, states, heads, taps):
+    )(core, tokens, dgate, dproj, small, dsmall, *wg, *wa, *wb)
+
+
+def adam(rates, sums, gate_grads, front_grads, states, heads, taps):
     outs = []
     at_refs = []
     for which, (master, first, second) in enumerate(states):
@@ -941,12 +1014,12 @@
         partial(
             adam_kernel, heads=heads, taps=taps, at_refs=at_refs, arrivals=len(gate_grads)
         ),
-        in_specs=[SMEM] + [vmem] * (2 + 2 * len(gate_grads) + len(flat)),
+        in_specs=[SMEM] + [vmem] * (3 * len(gate_grads) + len(flat)),
         out_specs=[vmem] * len(outs),
         out_shape=outs,
         compiler_params=pltpu.CompilerParams(vmem_limit_bytes=vmem_bytes),
         cost_estimate=cost(1, 1, 0),
-    )(rates, sums, norm_sums, *gate_grads, *front_grads, *flat)
+    )(rates, *sums, *gate_grads, *front_grads, *flat)
 
 
 def bit_count(extent):
@@ -983,11 +1056,9 @@
 
 def gather_seq(shard):
     block = shard
-    kept = []
     for done, bit in enumerate(reversed(range(bit_count(lax.axis_size("seq"))))):
         block = gather_bit(block, "seq", bit, done)
-        kept.append(block)
-    return block.reshape((-1,) + shard.shape), kept[0]
+    return block.reshape((-1,) + shard.shape)
 
 
 def dp_orders():
@@ -1008,9 +1079,19 @@
 
 def core_sums(send, keep):
     extent = lax.axis_size("seq")
-    total = keep + swap(send, "dp", 0).astype(f32)
     bits = bit_count(lax.axis_size("dp")) - 1
-    return total.reshape((2,) * bits + (extent, -1, send.shape[2]))
+    shape = (2,) * bits + (extent, -1, send.shape[2])
+    other = swap(send, "dp", 0)
+    return keep.reshape(shape), other.reshape(shape)
+
+
+def core_and_next(keep, other, order):
+    bit = order[-2]
+    at = sum(1 for b in order[:-2] if b > bit)
+    mine = (lax.axis_index("dp") >> bit) & 1
+    sent = pick(keep, 1 - mine, at) + pick(other, 1 - mine, at).astype(f32)
+    arrived = swap(sent.astype(bf16), "dp", bit)
+    return pick(keep, mine, at) + pick(other, mine, at).astype(f32), arrived
 
 
 def scatter_dp_bit(block, order, step):
@@ -1029,8 +1110,10 @@
     return arrivals
 
 
-def sum_over(block, axis):
-    for bit in range(bit_count(lax.axis_size(axis))):
+def sum_over(block, axis, *others):
+    for bit in reversed(range(bit_count(lax.axis_size(axis)))):
+        if bit == 0 and others:
+            block = after(block, *others)
         block = block + swap(block, axis, bit)
     return block
 
@@ -1109,7 +1192,8 @@
     me = lax.axis_index("dp") * seq_extent + lax.axis_index("seq")
     step_float = step_count[0].astype(f32)
     scales = 1.0 / (1.0 - hyper[1:3] ** step_float)
-    rates = jnp.concatenate([hyper, scales, jnp.stack([me.astype(f32), jnp.zeros((), f32)])])
+    place = lax.axis_index("seq")
+    rates = jnp.concatenate([hyper, scales, jnp.stack([me.astype(f32), place.astype(f32)])])
     core = (lax.axis_index("dp") & 1).astype(jnp.int32)[None]
     owners = lax.axis_size("dp") * seq_extent
     size = math.gcd(seq_extent, seq_count)
@@ -1126,38 +1210,58 @@
     wide_a = min(1024, inner)
     dims = (part, size, piece, width, inner, heads, taps)
 
-    small = jnp.zeros((8, conv_dim), bf16)
-    for at, row, count in (
-        (0, conv_params, conv_own),
-        (tap_rows, norm_gain[None, :], own_rows),
-        (tap_rows + 1, gate_gain[None, :], gate_own),
-    ):
-        small = lax.dynamic_update_slice(small, row.astype(bf16), (at, me * count))
     head = padded(head_params, 8, lanes)
     skip = jnp.repeat(head_params[2], inner // heads)[None, :]
     summing = summing_matrix(inner, heads)
 
     in_low = padded(in_weight.astype(bf16), own_rows, inner + conv_dim + lanes)
     out_low_own = out_weight.astype(bf16).reshape(2, own_rows, width)
+    own_small = jnp.concatenate(
+        [
+            padded(conv_params.astype(bf16), tap_rows, lanes),
+            padded(norm_gain.astype(bf16)[None, :], 1, lanes),
+            padded(gate_gain.astype(bf16)[None, :], 1, lanes),
+        ]
+    )
     shard = jnp.concatenate([in_low, out_low_own[0], out_low_own[1]], axis=1)
-    gathered, half_gathered = gather_seq(shard)
-    small = sum_over(after(small, half_gathered), "seq")
+    half = width // 2
+    both = jnp.concatenate([layer_in, out_grad[:, :, :half]], axis=2)
+    if own_rows >= tap_rows + 2:
+        shard = jnp.concatenate([shard, padded(own_small, own_rows, lanes)], axis=1)
+        gathered = gather_seq(shard)
+        seq_small = gathered[:, : tap_rows + 2, -lanes:]
+    else:
+        gathered = gather_seq(shard)
+        seq_small = gather_seq(padded(own_small, 8, lanes))[:, : tap_rows + 2]
+    tokens = to_sequences(after(both, shard), part, size)
+    small = jnp.zeros((8, conv_dim), bf16)
+    group = lax.axis_index("dp")
+    for at, rows, count in (
+        (0, tap_rows, conv_own),
+        (tap_rows, 1, own_rows),
+        (tap_rows + 1, 1, gate_own),
+    ):
+        piece_rows = jnp.concatenate(
+            [seq_small[z, at : at + rows, :count] for z in range(seq_extent)], axis=1
+        )
+        small = lax.dynamic_update_slice(small, piece_rows, (at, group * seq_extent * count))
     front_end = inner + conv_dim + lanes
     wg = gathered[:, :, :inner]
     wa = gathered[:, :, inner : inner + wide_a]
     wb = gathered[:, :, inner + wide_a : front_end]
     wo = jnp.stack(
-        [gathered[:, :, front_end : front_end + width], gathered[:, :, front_end + width :]],
+        [
+            gathered[:, :, front_end : front_end + width],
+            gathered[:, :, front_end + width : front_end + 2 * width],
+        ],
         axis=1,
     ).reshape(-1, 2 * own_rows, width)
-    tokens = to_sequences(after(layer_in, head, skip, shard, rates), part, size)
     order_a, order_b = dp_orders()
     last = len(order_a) - 1
     for step in range(last):
         wa = gather_dp_bit(wa, order_a, step)
         wb = gather_dp_bit(wb, order_b, step)
-    small = sum_over(small, "dp").astype(f32)
-    wg, wo = after((wg, wo), wa, wb, small)
+    wg, wo = after((wg, wo), wa, wb)
 
     def core_halves(block):
         block = block.reshape(owners // 2 // seq_extent, -1, block.shape[-1])
@@ -1165,24 +1269,25 @@
 
     wb = core_halves(wb)
     wa = core_halves(wa)
+    small = sum_over(small, "dp", tokens, wa, wb, head, skip).astype(f32)
     for step in range(last - 1):
         wg = gather_dp_bit(wg, order_a, step)
         wo = gather_dp_bit(wo, order_b, step)
-    wg, wo, tokens = lax.optimization_barrier((wg, wo, after(tokens, wa, wb)))
-    cots = to_sequences(after(out_grad, tokens), part, size)
+    cots_b = to_sequences(after(out_grad, tokens)[:, :, half:], part, size)
 
     edge = core
     if groups > 1:
-        edge = tokens.reshape(part, size * piece, width)[:, size * piece - 8 :, :]
+        edge = tokens.reshape(part, size * piece, -1)[:, size * piece - 8 :, :width]
         edge = shifted_by(edge, "seq", size).reshape(part * 8, width)
 
-    def forward(start):
-        return mixer_forward(
-            dims, core, tokens, wa, wb, small, head, skip, groups > 1, edge, start
-        )
-
+    def forward(start, kept, blocks):
+        weights = (wa, wb, small, head, skip)
+        grouped = groups > 1
+        return mixer_forward(dims, core, tokens, *weights, edge, start, grouped, kept, blocks)
+
+    start = core
     if groups > 1:
-        first_out = forward(jnp.zeros((part * state_dim, inner), f32))
+        first_out = forward(jnp.zeros((part * state_dim, inner), f32), None, (0, size))
         cum_last = first_out[3].reshape(part, size, piece, lanes)[:, :, piece - 1, :heads]
         decay = jnp.exp2(jnp.sum(cum_last, axis=1))
         decay = jnp.repeat(decay, inner // heads, axis=1)[:, None, :]
@@ -1196,46 +1301,52 @@
             return carried.reshape(part * state_dim, inner)
 
         start = relay(first_out[6], size)
-    else:
-        start = core
-    normed, ext, dtr, cum, y, sin, _ = forward(start)
-
+    normed, ext, dtr, cum, y, sin, _, _ = forward(start, None, (0, size))
     wg = core_halves(gather_dp_bit(wg, order_a, last - 1, normed))
     wo = core_halves(gather_dp_bit(wo, order_b, last - 1, normed))
     layer_rows, dy, dgate, dgain, *handed = gate_step(
-        dims, core, normed, tokens, cots, y, wg, wo, small
+        dims, core, normed, tokens, cots_b, y, wg, wo, small
     )
     layer_out = to_pieces(layer_rows, part, size, piece)
+    consts = (small, head, skip, summing, dgain)
+    saved = (ext, dtr, cum, y, sin, dy)
+
+    def backward(carry, block, fresh=False):
+        return list(mixer_backward(dims, saved, consts, carry, (block, 1), fresh))
+
+    def fresh_carry():
+        if groups == 1:
+            return (core, head, core, core)
+        lead = jnp.zeros((part * (conv_dim // lanes), 8, lanes), f32)
+        first_out = (core, head, jnp.zeros((part * state_dim, inner), f32), lead)
+        for block in reversed(range(size)):
+            first_out = backward(first_out, block)
+        return (core, head, relay(first_out[2], -size), lead)
+
     g_out = core_sums(*handed[:2])
     g_gate = core_sums(*handed[2:])
-    dy = after(dy, g_out, g_gate)
-    cut = size // 2
-    saved = (ext, dtr, cum, y, sin, dy)
-    consts = (small, head, skip, summing, dgain)
-
-    def backward(state, lead):
-        carry = (core, head, state, lead)
-        return list(
-            mixer_backward(dims, saved, consts, carry, (cut, size - cut), groups == 1)
-        )
-
-    if groups > 1:
-        zeros = (jnp.zeros((part * state_dim, inner), f32), jnp.zeros((part * 8, conv_dim), f32))
-        first_out = backward(*zeros)
-        first_out = mixer_backward(dims, saved, consts, first_out, (0, cut), False)
-        backward_out = backward(relay(first_out[2], -size), zeros[1])
-    else:
-        backward_out = backward(core, core)
-    for step in range(1, last):
-        g_out = scatter_dp_bit(g_out, order_a, step)
-        g_gate = scatter_dp_bit(g_gate, order_b, step)
-    backward_out[2], g_out, g_gate = lax.optimization_barrier((backward_out[2], g_out, g_gate))
-    dproj, dsmall, _, lead = mixer_backward(dims, saved, consts, backward_out, (0, cut), False)
-    g_out = scatter_dp_bit(g_out, order_a, last)
-    g_gate = scatter_dp_bit(g_gate, order_b, last)
+    carry = backward(fresh_carry(), size - 1, groups == 1)
+    for block in reversed(range(size - 1)):
+        carry[2], g_out, g_gate = lax.optimization_barrier((carry[2], g_out, g_gate))
+        step = size - 2 - block
+        if step == 0:
+            g_out = core_and_next(*g_out, order_a)
+            g_gate = core_and_next(*g_gate, order_b)
+        elif step == 1:
+            g_out = g_out[0] + g_out[1].astype(f32)
+            g_gate = g_gate[0] + g_gate[1].astype(f32)
+            for bit_step in range(2, last + 1):
+                g_out = scatter_dp_bit(g_out, order_a, bit_step)
+                g_gate = scatter_dp_bit(g_gate, order_b, bit_step)
+        elif step == 2:
+            g_rest = scatter_seq(
+                jnp.concatenate([g_gate, g_out[:, :own_rows], g_out[:, own_rows:]], axis=2)
+            )
+        carry = backward(carry, block)
+    dproj, dsmall, _, lead = carry
     if groups > 1:
         lead = shifted_by(lead.astype(bf16), "seq", -size).astype(f32)
-        lead = lead.reshape(part, 8, conv_dim)
+        lead = lead.reshape(part, -1, 8, lanes).transpose(0, 2, 1, 3).reshape(part, 8, conv_dim)
         fixes = []
         for row in range(taps - 1):
             terms = [small[tap] * lead[:, row - tap] for tap in range(row + 1)]
@@ -1245,23 +1356,24 @@
         ends = dproj[:, size * piece - (taps - 1) :].astype(f32) + fix
         dproj = dproj.at[:, size * piece - (taps - 1) :].set(ends.astype(bf16))
         dproj = dproj.reshape(-1, conv_dim + lanes)
-    g_rest = scatter_seq(
-        jnp.concatenate([g_gate, g_out[:, :own_rows], g_out[:, own_rows:]], axis=2)
-    )
-    sums = sum_over(dsmall, "seq")
-    tokens = after(tokens, layer_out, g_gate, g_out)
-    dx, d_gain, *handed = input_grad(dims, core, tokens, dgate, dproj, small, wg, wa, wb)
-    handed, dx, sums = after((handed, dx, sums), g_rest)
+    tokens, g_rest = lax.optimization_barrier((after(tokens, layer_out, dproj), g_rest))
+    dx, dsmall, *handed = input_grad(dims, core, tokens, dgate, dproj, small, dsmall, wg, wa, wb)
     g_a = core_sums(*handed[:2])
     g_b = core_sums(*handed[2:])
-    sums, d_gain = after((sums, d_gain), g_a, g_b)
-    for step in range(1, last + 1):
+    g_a = core_and_next(*g_a, order_a)
+    g_b = core_and_next(*g_b, order_b)
+    g_a = g_a[0] + g_a[1].astype(f32)
+    g_b = g_b[0] + g_b[1].astype(f32)
+    for step in range(2, last + 1):
         g_a = scatter_dp_bit(g_a, order_a, step)
         g_b = scatter_dp_bit(g_b, order_b, step)
     g_front = scatter_seq(jnp.concatenate([g_a, g_b], axis=2))
     in_grad = out_grad.astype(f32) + to_pieces(dx, part, size, piece).astype(f32)
-    sums = sum_over(sums, "dp")
-    norm_sums = sum_over(sum_over(d_gain, "dp"), "seq")
+    dsmall = sum_over(dsmall, "dp")
+    sums = [dsmall]
+    for distance in range(1, seq_extent):
+        route = [(i, (i + distance) % seq_extent) for i in range(seq_extent)]
+        sums.append(lax.ppermute(dsmall, "seq", route))
 
     states = (
         (norm_gain[None, :], norm_first[None, :], norm_second[None, :]),
@@ -1271,7 +1383,7 @@
         (out_weight, out_first, out_second),
         (head_params, head_first, head_second),
     )
-    new = adam(rates, sums, norm_sums, g_rest, g_front, states, heads, taps)
+    new = adam(rates, sums, g_rest, g_front, states, heads, taps)
     new = [array[0] if array.shape[0] == 1 else array for array in new]
     return (layer_out, in_grad, *new)
 

time: 348 us -> 313 us (0.90)
  Pallas kernels: 148 us -> 121 us
  waiting for transfers between devices: 79.2 us -> 66.6 us
  other arithmetic: 26.1 us -> 34.1 us
  starting transfers between devices: 75.5 us -> 68.7 us
    ppermute x41 -> x32, waiting for transfers between devices: 73.9 us -> 50.4 us  [swap(): return lax.ppermute(block, axis, [(i, i ^ 1 << bit) for i in devices])]
    ppermute x41 -> x32, starting transfers between devices: 50.7 us -> 31.8 us  [swap(): return lax.ppermute(block, axis, [(i, i ^ 1 << bit) for i in devices])]
    pallas_call x1, Pallas kernels: 38.3 us -> 25.8 us  [gate_step(): pl.pallas_call(partial(gate_kernel, gain_row=taps + 2), grid=(part, size)...]
    ppermute x0 -> x3, waiting for transfers between devices: none -> 9.35 us  [local(): sums.append(lax.ppermute(dsmall, 'seq', route))]
    pallas_call x2 -> x4, Pallas kernels: 57.7 us -> 49.7 us  [mixer_backward(): pl.pallas_call(partial(mixer_backward_kernel, heads=heads, inner=inner, t...]
    pallas_call x1, Pallas kernels: 30.4 us -> 24.5 us  [mixer_forward(): pl.pallas_call(partial(mixer_forward_kernel, heads=heads, inner=inner, ta...]
    ppermute x0 -> x3, starting transfers between devices: none -> 5.87 us  [local(): sums.append(lax.ppermute(dsmall, 'seq', route))]
    convert_element_type x4 -> x6, other arithmetic: 2.64 us -> 7.7 us  [the longest x4 6.38 us: core_and_next(): arrived = swap(sent.astype(bf16), 'dp', bit)]
  transfers between devices with their start and end apart: 51 -> 45, of which waited for: 27 -> 19; matrix products, arithmetic and copies ran while one was open for 8% -> 10% of each run, Pallas kernels for 32% -> 25%
where the time goes in v2:
time: 313 us; the launch traced here: 309 us
  Pallas kernels  121 us (39%)
  starting transfers between devices  68.7 us (22%)
  waiting for transfers between devices  66.6 us (21%)
  other arithmetic  34.1 us (11%)
  local copies, waits for them, and re-layouts  15.3 us (5%)
    ppermute x32, waiting for transfers between devices, swap(): return lax.ppermute(block, axis, [(i, i ^ 1 << bit) for i in devices])  50.4 us
    pallas_call x4, Pallas kernels, mixer_backward(): pl.pallas_call(partial(mixer_backward_kernel, heads=heads, inner=inner, t...  49.7 us
    ppermute x32, starting transfers between devices, swap(): return lax.ppermute(block, axis, [(i, i ^ 1 << bit) for i in devices])  31.8 us
    pallas_call x1, Pallas kernels, gate_step(): pl.pallas_call(partial(gate_kernel, gain_row=taps + 2), grid=(part, size)...  25.8 us
    pallas_call x1, Pallas kernels, mixer_forward(): pl.pallas_call(partial(mixer_forward_kernel, heads=heads, inner=inner, ta...  24.5 us
    pallas_call x1, Pallas kernels, input_grad(): pl.pallas_call(partial(input_grad_kernel, gain_row=taps + 1), grid=(part,...  17.6 us
    ppermute x6, starting transfers between devices, scatter_seq(): arrivals.append(lax.ppermute(sent, 'seq', route))  11.9 us
    another operation x20, other arithmetic, gather_bit(): return jnp.stack([low, high], axis=at)  10.6 us
  transfers between devices with their start and end apart: 45, of which 19 were waited for; matrix products, arithmetic and copies ran while one was open for 10% of the time, Pallas kernels for 25%

profile of v2, /device:TPU:0, one launch (start us, length us, event | category | flops | bytes accessed | tf_op | source)
XLA Modules:
  0.0 308.6 jit_solution(4359720823810084568)
XLA Ops:
  4.6 4.1 %collective-permute-start = (bf16[24,5120]{1,0:T(8,128)(2,1)S(1)}, bf16[24,5120]{1,0:T(8,128)(2,1)S(1)}, u32[]{:S(2)}, u32[]{:S(2)}) collective-permute-start(bf16[24,5120]{1,0:T(8,128)(2,1)S(1)} %fusion.11), channel_id=1, source_target_pairs={{0,2},{1,3},{2,0},{3,1},{4,6},{5,7},{6,4},{7,5},{8,10},{9,11},{10,... | collective-permute-start | bytes 737288 | tf_op jit(solution)/shard_map/ppermute | solution.py:1034
  8.7 11.2 %collective-permute-done = bf16[24,5120]{1,0:T(8,128)(2,1)S(1)} collective-permute-done((bf16[24,5120]{1,0:T(8,128)(2,1)S(1)}, bf16[24,5120]{1,0:T(8,128)(2,1)S(1)}, u32[]{:S(2)}, u32[]{:S(2)}) %collective-permute-start) | collective-permute-done | bytes 245792 | tf_op jit(solution)/shard_map/ppermute | solution.py:1034
  23.5 4.8 %all-to-all-start = ((bf16[4,256,1152]{2,1,0:T(8,128)(2,1)}), bf16[4,256,1152]{2,1,0:T(8,128)(2,1)S(1)}, u32[]{:S(2)}, u32[]{:S(2)}) async-start(bf16[4,256,1152]{2,1,0:T(8,128)(2,1)} %pad_maximum_fusion), calls=%async_computation | async-start | bytes 4718592 | tf_op jit(solution)/shard_map/all_to_all | solution.py:1130
  28.3 7.0 %collective-permute-done.1 = bf16[2,24,5120]{2,1,0:T(8,128)(2,1)S(1)} collective-permute-done((bf16[2,24,5120]{2,1,0:T(8,128)(2,1)}, bf16[2,24,5120]{2,1,0:T(8,128)(2,1)S(1)}, u32[]{:S(2)}, u32[]{:S(2)}) %collective-permute-start.1) | collective-permute-done | bytes 491552 | tf_op jit(solution)/shard_map/ppermute | solution.py:1034
  38.9 2.3 collective-permute-done.5
  46.6 2.5 collective-permute-done.6
  50.1 4.9 %collective-permute-done.3 = bf16[2,4,24,1024]{3,2,1,0:T(8,128)(2,1)S(1)} collective-permute-done((bf16[2,4,24,1024]{3,2,1,0:T(8,128)(2,1)S(1)}, bf16[2,4,24,1024]{3,2,1,0:T(8,128)(2,1)S(1)}, u32[]{:S(2)}, u32[]{:S(2)}) %collective-permute-start.3) | collective-permute-done | bytes 393248 | tf_op jit(solution)/shard_map/ppermute | solution.py:1034
  60.9 2.5 collective-permute-start.9
  71.3 5.7 %collective-permute-done.11 = bf16[4,24,1536]{2,1,0:T(8,128)(2,1)S(1)} collective-permute-done((bf16[4,24,1536]{2,1,0:T(8,128)(2,1)S(1)}, bf16[4,24,1536]{2,1,0:T(8,128)(2,1)S(1)}, u32[]{:S(2)}, u32[]{:S(2)}) %collective-permute-start.11) | collective-permute-done | bytes 294944 | tf_op jit(solution)/shard_map/ppermute | solution.py:1034
  78.6 3.8 %all-to-all-done = bf16[4,256,1152]{2,1,0:T(8,128)(2,1)S(1)} async-done(((bf16[4,256,1152]{2,1,0:T(8,128)(2,1)}), bf16[4,256,1152]{2,1,0:T(8,128)(2,1)S(1)}, u32[]{:S(2)}, u32[]{:S(2)}) %all-to-all-start) | async-done | bytes 2359328 | tf_op jit(solution)/shard_map/all_to_all | solution.py:1130
  85.9 2.1 slice.108
  88.0 4.4 %all-to-all-start.1 = ((bf16[4,256,384]{2,1,0:T(8,128)(2,1)}), bf16[4,256,384]{2,1,0:T(8,128)(2,1)}, u32[]{:S(2)}, u32[]{:S(2)}) async-start(bf16[4,256,384]{2,1,0:T(8,128)(2,1)} %slice.108), calls=%async_computation.1 | async-start | bytes 1572864 | tf_op jit(solution)/shard_map/all_to_all | solution.py:1130
  93.0 24.5 %shard_map.390 = (bf16[1024,768]{1,0:T(8,128)(2,1)}, f32[56,264,128]{2,1,0:T(8,128)}, f32[1024,128]{1,0:T(8,128)}, f32[1024,128]{1,0:T(8,128)}, f32[1024,1536]{1...) custom-call(s32[1]{0:T(128)} %bitcast.core_ref.edge_ref.start_ref.before_ref.next_ref._, ...), custom_call_target="tpu_custom_call" | custom-call | flops 1 | bytes 1 | tf_op jit(solution)/shard_map/pallas_call | solution.py:787
  124.9 25.8 %shard_map.391 = (bf16[1024,768]{1,0:T(8,128)(2,1)}, bf16[1024,1536]{1,0:T(8,128)(2,1)}, bf16[1024,1536]{1,0:T(8,128)(2,1)}, f32[8,1536]{1,0:T(8,128)}, bf16[4,1...) custom-call(s32[1]{0:T(128)} %bitcast.core_ref.edge_ref.start_ref.before_r, ...), custom_call_target="tpu_custom_call" | custom-call | flops 1 | bytes 1 | tf_op jit(solution)/shard_map/pallas_call | solution.py:852
  151.3 12.1 %shard_map.392 = (bf16[1024,1920]{1,0:T(8,128)(2,1)}, f32[8,1792]{1,0:T(8,128)}, f32[128,1536]{1,0:T(8,128)}, f32[14,8,128]{2,1,0:T(8,128)}) custom-call(f32[56,264,128]{2,1,0:T(8,128)} %get-tuple-element.112.ext_ref, f32[1024,128]{1,0:T(8,128)} %get-tuple-element.113.dtr_ref, f32[1024,128]{1,0:T(8,128)} %get-tuple-element.114.cum_ref, ...), custom_call_target="tpu_custom_call" | custom-call | flops 1 | bytes 1 | tf_op jit(solution)/shard_map/pallas_call | solution.py:911
  164.4 2.6 fusion.4
  170.5 5.2 %all-to-all-start.2 = ((bf16[4,256,768]{2,1,0:T(8,128)(2,1)}), bf16[4,256,768]{2,1,0:T(8,128)(2,1)S(1)}, u32[]{:S(2)}, u32[]{:S(2)}) async-start(bf16[4,256,768]{2,1,0:T(8,128)(2,1)} %bitcast.197), calls=%async_computation.2 | async-start | bytes 3145728 | tf_op jit(solution)/shard_map/all_to_all | solution.py:1146
  175.8 12.5 %shard_map.393 = (bf16[1024,1920]{1,0:T(8,128)(2,1)}, f32[8,1792]{1,0:T(8,128)}, f32[128,1536]{1,0:T(8,128)}, f32[14,8,128]{2,1,0:T(8,128)}) custom-call(f32[56,264,128]{2,1,0:T(8,128)} %get-tuple-element.112.ext_ref, f32[1024,128]{1,0:T(8,128)} %get-tuple-element.113.dtr_ref, ...), custom_call_target="tpu_custom_call", output_to_operand_aliasing={{0}: (14, {})} | custom-call | flops 1 | bytes 1 | tf_op jit(solution)/shard_map/pallas_call | solution.py:911
  193.6 12.7 %shard_map.394 = (bf16[1024,1920]{1,0:T(8,128)(2,1)}, f32[8,1792]{1,0:T(8,128)}, f32[128,1536]{1,0:T(8,128)}, f32[14,8,128]{2,1,0:T(8,128)}) custom-call(f32[56,264,128]{2,1,0:T(8,128)} %get-tuple-element.112.ext_ref, f32[1024,128]{1,0:T(8,128)} %get-tuple-element.113.dtr_ref, ...), custom_call_target="tpu_custom_call", output_to_operand_aliasing={{0}: (14, {})} | custom-call | flops 1 | bytes 1 | tf_op jit(solution)/shard_map/pallas_call | solution.py:911
  210.0 2.4 collective-permute-start.24
  214.6 12.4 %shard_map.395 = (bf16[1024,1920]{1,0:T(8,128)(2,1)}, f32[8,1792]{1,0:T(8,128)}, f32[128,1536]{1,0:T(8,128)}, f32[14,8,128]{2,1,0:T(8,128)}) custom-call(f32[56,264,128]{2,1,0:T(8,128)} %get-tuple-element.112.ext_ref, f32[1024,128]{1,0:T(8,128)} %get-tuple-element.113.dtr_ref, ...), custom_call_target="tpu_custom_call", output_to_operand_aliasing={{0}: (14, {})} | custom-call | flops 1 | bytes 1 | tf_op jit(solution)/shard_map/pallas_call | solution.py:911
  227.1 17.6 %shard_map.396 = (bf16[1024,768]{1,0:T(8,128)(2,1)}, f32[8,1792]{1,0:T(8,128)}, bf16[4,96,1024]{2,1,0:T(8,128)(2,1)}, f32[4,96,1024]{2,1,0:T(8,128)}, bf16[4,96,...) custom-call(s32[1]{0:T(128)} %bitcast.core_ref.edge_ref.start_ref.before_ref.next_ref._, bf16[1024,1152]{1,0:T(8,128)(2,1)} %bitcast.177, ...), custom_call_target="tpu_custom_call" | custom-call | flops 1 | bytes 1 | tf_op jit(solution)/shard_map/pallas_call | solution.py:968
  245.3 4.8 %all-to-all-start.3 = ((bf16[4,256,768]{2,1,0:T(8,128)(2,1)}), bf16[4,256,768]{2,1,0:T(8,128)(2,1)}, u32[]{:S(2)}, u32[]{:S(2)}) async-start(bf16[4,256,768]{2,1,0:T(8,128)(2,1)} %bitcast.198), calls=%async_computation.3 | async-start | bytes 3145728 | tf_op jit(solution)/shard_map/all_to_all | solution.py:1146
  264.2 2.4 collective-permute-start.30
  270.5 2.1 collective-permute-done.33
  275.9 4.0 %collective-permute-done.34 = bf16[4,24,1024]{2,1,0:T(8,128)(2,1)S(1)} collective-permute-done((bf16[4,24,1024]{2,1,0:T(8,128)(2,1)S(1)}, bf16[4,24,1024]{2,1,0:T(8,128)(2,1)S(1)}, u32[]{:S(2)}, u32[]{:S(2)}) %collective-permute-start.34) | collective-permute-done | bytes 196640 | tf_op jit(solution)/shard_map/ppermute | solution.py:1034
  280.1 2.1 collective-permute-start.38
  282.2 2.3 collective-permute-start.39
  286.7 9.3 %collective-permute-done.30.refs_2_ = f32[8,1792]{1,0:T(8,128)S(1)} collective-permute-done((f32[8,1792]{1,0:T(8,128)S(1)}, f32[8,1792]{1,0:T(8,128)S(1)}, u32[]{:S(2)}, u32[]{:S(2)}) %collective-permute-start.30) | collective-permute-done | bytes 57376 | tf_op jit(solution)/shard_map/ppermute | solution.py:1376
  296.1 3.1 %collective-permute-done.39.refs_10_ = bf16[24,1920]{1,0:T(8,128)(2,1)S(1)} collective-permute-done((bf16[24,1920]{1,0:T(8,128)(2,1)S(1)}, bf16[24,1920]{1,0:T(8,128)(2,1)S(1)}, u32[]{:S(2)}, u32[]{:S(2)}) %collective-permute-start.39) | collective-permute-done | bytes 92192 | tf_op jit(solution)/shard_map/ppermute | solution.py:1109
  299.9 3.7 %shard_map.397 = (f32[1,24]{1,0:T(1,128)}, f32[1,24]{1,0:T(1,128)}, f32[1,24]{1,0:T(1,128)}, f32[24,3352]{1,0:T(8,128)}, f32[24,3352]{1,0:T(8,128)}, /*index=5*/...) custom-call(f32[8]{0:T(128)} %pad_maximum_fusion.16.rates_ref, ...), custom_call_target="tpu_custom_call" | custom-call | flops 1 | bytes 1 | tf_op jit(solution)/shard_map/pallas_call | solution.py:1013
  303.7 3.4 %convert_add_fusion = f32[4,256,768]{2,1,0:T(8,128)} fusion(bf16[4,256,768]{2,1,0:T(8,128)(2,1)} %all-to-all-done.3, bf16[4,256,768]{2,1,0:T(8,128)(2,1)S(1)} %copy-done.3), kind=kLoop, calls=%fused_computation | loop fusion | flops 2359296 | bytes 6291456 | tf_op jit(solution)/shard_map/add | solution.py:1371
  (229 shorter events, 85.7 us)
Async XLA Ops:
  4.6 15.3 %collective-permute-start = (bf16[24,5120]{1,0:T(8,128)(2,1)S(1)}, bf16[24,5120]{1,0:T(8,128)(2,1)S(1)}, u32[]{:S(2)}, u32[]{:S(2)}) collective-permute-start(bf16[24,5120]{1,0:T(8,128)(2,1)S(1)} %fusion.11), channel_id=1, source_target_pairs={{0,2},{1,3},{2,0},{3,1},{4,6},{5,7},{6,4},{7,5},{8,10},{9,11},{10,... | collective-permute-start | bytes 737288 | tf_op jit(solution)/shard_map/ppermute | solution.py:1034
  20.9 14.4 %collective-permute-start.1 = (bf16[2,24,5120]{2,1,0:T(8,128)(2,1)}, bf16[2,24,5120]{2,1,0:T(8,128)(2,1)S(1)}, u32[]{:S(2)}, u32[]{:S(2)}) collective-permute-start(bf16[2,24,5120]{2,1,0:T(8,128)(2,1)} %pad_maximum_fusion.9), channel_id=1, source_target_pairs={{0,1},{1,0},{2,3},{3,2},{4,5},{5,4},{6,7},{7,6},{8,9},{9,8},{10,11... | collective-permute-start | bytes 1474568 | tf_op jit(solution)/shard_map/ppermute | solution.py:1034
  23.5 58.8 %all-to-all-start = ((bf16[4,256,1152]{2,1,0:T(8,128)(2,1)}), bf16[4,256,1152]{2,1,0:T(8,128)(2,1)S(1)}, u32[]{:S(2)}, u32[]{:S(2)}) async-start(bf16[4,256,1152]{2,1,0:T(8,128)(2,1)} %pad_maximum_fusion), calls=%async_computation | async-start | bytes 4718592 | tf_op jit(solution)/shard_map/all_to_all | solution.py:1130
  45.1 10.0 %collective-permute-start.3 = (bf16[2,4,24,1024]{3,2,1,0:T(8,128)(2,1)S(1)}, bf16[2,4,24,1024]{3,2,1,0:T(8,128)(2,1)S(1)}, u32[]{:S(2)}, u32[]{:S(2)}) collective-permute-start(bf16[2,4,24,1024]{3,2,1,0:T(8,128)(2,1)S(1)} %pad_maximum_fusion.10), channel_id=1, source_target_pairs={{0,8},{4,12},{8,0},{12,4},{16,24},{20,28},{24,16},{28,20},{1,9},{5... | collective-permute-start | bytes 1179656 | tf_op jit(solution)/shard_map/ppermute | solution.py:1034
  56.1 12.9 %collective-permute-start.14 = (bf16[4,48,768]{2,1,0:T(8,128)(2,1)}, bf16[4,48,768]{2,1,0:T(8,128)(2,1)}, u32[]{:S(2)}, u32[]{:S(2)}) collective-permute-start(bf16[4,48,768]{2,1,0:T(8,128)(2,1)} %bitcast.35), channel_id=1, source_target_pairs={{0,8},{4,12},{8,0},{12,4},{16,24},{20,28},{24,16},{28,20},{1,9},{5... | collective-permute-start | bytes 884744 | tf_op jit(solution)/shard_map/ppermute | solution.py:1034
  65.3 12.5 %collective-permute-start.7 = (bf16[4,96,896]{2,1,0:T(8,128)(2,1)}, bf16[4,96,896]{2,1,0:T(8,128)(2,1)S(1)}, u32[]{:S(2)}, u32[]{:S(2)}) collective-permute-start(bf16[4,96,896]{2,1,0:T(8,128)(2,1)} %bitcast.18.wb_own), channel_id=1, source_target_pairs={{0,4},{4,0},{8,12},{12,8},{16,20},{20,16},{24,28},{28,24},{1,5},{5... | collective-permute-start | bytes 2064392 | tf_op jit(solution)/shard_map/ppermute | solution.py:1034
  66.6 12.0 %collective-permute-start.4 = (bf16[4,96,1024]{2,1,0:T(8,128)(2,1)S(1)}, bf16[4,96,1024]{2,1,0:T(8,128)(2,1)}, u32[]{:S(2)}, u32[]{:S(2)}) collective-permute-start(bf16[4,96,1024]{2,1,0:T(8,128)(2,1)S(1)} %bitcast.181), channel_id=1, source_target_pairs={{0,4},{4,0},{8,12},{12,8},{16,20},{20,16},{24,28},{28,24},{1,5},{5... | collective-permute-start | bytes 2359304 | tf_op jit(solution)/shard_map/ppermute | solution.py:1034
  71.1 46.4 %collective-permute-start.15 = (bf16[2,4,48,768]{3,2,1,0:T(8,128)(2,1)}, bf16[2,4,48,768]{3,2,1,0:T(8,128)(2,1)}, u32[]{:S(2)}, u32[]{:S(2)}) collective-permute-start(bf16[2,4,48,768]{3,2,1,0:T(8,128)(2,1)} %pad_maximum_fusion.8), channel_id=1, source_target_pairs={{0,16},{4,20},{8,24},{12,28},{16,0},{20,4},{24,8},{28,12},{1,17},{... | collective-permute-start | bytes 1769480 | tf_op jit(solution)/shard_map/ppermute | solution.py:1034
  82.4 10.0 %collective-permute-start.10 = (bf16[8,1792]{1,0:T(8,128)(2,1)S(1)}, bf16[8,1792]{1,0:T(8,128)(2,1)S(1)}, u32[]{:S(2)}, u32[]{:S(2)}) collective-permute-start(bf16[8,1792]{1,0:T(8,128)(2,1)S(1)} %add.189), channel_id=1, source_target_pairs={{0,4},{4,0},{8,12},{12,8},{16,20},{20,16},{24,28},{28,24},{1,5},{5... | collective-permute-start | bytes 86024 | tf_op jit(solution)/shard_map/ppermute | solution.py:1034
  84.4 34.6 %collective-permute-start.12 = (bf16[2,4,24,1536]{3,2,1,0:T(8,128)(2,1)}, bf16[2,4,24,1536]{3,2,1,0:T(8,128)(2,1)}, u32[]{:S(2)}, u32[]{:S(2)}) collective-permute-start(bf16[2,4,24,1536]{3,2,1,0:T(8,128)(2,1)} %pad_maximum_fusion.7), channel_id=1, source_target_pairs={{0,8},{4,12},{8,0},{12,4},{16,24},{20,28},{24,16},{28,20},{1,9},{5... | collective-permute-start | bytes 1769480 | tf_op jit(solution)/shard_map/ppermute | solution.py:1034
  88.0 33.2 %all-to-all-start.1 = ((bf16[4,256,384]{2,1,0:T(8,128)(2,1)}), bf16[4,256,384]{2,1,0:T(8,128)(2,1)}, u32[]{:S(2)}, u32[]{:S(2)}) async-start(bf16[4,256,384]{2,1,0:T(8,128)(2,1)} %slice.108), calls=%async_computation.1 | async-start | bytes 1572864 | tf_op jit(solution)/shard_map/all_to_all | solution.py:1130
  150.7 12.7 %collective-permute-start.17 = (bf16[4,192,768]{2,1,0:T(8,128)(2,1)}, bf16[4,192,768]{2,1,0:T(8,128)(2,1)S(1)}, u32[]{:S(2)}, u32[]{:S(2)}) collective-permute-start(bf16[4,192,768]{2,1,0:T(8,128)(2,1)} %get-tuple-element.120), channel_id=1, source_target_pairs={{0,4},{4,0},{8,12},{12,8},{16,20},{20,16},{24,28},{28,24},{1,5},{5... | collective-permute-start | bytes 3538952 | tf_op jit(solution)/shard_map/ppermute | solution.py:1034
  150.9 12.5 %collective-permute-start.18 = (bf16[4,96,1536]{2,1,0:T(8,128)(2,1)}, bf16[4,96,1536]{2,1,0:T(8,128)(2,1)S(1)}, u32[]{:S(2)}, u32[]{:S(2)}) collective-permute-start(bf16[4,96,1536]{2,1,0:T(8,128)(2,1)} %get-tuple-element.122), channel_id=1, source_target_pairs={{0,4},{4,0},{8,12},{12,8},{16,20},{20,16},{24,28},{28,24},{1,5},{5... | collective-permute-start | bytes 3538952 | tf_op jit(solution)/shard_map/ppermute | solution.py:1034
  167.0 21.3 %collective-permute-start.20 = (bf16[2,4,24,1536]{3,2,1,0:T(8,128)(2,1)}, bf16[2,4,24,1536]{3,2,1,0:T(8,128)(2,1)S(1)}, u32[]{:S(2)}, u32[]{:S(2)}) collective-permute-start(bf16[2,4,24,1536]{3,2,1,0:T(8,128)(2,1)} %get-tuple-element.182), channel_id=1, source_target_pairs={{0,16},{4,20},{8,24},{12,28},{16,0},{20,4},{24,8},{28,12},{1,17},{... | collective-permute-start | bytes 1769480 | tf_op jit(solution)/shard_map/ppermute | solution.py:1034
  170.0 18.3 %collective-permute-start.19 = (bf16[2,4,48,768]{3,2,1,0:T(8,128)(2,1)}, bf16[2,4,48,768]{3,2,1,0:T(8,128)(2,1)}, u32[]{:S(2)}, u32[]{:S(2)}) collective-permute-start(bf16[2,4,48,768]{3,2,1,0:T(8,128)(2,1)} %get-tuple-element.184), channel_id=1, source_target_pairs={{0,8},{4,12},{8,0},{12,4},{16,24},{20,28},{24,16},{28,20},{1,9},{5... | collective-permute-start | bytes 1769480 | tf_op jit(solution)/shard_map/ppermute | solution.py:1034
  170.5 56.5 %all-to-all-start.2 = ((bf16[4,256,768]{2,1,0:T(8,128)(2,1)}), bf16[4,256,768]{2,1,0:T(8,128)(2,1)S(1)}, u32[]{:S(2)}, u32[]{:S(2)}) async-start(bf16[4,256,768]{2,1,0:T(8,128)(2,1)} %bitcast.197), calls=%async_computation.2 | async-start | bytes 3145728 | tf_op jit(solution)/shard_map/all_to_all | solution.py:1146
  190.3 16.0 %collective-permute-start.21 = (bf16[4,48,768]{2,1,0:T(8,128)(2,1)}, bf16[4,48,768]{2,1,0:T(8,128)(2,1)}, u32[]{:S(2)}, u32[]{:S(2)}) collective-permute-start(bf16[4,48,768]{2,1,0:T(8,128)(2,1)} %fusion.9), channel_id=1, source_target_pairs={{0,16},{4,20},{8,24},{12,28},{16,0},{20,4},{24,8},{28,12},{1,17},{... | collective-permute-start | bytes 884744 | tf_op jit(solution)/shard_map/ppermute | solution.py:1034
  192.1 15.4 %collective-permute-start.22 = (bf16[4,24,1536]{2,1,0:T(8,128)(2,1)S(1)}, bf16[4,24,1536]{2,1,0:T(8,128)(2,1)S(1)}, u32[]{:S(2)}, u32[]{:S(2)}) collective-permute-start(bf16[4,24,1536]{2,1,0:T(8,128)(2,1)S(1)} %fusion.10), channel_id=1, source_target_pairs={{0,8},{4,12},{8,0},{12,4},{16,24},{20,28},{24,16},{28,20},{1,9},{5... | collective-permute-start | bytes 884744 | tf_op jit(solution)/shard_map/ppermute | solution.py:1034
  207.9 19.1 %collective-permute-start.23 = (bf16[24,3072]{1,0:T(8,128)(2,1)S(1)}, bf16[24,3072]{1,0:T(8,128)(2,1)S(1)}, u32[]{:S(2)}, u32[]{:S(2)}) collective-permute-start(bf16[24,3072]{1,0:T(8,128)(2,1)S(1)} %get-tuple-element.188), channel_id=1, source_target_pairs={{0,1},{1,2},{2,3},{3,0},{4,5},{5,6},{6,7},{7,4},{8,9},{9,10},{10,1... | collective-permute-start | bytes 442376 | tf_op jit(solution)/shard_map/ppermute | solution.py:1109
  210.0 17.0 %collective-permute-start.24 = (bf16[24,3072]{1,0:T(8,128)(2,1)S(1)}, bf16[24,3072]{1,0:T(8,128)(2,1)S(1)}, u32[]{:S(2)}, u32[]{:S(2)}) collective-permute-start(bf16[24,3072]{1,0:T(8,128)(2,1)S(1)} %get-tuple-element.187), channel_id=1, source_target_pairs={{0,2},{1,3},{2,0},{3,1},{4,6},{5,7},{6,4},{7,5},{8,10},{9,11},{10,... | collective-permute-start | bytes 442376 | tf_op jit(solution)/shard_map/ppermute | solution.py:1109
  212.4 14.7 %collective-permute-start.25 = (bf16[24,3072]{1,0:T(8,128)(2,1)S(1)}, bf16[24,3072]{1,0:T(8,128)(2,1)S(1)}, u32[]{:S(2)}, u32[]{:S(2)}) collective-permute-start(bf16[24,3072]{1,0:T(8,128)(2,1)S(1)} %get-tuple-element.186), channel_id=1, source_target_pairs={{0,3},{1,0},{2,1},{3,2},{4,7},{5,4},{6,5},{7,6},{8,11},{9,8},{10,9... | collective-permute-start | bytes 442376 | tf_op jit(solution)/shard_map/ppermute | solution.py:1109
  244.7 10.2 %collective-permute-start.35 = (bf16[4,96,896]{2,1,0:T(8,128)(2,1)}, bf16[4,96,896]{2,1,0:T(8,128)(2,1)}, u32[]{:S(2)}, u32[]{:S(2)}) collective-permute-start(bf16[4,96,896]{2,1,0:T(8,128)(2,1)} %get-tuple-element.161), channel_id=1, source_target_pairs={{0,4},{4,0},{8,12},{12,8},{16,20},{20,16},{24,28},{28,24},{1,5},{5... | collective-permute-start | bytes 2064392 | tf_op jit(solution)/shard_map/ppermute | solution.py:1034
  244.8 14.7 %collective-permute-start.32 = (bf16[4,96,1024]{2,1,0:T(8,128)(2,1)}, bf16[4,96,1024]{2,1,0:T(8,128)(2,1)}, u32[]{:S(2)}, u32[]{:S(2)}) collective-permute-start(bf16[4,96,1024]{2,1,0:T(8,128)(2,1)} %get-tuple-element.159), channel_id=1, source_target_pairs={{0,4},{4,0},{8,12},{12,8},{16,20},{20,16},{24,28},{28,24},{1,5},{5... | collective-permute-start | bytes 2359304 | tf_op jit(solution)/shard_map/ppermute | solution.py:1034
  245.3 58.3 %all-to-all-start.3 = ((bf16[4,256,768]{2,1,0:T(8,128)(2,1)}), bf16[4,256,768]{2,1,0:T(8,128)(2,1)}, u32[]{:S(2)}, u32[]{:S(2)}) async-start(bf16[4,256,768]{2,1,0:T(8,128)(2,1)} %bitcast.198), calls=%async_computation.3 | async-start | bytes 3145728 | tf_op jit(solution)/shard_map/all_to_all | solution.py:1146
  256.2 11.8 %collective-permute-start.36 = (bf16[2,4,24,896]{3,2,1,0:T(8,128)(2,1)S(1)}, bf16[2,4,24,896]{3,2,1,0:T(8,128)(2,1)}, u32[]{:S(2)}, u32[]{:S(2)}) collective-permute-start(bf16[2,4,24,896]{3,2,1,0:T(8,128)(2,1)S(1)} %fusion.8), channel_id=1, source_target_pairs={{0,16},{4,20},{8,24},{12,28},{16,0},{20,4},{24,8},{28,12},{1,17},{... | collective-permute-start | bytes 1032200 | tf_op jit(solution)/shard_map/ppermute | solution.py:1034
  260.7 12.0 %collective-permute-start.33 = (bf16[2,4,24,1024]{3,2,1,0:T(8,128)(2,1)S(1)}, bf16[2,4,24,1024]{3,2,1,0:T(8,128)(2,1)S(1)}, u32[]{:S(2)}, u32[]{:S(2)}) collective-permute-start(bf16[2,4,24,1024]{3,2,1,0:T(8,128)(2,1)S(1)} %fusion.7), channel_id=1, source_target_pairs={{0,8},{4,12},{8,0},{12,4},{16,24},{20,28},{24,16},{28,20},{1,9},{5... | collective-permute-start | bytes 1179656 | tf_op jit(solution)/shard_map/ppermute | solution.py:1034
  262.1 22.3 %collective-permute-start.29 = (f32[8,1792]{1,0:T(8,128)S(1)}, f32[8,1792]{1,0:T(8,128)S(1)}, u32[]{:S(2)}, u32[]{:S(2)}) collective-permute-start(f32[8,1792]{1,0:T(8,128)S(1)} %add.216.refs_0_), channel_id=1, source_target_pairs={{0,1},{1,2},{2,3},{3,0},{4,5},{5,6},{6,7},{7,4},{8,9},{9,10},{10,1... | collective-permute-start | bytes 172040 | tf_op jit(solution)/shard_map/ppermute | solution.py:1376
  264.2 31.9 %collective-permute-start.30 = (f32[8,1792]{1,0:T(8,128)S(1)}, f32[8,1792]{1,0:T(8,128)S(1)}, u32[]{:S(2)}, u32[]{:S(2)}) collective-permute-start(f32[8,1792]{1,0:T(8,128)S(1)} %add.216.refs_0_), channel_id=1, source_target_pairs={{0,2},{1,3},{2,0},{3,1},{4,6},{5,7},{6,4},{7,5},{8,10},{9,11},{10,... | collective-permute-start | bytes 172040 | tf_op jit(solution)/shard_map/ppermute | solution.py:1376
  266.6 29.5 %collective-permute-start.31 = (f32[8,1792]{1,0:T(8,128)S(1)}, f32[8,1792]{1,0:T(8,128)S(1)}, u32[]{:S(2)}, u32[]{:S(2)}) collective-permute-start(f32[8,1792]{1,0:T(8,128)S(1)} %add.216.refs_0_), channel_id=1, source_target_pairs={{0,3},{1,0},{2,1},{3,2},{4,7},{5,4},{6,5},{7,6},{8,11},{9,8},{10,9... | collective-permute-start | bytes 172040 | tf_op jit(solution)/shard_map/ppermute | solution.py:1376
  280.1 16.0 %collective-permute-start.38 = (bf16[24,1920]{1,0:T(8,128)(2,1)S(1)}, bf16[24,1920]{1,0:T(8,128)(2,1)S(1)}, u32[]{:S(2)}, u32[]{:S(2)}) collective-permute-start(bf16[24,1920]{1,0:T(8,128)(2,1)S(1)} %get-tuple-element.216), channel_id=1, source_target_pairs={{0,1},{1,2},{2,3},{3,0},{4,5},{5,6},{6,7},{7,4},{8,9},{9,10},{10,1... | collective-permute-start | bytes 276488 | tf_op jit(solution)/shard_map/ppermute | solution.py:1109
  282.2 17.0 %collective-permute-start.39 = (bf16[24,1920]{1,0:T(8,128)(2,1)S(1)}, bf16[24,1920]{1,0:T(8,128)(2,1)S(1)}, u32[]{:S(2)}, u32[]{:S(2)}) collective-permute-start(bf16[24,1920]{1,0:T(8,128)(2,1)S(1)} %get-tuple-element.217), channel_id=1, source_target_pairs={{0,2},{1,3},{2,0},{3,1},{4,6},{5,7},{6,4},{7,5},{8,10},{9,11},{10,... | collective-permute-start | bytes 276488 | tf_op jit(solution)/shard_map/ppermute | solution.py:1109
  284.5 14.7 %collective-permute-start.40 = (bf16[24,1920]{1,0:T(8,128)(2,1)S(1)}, bf16[24,1920]{1,0:T(8,128)(2,1)S(1)}, u32[]{:S(2)}, u32[]{:S(2)}) collective-permute-start(bf16[24,1920]{1,0:T(8,128)(2,1)S(1)} %get-tuple-element.215), channel_id=1, source_target_pairs={{0,3},{1,0},{2,1},{3,2},{4,7},{5,4},{6,5},{7,6},{8,11},{9,8},{10,9... | collective-permute-start | bytes 276488 | tf_op jit(solution)/shard_map/ppermute | solution.py:1109
  (52 other events, 366.2 us)

commit v3 on v2

--- a/solution.py
+++ b/solution.py
@@ -593,13 +593,6 @@
     wb_other,
     dx_ref,
     dsmall_ref,
-    a_send,
-    a_keep,
-    b_send,
-    b_keep,
-    normed_ref,
-    a_sum,
-    b_sum,
     wg_ref,
     wa_ref,
     wb_ref,
@@ -618,8 +611,6 @@
         copies += fetch_weight(core_ref, wa_own, wa_other, wa_ref, wa_sems)
         copies += fetch_weight(core_ref, wb_own, wb_other, wb_ref, wb_sems)
         dsmall_ref[...] = dsmall_in_ref[...]
-        a_sum[...] = jnp.zeros_like(a_sum)
-        b_sum[...] = jnp.zeros_like(b_sum)
         for copy in copies:
             copy.wait()
 
@@ -636,20 +627,26 @@
         scaled * d_normed, axis=0, keepdims=True
     )
     gain = small_ref[gain_row : gain_row + 1, :width]
-    normed_ref[...] = (scaled * gain).astype(bf16)
-    add_product(a_sum, normed_ref, dproj_ref[:, :wide_a])
-    add_product(b_sum, normed_ref, dproj_ref[:, wide_a:])
     inner_grad = gain * d_normed
     cross = jnp.mean(scaled * inner_grad, axis=-1, keepdims=True)
     dx_ref[...] = (scale * (inner_grad - scaled * cross)).astype(bf16)
-    last = jnp.logical_and(
-        pl.program_id(0) == pl.num_programs(0) - 1, pl.program_id(1) == pl.num_programs(1) - 1
-    )
-
-    @pl.when(last)
-    def _():
-        hand_out(core_ref[0], a_sum, a_send, a_keep)
-        hand_out(core_ref[0], b_sum, b_send, b_keep)
+
+
+def front_grad_kernel(
+    core_ref, normed_ref, dproj_ref, a_send, a_keep, b_send, b_keep, a_sum, b_sum
+):
+    turned = normed_ref[...].T
+    at = 0
+    for total, send, keep in ((a_sum, a_send, a_keep), (b_sum, b_send, b_keep)):
+        for column in range(0, total.shape[1], lanes):
+            here = slice(column, column + lanes)
+            if column % (2 * lanes) == 0 and column + 2 * lanes <= total.shape[1]:
+                here = slice(column, column + 2 * lanes)
+            elif column % (2 * lanes) != 0:
+                continue
+            total[:, here] = dot(turned, dproj_ref[:, at + here.start : at + here.stop])
+        at += total.shape[1]
+        hand_out(core_ref[0], total, send, keep)
 
 
 def adam_kernel(
@@ -695,7 +692,6 @@
     half = inner // 2
     update(4, rest[:, inner : inner + half], (slice(0, rows), slice(None)))
     update(4, rest[:, inner + half :], (slice(rows, 2 * rows), slice(None)))
-    me = rates_ref[6].astype(jnp.int32)
 
     place = rates_ref[7].astype(jnp.int32)
     terms = [ref[...] for ref in sum_refs]
@@ -705,7 +701,7 @@
 
     def own(at, count):
         wide = sums.shape[1]
-        shift = lax.rem(wide - me * count, wide)
+        shift = lax.rem(wide - place * count, wide)
         return pltpu.roll(sums, shift, 1)[at, :count]
 
     update(0, own(slice(taps + 1, taps + 2), ins[0].shape[1]), everything)
@@ -962,9 +958,6 @@
 def input_grad(dims, core, tokens, dgate, dproj, small, dsmall, wg, wa, wb):
     part, size, piece, width, inner, heads, taps = dims
     rows = part * size * piece
-    blocks = wa[0].shape[0]
-    wide_a, wide_b = wa[0].shape[2], wb[0].shape[2]
-    handed = handed_out(width, wide_a, blocks) + handed_out(width, wide_b, blocks)
     return pl.pallas_call(
         partial(input_grad_kernel, gain_row=taps + 1),
         grid=(part, size),
@@ -982,22 +975,31 @@
             ANY,
             ANY,
         ],
-        out_specs=[by_block((piece, width), size), whole(dsmall.shape)]
-        + [whole(array.shape) for array in handed],
+        out_specs=[by_block((piece, width), size), whole(dsmall.shape)],
         out_shape=[
             jax.ShapeDtypeStruct((rows, width), bf16),
             jax.ShapeDtypeStruct(dsmall.shape, f32),
-        ]
-        + handed,
-        scratch_shapes=[
-            pltpu.VMEM((piece, width), bf16),
-            pltpu.VMEM((width, wide_a), f32),
-            pltpu.VMEM((width, wide_b), f32),
-        ]
-        + weight_scratch(wg, wa, wb),
+        ],
+        scratch_shapes=weight_scratch(wg, wa, wb),
         compiler_params=params(),
         cost_estimate=cost(1, 1, 0),
     )(core, tokens, dgate, dproj, small, dsmall, *wg, *wa, *wb)
+
+
+def front_grad(core, normed, dproj, wide_a, blocks):
+    width = normed.shape[1]
+    wide_b = dproj.shape[1] - wide_a
+    handed = handed_out(width, wide_a, blocks) + handed_out(width, wide_b, blocks)
+    vmem = pl.BlockSpec(memory_space=pltpu.VMEM)
+    return pl.pallas_call(
+        front_grad_kernel,
+        in_specs=[SMEM, vmem, vmem],
+        out_specs=[vmem] * 4,
+        out_shape=handed,
+        scratch_shapes=[pltpu.VMEM((width, wide_a), f32), pltpu.VMEM((width, wide_b), f32)],
+        compiler_params=pltpu.CompilerParams(vmem_limit_bytes=vmem_bytes),
+        cost_estimate=cost(6_000_000_000, 20_000_000, 0),
+    )(core, normed, dproj)
 
 
 def adam(rates, sums, gate_grads, front_grads, states, heads, taps):
@@ -1054,10 +1056,10 @@
     return jnp.stack([low, high], axis=at)
 
 
-def gather_seq(shard):
+def gather_seq(shard, *others):
     block = shard
     for done, bit in enumerate(reversed(range(bit_count(lax.axis_size("seq"))))):
-        block = gather_bit(block, "seq", bit, done)
+        block = gather_bit(block, "seq", bit, done, *(others if done == 0 else ()))
     return block.reshape((-1,) + shard.shape)
 
 
@@ -1110,10 +1112,8 @@
     return arrivals
 
 
-def sum_over(block, axis, *others):
-    for bit in reversed(range(bit_count(lax.axis_size(axis)))):
-        if bit == 0 and others:
-            block = after(block, *others)
+def sum_bits(block, axis, bits):
+    for bit in bits:
         block = block + swap(block, axis, bit)
     return block
 
@@ -1224,11 +1224,12 @@
         ]
     )
     shard = jnp.concatenate([in_low, out_low_own[0], out_low_own[1]], axis=1)
-    half = width // 2
+    half = width // 6
     both = jnp.concatenate([layer_in, out_grad[:, :, :half]], axis=2)
+    second = lax.optimization_barrier(out_grad[:, :, half:])
     if own_rows >= tap_rows + 2:
         shard = jnp.concatenate([shard, padded(own_small, own_rows, lanes)], axis=1)
-        gathered = gather_seq(shard)
+        gathered = gather_seq(shard, both, second, head, skip)
         seq_small = gathered[:, : tap_rows + 2, -lanes:]
     else:
         gathered = gather_seq(shard)
@@ -1261,7 +1262,13 @@
     for step in range(last):
         wa = gather_dp_bit(wa, order_a, step)
         wb = gather_dp_bit(wb, order_b, step)
-    wg, wo = after((wg, wo), wa, wb)
+    small = sum_bits(small, "dp", order_a[:-1])
+    for step in range(last):
+        if step == 1:
+            wg, wo = after((wg, wo), wa, wb, small)
+        if step < last - 1:
+            wg = gather_dp_bit(wg, order_a, step)
+            wo = gather_dp_bit(wo, order_b, step)
 
     def core_halves(block):
         block = block.reshape(owners // 2 // seq_extent, -1, block.shape[-1])
@@ -1269,11 +1276,8 @@
 
     wb = core_halves(wb)
     wa = core_halves(wa)
-    small = sum_over(small, "dp", tokens, wa, wb, head, skip).astype(f32)
-    for step in range(last - 1):
-        wg = gather_dp_bit(wg, order_a, step)
-        wo = gather_dp_bit(wo, order_b, step)
-    cots_b = to_sequences(after(out_grad, tokens)[:, :, half:], part, size)
+    small = sum_bits(after(small, tokens, wa, wb, head, skip), "dp", [0]).astype(f32)
+    cots_b = to_sequences(after(second, tokens), part, size)
 
     edge = core
     if groups > 1:
@@ -1357,7 +1361,9 @@
         dproj = dproj.at[:, size * piece - (taps - 1) :].set(ends.astype(bf16))
         dproj = dproj.reshape(-1, conv_dim + lanes)
     tokens, g_rest = lax.optimization_barrier((after(tokens, layer_out, dproj), g_rest))
-    dx, dsmall, *handed = input_grad(dims, core, tokens, dgate, dproj, small, dsmall, wg, wa, wb)
+    dx, dsmall = input_grad(dims, core, tokens, dgate, dproj, small, dsmall, wg, wa, wb)
+    dsmall = sum_bits(dsmall, "dp", [0])
+    handed = front_grad(core, after(normed, dsmall), dproj, wide_a, owners // 2 // seq_extent)
     g_a = core_sums(*handed[:2])
     g_b = core_sums(*handed[2:])
     g_a = core_and_next(*g_a, order_a)
@@ -1367,9 +1373,26 @@
     for step in range(2, last + 1):
         g_a = scatter_dp_bit(g_a, order_a, step)
         g_b = scatter_dp_bit(g_b, order_b, step)
-    g_front = scatter_seq(jnp.concatenate([g_a, g_b], axis=2))
-    in_grad = out_grad.astype(f32) + to_pieces(dx, part, size, piece).astype(f32)
-    dsmall = sum_over(dsmall, "dp")
+    pieces = to_pieces(dx, part, size, piece)
+    in_grad = out_grad.astype(f32) + pieces.astype(f32)
+    g_front = scatter_seq(after(jnp.concatenate([g_a, g_b], axis=2), pieces))
+    dsmall = sum_bits(dsmall, "dp", order_a[-2::-1])
+    slab_wide = -(-max(3 * lanes, seq_extent * max(conv_own, own_rows, gate_own)) // lanes) * lanes
+    slab = [
+        padded(
+            lax.dynamic_slice(
+                dsmall, (at, group * seq_extent * count), (rows, seq_extent * count)
+            ),
+            rows,
+            slab_wide,
+        )
+        for at, rows, count in (
+            (0, tap_rows, conv_own),
+            (tap_rows, 1, own_rows),
+            (tap_rows + 1, 1, gate_own),
+        )
+    ]
+    dsmall = jnp.concatenate(slab + [dsmall[tap_rows + 2 :, :slab_wide]])
     sums = [dsmall]
     for distance in range(1, seq_extent):
         route = [(i, (i + distance) % seq_extent) for i in range(seq_extent)]

time: 313 us -> 299 us (0.955)
  waiting for transfers between devices: 66.6 us -> 55.8 us
  starting transfers between devices: 68.7 us -> 64.5 us
    ppermute x3, waiting for transfers between devices: 9.35 us -> 0.01 us  [local(): sums.append(lax.ppermute(dsmall, 'seq', route))]
    all_to_all x2, waiting for transfers between devices: 0.01 us -> 8.54 us  [to_pieces(): lax.all_to_all(block, 'seq', 0, 0, axis_index_groups=seq_groups(size), ti...]
    pallas_call x0 -> x1, Pallas kernels: none -> 7.53 us  [front_grad(): pl.pallas_call(front_grad_kernel, in_specs=[SMEM, vmem, vmem], out_specs=...]
    ppermute x32, waiting for transfers between devices: 50.4 us -> 44.6 us  [swap(): return lax.ppermute(block, axis, [(i, i ^ 1 << bit) for i in devices])]
    pallas_call x1, Pallas kernels: 17.6 us -> 12.7 us  [input_grad(): pl.pallas_call(partial(input_grad_kernel, gain_row=taps + 1), grid=(part,...]
    another operation x20, other arithmetic: 10.6 us -> 6.4 us  [gather_bit(): return jnp.stack([low, high], axis=at)]
    unnamed x77 -> x69, local copies, waits for them, and re-layouts: 7.01 us -> 7.88 us
  transfers between devices with their start and end apart: 45 -> 45, of which waited for: 19 -> 19; matrix products, arithmetic and copies ran while one was open for 10% -> 11% of each run, Pallas kernels for 25% -> 25%
where the time goes in v3:
time: 299 us; the launch traced here: 294 us
  Pallas kernels  124 us (41%)
  starting transfers between devices  64.5 us (22%)
  waiting for transfers between devices  55.8 us (19%)
  other arithmetic  31.4 us (11%)
  local copies, waits for them, and re-layouts  16.2 us (5%)
    pallas_call x4, Pallas kernels, mixer_backward(): pl.pallas_call(partial(mixer_backward_kernel, heads=heads, inner=inner, t...  49.8 us
    ppermute x32, waiting for transfers between devices, swap(): return lax.ppermute(block, axis, [(i, i ^ 1 << bit) for i in devices])  44.6 us
    ppermute x32, starting transfers between devices, swap(): return lax.ppermute(block, axis, [(i, i ^ 1 << bit) for i in devices])  28.9 us
    pallas_call x1, Pallas kernels, gate_step(): pl.pallas_call(partial(gate_kernel, gain_row=taps + 2), grid=(part, size)...  25.6 us
    pallas_call x1, Pallas kernels, mixer_forward(): pl.pallas_call(partial(mixer_forward_kernel, heads=heads, inner=inner, ta...  24.4 us
    pallas_call x1, Pallas kernels, input_grad(): pl.pallas_call(partial(input_grad_kernel, gain_row=taps + 1), grid=(part,...  12.7 us
    all_to_all x2, starting transfers between devices, to_sequences(): lax.all_to_all(block, 'seq', 0, 0, axis_index_groups=seq_groups(size), ti...  10.4 us
    ppermute x6, starting transfers between devices, scatter_seq(): arrivals.append(lax.ppermute(sent, 'seq', route))  9.78 us
  transfers between devices with their start and end apart: 45, of which 19 were waited for; matrix products, arithmetic and copies ran while one was open for 11% of the time, Pallas kernels for 25%

profile of v3, /device:TPU:0, one launch (start us, length us, event | category | flops | bytes accessed | tf_op | source)
XLA Modules:
  0.0 294.2 jit_solution(8181862605132914728)
XLA Ops:
  4.8 4.1 %collective-permute-start = (bf16[24,5120]{1,0:T(8,128)(2,1)S(1)}, bf16[24,5120]{1,0:T(8,128)(2,1)S(1)}, u32[]{:S(2)}, u32[]{:S(2)}) collective-permute-start(bf16[24,5120]{1,0:T(8,128)(2,1)S(1)} %fusion.11), channel_id=1, source_target_pairs={{0,2},{1,3},{2,0},{3,1},{4,6},{5,7},{6,4},{7,5},{8,10},{9,11},{10,... | collective-permute-start | bytes 737288 | tf_op jit(solution)/shard_map/ppermute | solution.py:1036
  11.4 2.8 pad_maximum_fusion
  14.2 5.9 %collective-permute-done = bf16[24,5120]{1,0:T(8,128)(2,1)S(1)} collective-permute-done((bf16[24,5120]{1,0:T(8,128)(2,1)S(1)}, bf16[24,5120]{1,0:T(8,128)(2,1)S(1)}, u32[]{:S(2)}, u32[]{:S(2)}) %collective-permute-start) | collective-permute-done | bytes 245792 | tf_op jit(solution)/shard_map/ppermute | solution.py:1036
  21.0 4.6 %all-to-all-start = ((bf16[4,256,896]{2,1,0:T(8,128)(2,1)}), bf16[4,256,896]{2,1,0:T(8,128)(2,1)S(1)}, u32[]{:S(2)}, u32[]{:S(2)}) async-start(bf16[4,256,896]{2,1,0:T(8,128)(2,1)} %pad_maximum_fusion), calls=%async_computation | async-start | bytes 3670016 | tf_op jit(solution)/shard_map/all_to_all | solution.py:1130
  25.7 8.8 %collective-permute-done.1 = bf16[2,24,5120]{2,1,0:T(8,128)(2,1)S(1)} collective-permute-done((bf16[2,24,5120]{2,1,0:T(8,128)(2,1)S(1)}, bf16[2,24,5120]{2,1,0:T(8,128)(2,1)S(1)}, u32[]{:S(2)}, u32[]{:S(2)}) %collective-permute-start.1) | collective-permute-done | bytes 491552 | tf_op jit(solution)/shard_map/ppermute | solution.py:1036
  37.5 1.9 collective-permute-start.5
  39.8 2.1 collective-permute-start.9
  46.0 8.6 %collective-permute-done.2 = bf16[4,24,1024]{2,1,0:T(8,128)(2,1)S(1)} collective-permute-done((bf16[4,24,1024]{2,1,0:T(8,128)(2,1)S(1)}, bf16[4,24,1024]{2,1,0:T(8,128)(2,1)S(1)}, u32[]{:S(2)}, u32[]{:S(2)}) %collective-permute-start.2) | collective-permute-done | bytes 196640 | tf_op jit(solution)/shard_map/ppermute | solution.py:1036
  58.6 4.0 %collective-permute-done.3 = bf16[2,4,24,1024]{3,2,1,0:T(8,128)(2,1)S(1)} collective-permute-done((bf16[2,4,24,1024]{3,2,1,0:T(8,128)(2,1)S(1)}, bf16[2,4,24,1024]{3,2,1,0:T(8,128)(2,1)S(1)}, u32[]{:S(2)}, u32[]{:S(2)}) %collective-permute-start.3) | collective-permute-done | bytes 393248 | tf_op jit(solution)/shard_map/ppermute | solution.py:1036
  69.7 5.8 %all-to-all-start.1 = ((bf16[4,256,640]{2,1,0:T(8,128)(2,1)}), bf16[4,256,640]{2,1,0:T(8,128)(2,1)S(1)}, u32[]{:S(2)}, u32[]{:S(2)}) async-start(bf16[4,256,640]{2,1,0:T(8,128)(2,1)} %slice.96), calls=%async_computation.1 | async-start | bytes 2621440 | tf_op jit(solution)/shard_map/all_to_all | solution.py:1130
  76.1 24.4 %shard_map.390 = (bf16[1024,768]{1,0:T(8,128)(2,1)}, f32[56,264,128]{2,1,0:T(8,128)}, f32[1024,128]{1,0:T(8,128)}, f32[1024,128]{1,0:T(8,128)}, f32[1024,1536]{1...) custom-call(s32[1]{0:T(128)} %bitcast.core_ref.edge_ref.start_ref.before_ref.next_ref._, ...), custom_call_target="tpu_custom_call" | custom-call | flops 1 | bytes 1 | tf_op jit(solution)/shard_map/pallas_call | solution.py:783
  108.5 25.6 %shard_map.391 = (bf16[1024,768]{1,0:T(8,128)(2,1)}, bf16[1024,1536]{1,0:T(8,128)(2,1)}, bf16[1024,1536]{1,0:T(8,128)(2,1)}, f32[8,1536]{1,0:T(8,128)}, bf16[4,1...) custom-call(s32[1]{0:T(128)} %bitcast.core_ref.edge_ref.start_ref.before_r, ...), custom_call_target="tpu_custom_call" | custom-call | flops 1 | bytes 1 | tf_op jit(solution)/shard_map/pallas_call | solution.py:848
  134.7 12.1 %shard_map.392 = (bf16[1024,1920]{1,0:T(8,128)(2,1)}, f32[8,1792]{1,0:T(8,128)}, f32[128,1536]{1,0:T(8,128)}, f32[14,8,128]{2,1,0:T(8,128)}) custom-call(f32[56,264,128]{2,1,0:T(8,128)} %get-tuple-element.116.ext_ref, f32[1024,128]{1,0:T(8,128)} %get-tuple-element.117.dtr_ref, f32[1024,128]{1,0:T(8,128)} %get-tuple-element.118.cum_ref, ...), custom_call_target="tpu_custom_call" | custom-call | flops 1 | bytes 1 | tf_op jit(solution)/shard_map/pallas_call | solution.py:907
  147.8 2.6 fusion.4
  153.5 5.2 %all-to-all-start.2 = ((bf16[4,256,768]{2,1,0:T(8,128)(2,1)}), bf16[4,256,768]{2,1,0:T(8,128)(2,1)S(1)}, u32[]{:S(2)}, u32[]{:S(2)}) async-start(bf16[4,256,768]{2,1,0:T(8,128)(2,1)} %bitcast.204), calls=%async_computation.2 | async-start | bytes 3145728 | tf_op jit(solution)/shard_map/all_to_all | solution.py:1146
  158.7 12.5 %shard_map.393 = (bf16[1024,1920]{1,0:T(8,128)(2,1)}, f32[8,1792]{1,0:T(8,128)}, f32[128,1536]{1,0:T(8,128)}, f32[14,8,128]{2,1,0:T(8,128)}) custom-call(f32[56,264,128]{2,1,0:T(8,128)} %get-tuple-element.116.ext_ref, f32[1024,128]{1,0:T(8,128)} %get-tuple-element.117.dtr_ref, ...), custom_call_target="tpu_custom_call", output_to_operand_aliasing={{0}: (14, {})} | custom-call | flops 1 | bytes 1 | tf_op jit(solution)/shard_map/pallas_call | solution.py:907
  176.9 12.8 %shard_map.394 = (bf16[1024,1920]{1,0:T(8,128)(2,1)}, f32[8,1792]{1,0:T(8,128)}, f32[128,1536]{1,0:T(8,128)}, f32[14,8,128]{2,1,0:T(8,128)}) custom-call(f32[56,264,128]{2,1,0:T(8,128)} %get-tuple-element.116.ext_ref, f32[1024,128]{1,0:T(8,128)} %get-tuple-element.117.dtr_ref, ...), custom_call_target="tpu_custom_call", output_to_operand_aliasing={{0}: (14, {})} | custom-call | flops 1 | bytes 1 | tf_op jit(solution)/shard_map/pallas_call | solution.py:907
  191.3 2.1 collective-permute-start.23
  193.4 2.4 collective-permute-start.24
  198.0 12.4 %shard_map.395 = (bf16[1024,1920]{1,0:T(8,128)(2,1)}, f32[8,1792]{1,0:T(8,128)}, f32[128,1536]{1,0:T(8,128)}, f32[14,8,128]{2,1,0:T(8,128)}) custom-call(f32[56,264,128]{2,1,0:T(8,128)} %get-tuple-element.116.ext_ref, f32[1024,128]{1,0:T(8,128)} %get-tuple-element.117.dtr_ref, ...), custom_call_target="tpu_custom_call", output_to_operand_aliasing={{0}: (14, {})} | custom-call | flops 1 | bytes 1 | tf_op jit(solution)/shard_map/pallas_call | solution.py:907
  210.4 12.7 %shard_map.396 = (bf16[1024,768]{1,0:T(8,128)(2,1)}, f32[8,1792]{1,0:T(8,128)}) custom-call(s32[1]{0:T(128)} %bitcast.core_ref.edge_ref.start_ref.before_ref.next_ref._, bf16[1024,896]{1,0:T(8,128)(2,1)} %bitcast.179, bf16[1024,1536]{1,0:T(8,128)(2,1)} %get-tuple-element.154.dgate_ref, bf16[1024,1920]{1,0:T(8,128)(2,1)} %get-tuple-element.149.dproj_ref, ...), custom_call_target="tpu_custom_call" | custom-call | flops 1 | bytes 1 | tf_op jit(solution)/shard_map/pallas_call | solution.py:961
  225.6 7.5 %shard_map.397 = (bf16[4,96,1024]{2,1,0:T(8,128)(2,1)}, f32[4,96,1024]{2,1,0:T(8,128)}, bf16[4,96,896]{2,1,0:T(8,128)(2,1)}, f32[4,96,896]{2,1,0:T(8,128)}) custom-call(s32[1]{0:T(128)} %bitcast.core_ref.edge_ref.start_ref.before_ref.next_ref._, bf16[1024,768]{1,0:T(8,128)(2,1)} %get-tuple-element.162.normed_ref, bf16[1024,1920]{1,0:T(8,128)(2,1)} %get-tuple-element.149.dproj_ref), custom_call_target="tpu_custom_call" | custom-call | flops 6000000000 | bytes 20000000 | tf_op jit(solution)/shard_map/pallas_call | solution.py:994
  233.9 4.4 %all-to-all-start.3 = ((bf16[4,256,768]{2,1,0:T(8,128)(2,1)}), bf16[4,256,768]{2,1,0:T(8,128)(2,1)}, u32[]{:S(2)}, u32[]{:S(2)}) async-start(bf16[4,256,768]{2,1,0:T(8,128)(2,1)} %bitcast.63), calls=%async_computation.3 | async-start | bytes 3145728 | tf_op jit(solution)/shard_map/all_to_all | solution.py:1146
  239.6 2.9 %collective-permute-done.27 = f32[8,1792]{1,0:T(8,128)S(1)} collective-permute-done((f32[8,1792]{1,0:T(8,128)S(1)}, f32[8,1792]{1,0:T(8,128)S(1)}, u32[]{:S(2)}, u32[]{:S(2)}) %collective-permute-start.27) | collective-permute-done | bytes 57376 | tf_op jit(solution)/shard_map/ppermute | solution.py:1036
  243.8 3.0 %collective-permute-done.28 = f32[8,1792]{1,0:T(8,128)S(1)} collective-permute-done((f32[8,1792]{1,0:T(8,128)S(1)}, f32[8,1792]{1,0:T(8,128)S(1)}, u32[]{:S(2)}, u32[]{:S(2)}) %collective-permute-start.28) | collective-permute-done | bytes 57376 | tf_op jit(solution)/shard_map/ppermute | solution.py:1036
  251.3 2.0 collective-permute-start.29
  253.2 2.4 collective-permute-start.30
  263.7 3.7 %collective-permute-done.34 = bf16[4,24,1024]{2,1,0:T(8,128)(2,1)S(1)} collective-permute-done((bf16[4,24,1024]{2,1,0:T(8,128)(2,1)S(1)}, bf16[4,24,1024]{2,1,0:T(8,128)(2,1)S(1)}, u32[]{:S(2)}, u32[]{:S(2)}) %collective-permute-start.34) | collective-permute-done | bytes 196640 | tf_op jit(solution)/shard_map/ppermute | solution.py:1036
  268.3 8.5 %all-to-all-done.3 = bf16[4,256,768]{2,1,0:T(8,128)(2,1)} async-done(((bf16[4,256,768]{2,1,0:T(8,128)(2,1)}), bf16[4,256,768]{2,1,0:T(8,128)(2,1)}, u32[]{:S(2)}, u32[]{:S(2)}) %all-to-all-start.3) | async-done | bytes 1572896 | tf_op jit(solution)/shard_map/all_to_all | solution.py:1146
  278.1 2.0 collective-permute-start.39
  280.1 3.4 %convert_add_fusion = f32[4,256,768]{2,1,0:T(8,128)} fusion(bf16[4,256,768]{2,1,0:T(8,128)(2,1)} %all-to-all-done.3, bf16[4,256,768]{2,1,0:T(8,128)(2,1)S(1)} %copy-done.5), kind=kLoop, calls=%fused_computation | loop fusion | flops 2359296 | bytes 6291456 | tf_op jit(solution)/shard_map/add | solution.py:1377
  289.1 3.5 %shard_map.398 = (f32[1,24]{1,0:T(1,128)}, f32[1,24]{1,0:T(1,128)}, f32[1,24]{1,0:T(1,128)}, f32[24,3352]{1,0:T(8,128)}, f32[24,3352]{1,0:T(8,128)}, /*index=5*/...) custom-call(f32[8]{0:T(128)} %pad_maximum_fusion.17.rates_ref, ...), custom_call_target="tpu_custom_call" | custom-call | flops 1 | bytes 1 | tf_op jit(solution)/shard_map/pallas_call | solution.py:1015
  (228 shorter events, 74.8 us)
Async XLA Ops:
  4.8 15.3 %collective-permute-start = (bf16[24,5120]{1,0:T(8,128)(2,1)S(1)}, bf16[24,5120]{1,0:T(8,128)(2,1)S(1)}, u32[]{:S(2)}, u32[]{:S(2)}) collective-permute-start(bf16[24,5120]{1,0:T(8,128)(2,1)S(1)} %fusion.11), channel_id=1, source_target_pairs={{0,2},{1,3},{2,0},{3,1},{4,6},{5,7},{6,4},{7,5},{8,10},{9,11},{10,... | collective-permute-start | bytes 737288 | tf_op jit(solution)/shard_map/ppermute | solution.py:1036
  20.3 14.2 %collective-permute-start.1 = (bf16[2,24,5120]{2,1,0:T(8,128)(2,1)S(1)}, bf16[2,24,5120]{2,1,0:T(8,128)(2,1)S(1)}, u32[]{:S(2)}, u32[]{:S(2)}) collective-permute-start(bf16[2,24,5120]{2,1,0:T(8,128)(2,1)S(1)} %pad_maximum_fusion.10), channel_id=1, source_target_pairs={{0,1},{1,0},{2,3},{3,2},{4,5},{5,4},{6,7},{7,6},{8,9},{9,8},{10,11... | collective-permute-start | bytes 1474568 | tf_op jit(solution)/shard_map/ppermute | solution.py:1036
  21.0 47.2 %all-to-all-start = ((bf16[4,256,896]{2,1,0:T(8,128)(2,1)}), bf16[4,256,896]{2,1,0:T(8,128)(2,1)S(1)}, u32[]{:S(2)}, u32[]{:S(2)}) async-start(bf16[4,256,896]{2,1,0:T(8,128)(2,1)} %pad_maximum_fusion), calls=%async_computation | async-start | bytes 3670016 | tf_op jit(solution)/shard_map/all_to_all | solution.py:1130
  37.5 7.8 %collective-permute-start.5 = (bf16[4,24,896]{2,1,0:T(8,128)(2,1)S(1)}, bf16[4,24,896]{2,1,0:T(8,128)(2,1)S(1)}, u32[]{:S(2)}, u32[]{:S(2)}) collective-permute-start(bf16[4,24,896]{2,1,0:T(8,128)(2,1)S(1)} %slice.122), channel_id=1, source_target_pairs={{0,8},{4,12},{8,0},{12,4},{16,24},{20,28},{24,16},{28,20},{1,9},{5... | collective-permute-start | bytes 516104 | tf_op jit(solution)/shard_map/ppermute | solution.py:1036
  42.0 14.1 %collective-permute-start.12 = (bf16[4,48,768]{2,1,0:T(8,128)(2,1)S(1)}, bf16[4,48,768]{2,1,0:T(8,128)(2,1)S(1)}, u32[]{:S(2)}, u32[]{:S(2)}) collective-permute-start(bf16[4,48,768]{2,1,0:T(8,128)(2,1)S(1)} %bitcast.209), channel_id=1, source_target_pairs={{0,8},{4,12},{8,0},{12,4},{16,24},{20,28},{24,16},{28,20},{1,9},{5... | collective-permute-start | bytes 884744 | tf_op jit(solution)/shard_map/ppermute | solution.py:1036
  42.1 20.8 %collective-permute-start.11 = (bf16[4,24,1536]{2,1,0:T(8,128)(2,1)S(1)}, bf16[4,24,1536]{2,1,0:T(8,128)(2,1)S(1)}, u32[]{:S(2)}, u32[]{:S(2)}) collective-permute-start(bf16[4,24,1536]{2,1,0:T(8,128)(2,1)S(1)} %slice.135), channel_id=1, source_target_pairs={{0,16},{4,20},{8,24},{12,28},{16,0},{20,4},{24,8},{28,12},{1,17},{... | collective-permute-start | bytes 884744 | tf_op jit(solution)/shard_map/ppermute | solution.py:1036
  43.7 10.9 %collective-permute-start.2 = (bf16[4,24,1024]{2,1,0:T(8,128)(2,1)S(1)}, bf16[4,24,1024]{2,1,0:T(8,128)(2,1)S(1)}, u32[]{:S(2)}, u32[]{:S(2)}) collective-permute-start(bf16[4,24,1024]{2,1,0:T(8,128)(2,1)S(1)} %slice.121), channel_id=1, source_target_pairs={{0,16},{4,20},{8,24},{12,28},{16,0},{20,4},{24,8},{28,12},{1,17},{... | collective-permute-start | bytes 589832 | tf_op jit(solution)/shard_map/ppermute | solution.py:1036
  45.4 12.9 %collective-permute-start.6 = (bf16[2,4,24,896]{3,2,1,0:T(8,128)(2,1)S(1)}, bf16[2,4,24,896]{3,2,1,0:T(8,128)(2,1)S(1)}, u32[]{:S(2)}, u32[]{:S(2)}) collective-permute-start(bf16[2,4,24,896]{3,2,1,0:T(8,128)(2,1)S(1)} %pad_maximum_fusion.12), channel_id=1, source_target_pairs={{0,16},{4,20},{8,24},{12,28},{16,0},{20,4},{24,8},{28,12},{1,17},{... | collective-permute-start | bytes 1032200 | tf_op jit(solution)/shard_map/ppermute | solution.py:1036
  54.7 7.8 %collective-permute-start.3 = (bf16[2,4,24,1024]{3,2,1,0:T(8,128)(2,1)S(1)}, bf16[2,4,24,1024]{3,2,1,0:T(8,128)(2,1)S(1)}, u32[]{:S(2)}, u32[]{:S(2)}) collective-permute-start(bf16[2,4,24,1024]{3,2,1,0:T(8,128)(2,1)S(1)} %pad_maximum_fusion.11), channel_id=1, source_target_pairs={{0,8},{4,12},{8,0},{12,4},{16,24},{20,28},{24,16},{28,20},{1,9},{5... | collective-permute-start | bytes 1179656 | tf_op jit(solution)/shard_map/ppermute | solution.py:1036
  64.9 35.6 %collective-permute-start.15 = (bf16[2,4,48,768]{3,2,1,0:T(8,128)(2,1)}, bf16[2,4,48,768]{3,2,1,0:T(8,128)(2,1)}, u32[]{:S(2)}, u32[]{:S(2)}) collective-permute-start(bf16[2,4,48,768]{3,2,1,0:T(8,128)(2,1)} %pad_maximum_fusion.9), channel_id=1, source_target_pairs={{0,16},{4,20},{8,24},{12,28},{16,0},{20,4},{24,8},{28,12},{1,17},{... | collective-permute-start | bytes 1769480 | tf_op jit(solution)/shard_map/ppermute | solution.py:1036
  68.2 33.9 %collective-permute-start.13 = (bf16[2,4,24,1536]{3,2,1,0:T(8,128)(2,1)}, bf16[2,4,24,1536]{3,2,1,0:T(8,128)(2,1)}, u32[]{:S(2)}, u32[]{:S(2)}) collective-permute-start(bf16[2,4,24,1536]{3,2,1,0:T(8,128)(2,1)} %pad_maximum_fusion.8), channel_id=1, source_target_pairs={{0,8},{4,12},{8,0},{12,4},{16,24},{20,28},{24,16},{28,20},{1,9},{5... | collective-permute-start | bytes 1769480 | tf_op jit(solution)/shard_map/ppermute | solution.py:1036
  69.7 37.7 %all-to-all-start.1 = ((bf16[4,256,640]{2,1,0:T(8,128)(2,1)}), bf16[4,256,640]{2,1,0:T(8,128)(2,1)S(1)}, u32[]{:S(2)}, u32[]{:S(2)}) async-start(bf16[4,256,640]{2,1,0:T(8,128)(2,1)} %slice.96), calls=%async_computation.1 | async-start | bytes 2621440 | tf_op jit(solution)/shard_map/all_to_all | solution.py:1130
  134.1 12.7 %collective-permute-start.17 = (bf16[4,192,768]{2,1,0:T(8,128)(2,1)}, bf16[4,192,768]{2,1,0:T(8,128)(2,1)S(1)}, u32[]{:S(2)}, u32[]{:S(2)}) collective-permute-start(bf16[4,192,768]{2,1,0:T(8,128)(2,1)} %get-tuple-element.124), channel_id=1, source_target_pairs={{0,4},{4,0},{8,12},{12,8},{16,20},{20,16},{24,28},{28,24},{1,5},{5... | collective-permute-start | bytes 3538952 | tf_op jit(solution)/shard_map/ppermute | solution.py:1036
  134.3 12.5 %collective-permute-start.18 = (bf16[4,96,1536]{2,1,0:T(8,128)(2,1)}, bf16[4,96,1536]{2,1,0:T(8,128)(2,1)S(1)}, u32[]{:S(2)}, u32[]{:S(2)}) collective-permute-start(bf16[4,96,1536]{2,1,0:T(8,128)(2,1)} %get-tuple-element.126), channel_id=1, source_target_pairs={{0,4},{4,0},{8,12},{12,8},{16,20},{20,16},{24,28},{28,24},{1,5},{5... | collective-permute-start | bytes 3538952 | tf_op jit(solution)/shard_map/ppermute | solution.py:1036
  150.4 20.8 %collective-permute-start.20 = (bf16[2,4,24,1536]{3,2,1,0:T(8,128)(2,1)}, bf16[2,4,24,1536]{3,2,1,0:T(8,128)(2,1)S(1)}, u32[]{:S(2)}, u32[]{:S(2)}) collective-permute-start(bf16[2,4,24,1536]{3,2,1,0:T(8,128)(2,1)} %get-tuple-element.188), channel_id=1, source_target_pairs={{0,16},{4,20},{8,24},{12,28},{16,0},{20,4},{24,8},{28,12},{1,17},{... | collective-permute-start | bytes 1769480 | tf_op jit(solution)/shard_map/ppermute | solution.py:1036
  152.4 18.8 %collective-permute-start.19 = (bf16[2,4,48,768]{3,2,1,0:T(8,128)(2,1)}, bf16[2,4,48,768]{3,2,1,0:T(8,128)(2,1)}, u32[]{:S(2)}, u32[]{:S(2)}) collective-permute-start(bf16[2,4,48,768]{3,2,1,0:T(8,128)(2,1)} %get-tuple-element.190), channel_id=1, source_target_pairs={{0,8},{4,12},{8,0},{12,4},{16,24},{20,28},{24,16},{28,20},{1,9},{5... | collective-permute-start | bytes 1769480 | tf_op jit(solution)/shard_map/ppermute | solution.py:1036
  153.5 56.9 %all-to-all-start.2 = ((bf16[4,256,768]{2,1,0:T(8,128)(2,1)}), bf16[4,256,768]{2,1,0:T(8,128)(2,1)S(1)}, u32[]{:S(2)}, u32[]{:S(2)}) async-start(bf16[4,256,768]{2,1,0:T(8,128)(2,1)} %bitcast.204), calls=%async_computation.2 | async-start | bytes 3145728 | tf_op jit(solution)/shard_map/all_to_all | solution.py:1146
  173.3 16.4 %collective-permute-start.21 = (bf16[4,48,768]{2,1,0:T(8,128)(2,1)}, bf16[4,48,768]{2,1,0:T(8,128)(2,1)}, u32[]{:S(2)}, u32[]{:S(2)}) collective-permute-start(bf16[4,48,768]{2,1,0:T(8,128)(2,1)} %fusion.9), channel_id=1, source_target_pairs={{0,16},{4,20},{8,24},{12,28},{16,0},{20,4},{24,8},{28,12},{1,17},{... | collective-permute-start | bytes 884744 | tf_op jit(solution)/shard_map/ppermute | solution.py:1036
  175.9 14.9 %collective-permute-start.22 = (bf16[4,24,1536]{2,1,0:T(8,128)(2,1)S(1)}, bf16[4,24,1536]{2,1,0:T(8,128)(2,1)S(1)}, u32[]{:S(2)}, u32[]{:S(2)}) collective-permute-start(bf16[4,24,1536]{2,1,0:T(8,128)(2,1)S(1)} %fusion.10), channel_id=1, source_target_pairs={{0,8},{4,12},{8,0},{12,4},{16,24},{20,28},{24,16},{28,20},{1,9},{5... | collective-permute-start | bytes 884744 | tf_op jit(solution)/shard_map/ppermute | solution.py:1036
  191.3 19.1 %collective-permute-start.23 = (bf16[24,3072]{1,0:T(8,128)(2,1)S(1)}, bf16[24,3072]{1,0:T(8,128)(2,1)S(1)}, u32[]{:S(2)}, u32[]{:S(2)}) collective-permute-start(bf16[24,3072]{1,0:T(8,128)(2,1)S(1)} %get-tuple-element.196), channel_id=1, source_target_pairs={{0,1},{1,2},{2,3},{3,0},{4,5},{5,6},{6,7},{7,4},{8,9},{9,10},{10,1... | collective-permute-start | bytes 442376 | tf_op jit(solution)/shard_map/ppermute | solution.py:1111
  193.4 17.0 %collective-permute-start.24 = (bf16[24,3072]{1,0:T(8,128)(2,1)S(1)}, bf16[24,3072]{1,0:T(8,128)(2,1)S(1)}, u32[]{:S(2)}, u32[]{:S(2)}) collective-permute-start(bf16[24,3072]{1,0:T(8,128)(2,1)S(1)} %get-tuple-element.195), channel_id=1, source_target_pairs={{0,2},{1,3},{2,0},{3,1},{4,6},{5,7},{6,4},{7,5},{8,10},{9,11},{10,... | collective-permute-start | bytes 442376 | tf_op jit(solution)/shard_map/ppermute | solution.py:1111
  195.8 14.7 %collective-permute-start.25 = (bf16[24,3072]{1,0:T(8,128)(2,1)S(1)}, bf16[24,3072]{1,0:T(8,128)(2,1)S(1)}, u32[]{:S(2)}, u32[]{:S(2)}) collective-permute-start(bf16[24,3072]{1,0:T(8,128)(2,1)S(1)} %get-tuple-element.194), channel_id=1, source_target_pairs={{0,3},{1,0},{2,1},{3,2},{4,7},{5,4},{6,5},{7,6},{8,11},{9,8},{10,9... | collective-permute-start | bytes 442376 | tf_op jit(solution)/shard_map/ppermute | solution.py:1111
  233.1 13.9 %collective-permute-start.35 = (bf16[4,96,896]{2,1,0:T(8,128)(2,1)}, bf16[4,96,896]{2,1,0:T(8,128)(2,1)}, u32[]{:S(2)}, u32[]{:S(2)}) collective-permute-start(bf16[4,96,896]{2,1,0:T(8,128)(2,1)} %get-tuple-element.166), channel_id=1, source_target_pairs={{0,4},{4,0},{8,12},{12,8},{16,20},{20,16},{24,28},{28,24},{1,5},{5... | collective-permute-start | bytes 2064392 | tf_op jit(solution)/shard_map/ppermute | solution.py:1036
  233.9 43.0 %all-to-all-start.3 = ((bf16[4,256,768]{2,1,0:T(8,128)(2,1)}), bf16[4,256,768]{2,1,0:T(8,128)(2,1)}, u32[]{:S(2)}, u32[]{:S(2)}) async-start(bf16[4,256,768]{2,1,0:T(8,128)(2,1)} %bitcast.63), calls=%async_computation.3 | async-start | bytes 3145728 | tf_op jit(solution)/shard_map/all_to_all | solution.py:1146
  239.4 9.6 %collective-permute-start.32 = (bf16[4,96,1024]{2,1,0:T(8,128)(2,1)}, bf16[4,96,1024]{2,1,0:T(8,128)(2,1)}, u32[]{:S(2)}, u32[]{:S(2)}) collective-permute-start(bf16[4,96,1024]{2,1,0:T(8,128)(2,1)} %get-tuple-element.164), channel_id=1, source_target_pairs={{0,4},{4,0},{8,12},{12,8},{16,20},{20,16},{24,28},{28,24},{1,5},{5... | collective-permute-start | bytes 2359304 | tf_op jit(solution)/shard_map/ppermute | solution.py:1036
  248.3 8.7 %collective-permute-start.36 = (bf16[2,4,24,896]{3,2,1,0:T(8,128)(2,1)S(1)}, bf16[2,4,24,896]{3,2,1,0:T(8,128)(2,1)S(1)}, u32[]{:S(2)}, u32[]{:S(2)}) collective-permute-start(bf16[2,4,24,896]{3,2,1,0:T(8,128)(2,1)S(1)} %fusion.8), channel_id=1, source_target_pairs={{0,16},{4,20},{8,24},{12,28},{16,0},{20,4},{24,8},{28,12},{1,17},{... | collective-permute-start | bytes 1032200 | tf_op jit(solution)/shard_map/ppermute | solution.py:1036
  250.1 10.3 %collective-permute-start.33 = (bf16[2,4,24,1024]{3,2,1,0:T(8,128)(2,1)S(1)}, bf16[2,4,24,1024]{3,2,1,0:T(8,128)(2,1)S(1)}, u32[]{:S(2)}, u32[]{:S(2)}) collective-permute-start(bf16[2,4,24,1024]{3,2,1,0:T(8,128)(2,1)S(1)} %fusion.7), channel_id=1, source_target_pairs={{0,8},{4,12},{8,0},{12,4},{16,24},{20,28},{24,16},{28,20},{1,9},{5... | collective-permute-start | bytes 1179656 | tf_op jit(solution)/shard_map/ppermute | solution.py:1036
  251.3 32.2 %collective-permute-start.29 = (f32[8,384]{1,0:T(8,128)S(1)}, f32[8,384]{1,0:T(8,128)S(1)}, u32[]{:S(2)}, u32[]{:S(2)}) collective-permute-start(f32[8,384]{1,0:T(8,128)S(1)} %fusion.22.refs_0_), channel_id=1, source_target_pairs={{0,1},{1,2},{2,3},{3,0},{4,5},{5,6},{6,7},{7,4},{8,9},{9,10},{10,1... | collective-permute-start | bytes 36872 | tf_op jit(solution)/shard_map/ppermute | solution.py:1399
  253.2 33.7 %collective-permute-start.30 = (f32[8,384]{1,0:T(8,128)S(1)}, f32[8,384]{1,0:T(8,128)S(1)}, u32[]{:S(2)}, u32[]{:S(2)}) collective-permute-start(f32[8,384]{1,0:T(8,128)S(1)} %fusion.22.refs_0_), channel_id=1, source_target_pairs={{0,2},{1,3},{2,0},{3,1},{4,6},{5,7},{6,4},{7,5},{8,10},{9,11},{10,... | collective-permute-start | bytes 36872 | tf_op jit(solution)/shard_map/ppermute | solution.py:1399
  255.6 31.3 %collective-permute-start.31 = (f32[8,384]{1,0:T(8,128)S(1)}, f32[8,384]{1,0:T(8,128)S(1)}, u32[]{:S(2)}, u32[]{:S(2)}) collective-permute-start(f32[8,384]{1,0:T(8,128)S(1)} %fusion.22.refs_0_), channel_id=1, source_target_pairs={{0,3},{1,0},{2,1},{3,2},{4,7},{5,4},{6,5},{7,6},{8,11},{9,8},{10,9... | collective-permute-start | bytes 36872 | tf_op jit(solution)/shard_map/ppermute | solution.py:1399
  278.0 8.9 %collective-permute-start.38 = (bf16[24,1920]{1,0:T(8,128)(2,1)S(1)}, bf16[24,1920]{1,0:T(8,128)(2,1)S(1)}, u32[]{:S(2)}, u32[]{:S(2)}) collective-permute-start(bf16[24,1920]{1,0:T(8,128)(2,1)S(1)} %get-tuple-element.225), channel_id=1, source_target_pairs={{0,1},{1,2},{2,3},{3,0},{4,5},{5,6},{6,7},{7,4},{8,9},{9,10},{10,1... | collective-permute-start | bytes 276488 | tf_op jit(solution)/shard_map/ppermute | solution.py:1111
  278.1 8.9 %collective-permute-start.39 = (bf16[24,1920]{1,0:T(8,128)(2,1)S(1)}, bf16[24,1920]{1,0:T(8,128)(2,1)S(1)}, u32[]{:S(2)}, u32[]{:S(2)}) collective-permute-start(bf16[24,1920]{1,0:T(8,128)(2,1)S(1)} %get-tuple-element.224), channel_id=1, source_target_pairs={{0,2},{1,3},{2,0},{3,1},{4,6},{5,7},{6,4},{7,5},{8,10},{9,11},{10,... | collective-permute-start | bytes 276488 | tf_op jit(solution)/shard_map/ppermute | solution.py:1111
  (48 other events, 260.4 us)

commit v4 on v2

--- a/solution.py
+++ b/solution.py
@@ -695,7 +695,6 @@
     half = inner // 2
     update(4, rest[:, inner : inner + half], (slice(0, rows), slice(None)))
     update(4, rest[:, inner + half :], (slice(rows, 2 * rows), slice(None)))
-    me = rates_ref[6].astype(jnp.int32)
 
     place = rates_ref[7].astype(jnp.int32)
     terms = [ref[...] for ref in sum_refs]
@@ -705,7 +704,7 @@
 
     def own(at, count):
         wide = sums.shape[1]
-        shift = lax.rem(wide - me * count, wide)
+        shift = lax.rem(wide - place * count, wide)
         return pltpu.roll(sums, shift, 1)[at, :count]
 
     update(0, own(slice(taps + 1, taps + 2), ins[0].shape[1]), everything)
@@ -1054,10 +1053,10 @@
     return jnp.stack([low, high], axis=at)
 
 
-def gather_seq(shard):
+def gather_seq(shard, *others):
     block = shard
     for done, bit in enumerate(reversed(range(bit_count(lax.axis_size("seq"))))):
-        block = gather_bit(block, "seq", bit, done)
+        block = gather_bit(block, "seq", bit, done, *(others if done == 0 else ()))
     return block.reshape((-1,) + shard.shape)
 
 
@@ -1110,10 +1109,8 @@
     return arrivals
 
 
-def sum_over(block, axis, *others):
-    for bit in reversed(range(bit_count(lax.axis_size(axis)))):
-        if bit == 0 and others:
-            block = after(block, *others)
+def sum_bits(block, axis, bits):
+    for bit in bits:
         block = block + swap(block, axis, bit)
     return block
 
@@ -1224,11 +1221,12 @@
         ]
     )
     shard = jnp.concatenate([in_low, out_low_own[0], out_low_own[1]], axis=1)
-    half = width // 2
+    half = width // 6
     both = jnp.concatenate([layer_in, out_grad[:, :, :half]], axis=2)
+    second = lax.optimization_barrier(out_grad[:, :, half:])
     if own_rows >= tap_rows + 2:
         shard = jnp.concatenate([shard, padded(own_small, own_rows, lanes)], axis=1)
-        gathered = gather_seq(shard)
+        gathered = gather_seq(shard, both, second, head, skip)
         seq_small = gathered[:, : tap_rows + 2, -lanes:]
     else:
         gathered = gather_seq(shard)
@@ -1261,7 +1259,13 @@
     for step in range(last):
         wa = gather_dp_bit(wa, order_a, step)
         wb = gather_dp_bit(wb, order_b, step)
-    wg, wo = after((wg, wo), wa, wb)
+    small = sum_bits(small, "dp", order_a[:-1])
+    for step in range(last):
+        if step == 1:
+            wg, wo = after((wg, wo), wa, wb, small)
+        if step < last - 1:
+            wg = gather_dp_bit(wg, order_a, step)
+            wo = gather_dp_bit(wo, order_b, step)
 
     def core_halves(block):
         block = block.reshape(owners // 2 // seq_extent, -1, block.shape[-1])
@@ -1269,11 +1273,8 @@
 
     wb = core_halves(wb)
     wa = core_halves(wa)
-    small = sum_over(small, "dp", tokens, wa, wb, head, skip).astype(f32)
-    for step in range(last - 1):
-        wg = gather_dp_bit(wg, order_a, step)
-        wo = gather_dp_bit(wo, order_b, step)
-    cots_b = to_sequences(after(out_grad, tokens)[:, :, half:], part, size)
+    small = sum_bits(after(small, tokens, wa, wb, head, skip), "dp", [0]).astype(f32)
+    cots_b = to_sequences(after(second, tokens), part, size)
 
     edge = core
     if groups > 1:
@@ -1311,38 +1312,36 @@
     consts = (small, head, skip, summing, dgain)
     saved = (ext, dtr, cum, y, sin, dy)
 
-    def backward(carry, block, fresh=False):
-        return list(mixer_backward(dims, saved, consts, carry, (block, 1), fresh))
+    def backward(carry, blocks, fresh=False):
+        return list(mixer_backward(dims, saved, consts, carry, blocks, fresh))
 
     def fresh_carry():
         if groups == 1:
             return (core, head, core, core)
         lead = jnp.zeros((part * (conv_dim // lanes), 8, lanes), f32)
         first_out = (core, head, jnp.zeros((part * state_dim, inner), f32), lead)
-        for block in reversed(range(size)):
-            first_out = backward(first_out, block)
+        first_out = backward(first_out, (0, size))
         return (core, head, relay(first_out[2], -size), lead)
 
+    calls = [(size - 1, 1), (size - 2, 1), (0, size - 2)]
     g_out = core_sums(*handed[:2])
     g_gate = core_sums(*handed[2:])
-    carry = backward(fresh_carry(), size - 1, groups == 1)
-    for block in reversed(range(size - 1)):
-        carry[2], g_out, g_gate = lax.optimization_barrier((carry[2], g_out, g_gate))
-        step = size - 2 - block
-        if step == 0:
-            g_out = core_and_next(*g_out, order_a)
-            g_gate = core_and_next(*g_gate, order_b)
-        elif step == 1:
-            g_out = g_out[0] + g_out[1].astype(f32)
-            g_gate = g_gate[0] + g_gate[1].astype(f32)
-            for bit_step in range(2, last + 1):
-                g_out = scatter_dp_bit(g_out, order_a, bit_step)
-                g_gate = scatter_dp_bit(g_gate, order_b, bit_step)
-        elif step == 2:
-            g_rest = scatter_seq(
-                jnp.concatenate([g_gate, g_out[:, :own_rows], g_out[:, own_rows:]], axis=2)
-            )
-        carry = backward(carry, block)
+    carry = backward(fresh_carry(), calls[0], groups == 1)
+    carry[2], g_out, g_gate = lax.optimization_barrier((carry[2], g_out, g_gate))
+    g_out = core_and_next(*g_out, order_a)
+    g_gate = core_and_next(*g_gate, order_b)
+    carry = backward(carry, calls[1])
+    carry[2], g_out, g_gate = lax.optimization_barrier((carry[2], g_out, g_gate))
+    g_out = g_out[0] + g_out[1].astype(f32)
+    g_gate = g_gate[0] + g_gate[1].astype(f32)
+    for step in range(2, last + 1):
+        g_out = scatter_dp_bit(g_out, order_a, step)
+        g_gate = scatter_dp_bit(g_gate, order_b, step)
+    carry = backward(carry, calls[2])
+    carry[0], g_out, g_gate = lax.optimization_barrier((carry[0], g_out, g_gate))
+    g_rest = scatter_seq(
+        jnp.concatenate([g_gate, g_out[:, :own_rows], g_out[:, own_rows:]], axis=2)
+    )
     dproj, dsmall, _, lead = carry
     if groups > 1:
         lead = shifted_by(lead.astype(bf16), "seq", -size).astype(f32)
@@ -1356,8 +1355,9 @@
         ends = dproj[:, size * piece - (taps - 1) :].astype(f32) + fix
         dproj = dproj.at[:, size * piece - (taps - 1) :].set(ends.astype(bf16))
         dproj = dproj.reshape(-1, conv_dim + lanes)
-    tokens, g_rest = lax.optimization_barrier((after(tokens, layer_out, dproj), g_rest))
+    tokens = after(tokens, layer_out, dproj)
     dx, dsmall, *handed = input_grad(dims, core, tokens, dgate, dproj, small, dsmall, wg, wa, wb)
+    dx, dsmall, handed, g_rest = lax.optimization_barrier((dx, dsmall, handed, g_rest))
     g_a = core_sums(*handed[:2])
     g_b = core_sums(*handed[2:])
     g_a = core_and_next(*g_a, order_a)
@@ -1367,9 +1367,27 @@
     for step in range(2, last + 1):
         g_a = scatter_dp_bit(g_a, order_a, step)
         g_b = scatter_dp_bit(g_b, order_b, step)
+    pieces = to_pieces(dx, part, size, piece)
+    in_grad = out_grad.astype(f32) + pieces.astype(f32)
     g_front = scatter_seq(jnp.concatenate([g_a, g_b], axis=2))
-    in_grad = out_grad.astype(f32) + to_pieces(dx, part, size, piece).astype(f32)
-    dsmall = sum_over(dsmall, "dp")
+    dsmall = sum_bits(dsmall, "dp", order_a[:0:-1])
+    dsmall = sum_bits(after(dsmall, pieces), "dp", order_a[:1])
+    slab_wide = -(-max(3 * lanes, seq_extent * max(conv_own, own_rows, gate_own)) // lanes) * lanes
+    slab = [
+        padded(
+            lax.dynamic_slice(
+                dsmall, (at, group * seq_extent * count), (rows, seq_extent * count)
+            ),
+            rows,
+            slab_wide,
+        )
+        for at, rows, count in (
+            (0, tap_rows, conv_own),
+            (tap_rows, 1, own_rows),
+            (tap_rows + 1, 1, gate_own),
+        )
+    ]
+    dsmall = jnp.concatenate(slab + [dsmall[tap_rows + 2 :, :slab_wide]])
     sums = [dsmall]
     for distance in range(1, seq_extent):
         route = [(i, (i + distance) % seq_extent) for i in range(seq_extent)]

time: 313 us -> 294 us (0.939)
  waiting for transfers between devices: 66.6 us -> 56.4 us
  starting transfers between devices: 68.7 us -> 64.2 us
    all_to_all x2, waiting for transfers between devices: 0.01 us -> 12.3 us  [to_pieces(): lax.all_to_all(block, 'seq', 0, 0, axis_index_groups=seq_groups(size), ti...]
    ppermute x3, waiting for transfers between devices: 9.35 us -> 0.01 us  [local(): sums.append(lax.ppermute(dsmall, 'seq', route))]
    ppermute x32, waiting for transfers between devices: 50.4 us -> 42.6 us  [swap(): return lax.ppermute(block, axis, [(i, i ^ 1 << bit) for i in devices])]
    another operation x20, other arithmetic: 10.6 us -> 6.41 us  [gather_bit(): return jnp.stack([low, high], axis=at)]
    pallas_call x4 -> x3, Pallas kernels: 49.7 us -> 46.5 us  [mixer_backward(): pl.pallas_call(partial(mixer_backward_kernel, heads=heads, inner=inner, t...]
    unnamed x77 -> x75, local copies, waits for them, and re-layouts: 7.01 us -> 8.09 us
  transfers between devices with their start and end apart: 45 -> 45, of which waited for: 19 -> 16; matrix products, arithmetic and copies ran while one was open for 10% -> 11% of each run, Pallas kernels for 25% -> 31%
where the time goes in v4:
time: 294 us; the launch traced here: 289 us
  Pallas kernels  118 us (40%)
  starting transfers between devices  64.2 us (22%)
  waiting for transfers between devices  56.4 us (19%)
  other arithmetic  34.3 us (12%)
  local copies, waits for them, and re-layouts  13.7 us (5%)
    pallas_call x3, Pallas kernels, mixer_backward(): pl.pallas_call(partial(mixer_backward_kernel, heads=heads, inner=inner, t...  46.5 us
    ppermute x32, waiting for transfers between devices, swap(): return lax.ppermute(block, axis, [(i, i ^ 1 << bit) for i in devices])  42.6 us
    ppermute x32, starting transfers between devices, swap(): return lax.ppermute(block, axis, [(i, i ^ 1 << bit) for i in devices])  29.4 us
    pallas_call x1, Pallas kernels, gate_step(): pl.pallas_call(partial(gate_kernel, gain_row=taps + 2), grid=(part, size)...  25.5 us
    pallas_call x1, Pallas kernels, mixer_forward(): pl.pallas_call(partial(mixer_forward_kernel, heads=heads, inner=inner, ta...  24.4 us
    pallas_call x1, Pallas kernels, input_grad(): pl.pallas_call(partial(input_grad_kernel, gain_row=taps + 1), grid=(part,...  17.8 us
    all_to_all x2, waiting for transfers between devices, to_pieces(): lax.all_to_all(block, 'seq', 0, 0, axis_index_groups=seq_groups(size), ti...  12.3 us
    all_to_all x2, starting transfers between devices, to_sequences(): lax.all_to_all(block, 'seq', 0, 0, axis_index_groups=seq_groups(size), ti...  10.4 us
  transfers between devices with their start and end apart: 45, of which 16 were waited for; matrix products, arithmetic and copies ran while one was open for 11% of the time, Pallas kernels for 31%

profile of v4, /device:TPU:0, one launch (start us, length us, event | category | flops | bytes accessed | tf_op | source)
XLA Modules:
  0.0 289.0 jit_solution(9251206706035611676)
XLA Ops:
  4.8 4.1 %collective-permute-start = (bf16[24,5120]{1,0:T(8,128)(2,1)S(1)}, bf16[24,5120]{1,0:T(8,128)(2,1)S(1)}, u32[]{:S(2)}, u32[]{:S(2)}) collective-permute-start(bf16[24,5120]{1,0:T(8,128)(2,1)S(1)} %fusion.11), channel_id=1, source_target_pairs={{0,2},{1,3},{2,0},{3,1},{4,6},{5,7},{6,4},{7,5},{8,10},{9,11},{10,... | collective-permute-start | bytes 737288 | tf_op jit(solution)/shard_map/ppermute | solution.py:1033
  11.4 2.8 pad_maximum_fusion
  14.2 5.9 %collective-permute-done = bf16[24,5120]{1,0:T(8,128)(2,1)S(1)} collective-permute-done((bf16[24,5120]{1,0:T(8,128)(2,1)S(1)}, bf16[24,5120]{1,0:T(8,128)(2,1)S(1)}, u32[]{:S(2)}, u32[]{:S(2)}) %collective-permute-start) | collective-permute-done | bytes 245792 | tf_op jit(solution)/shard_map/ppermute | solution.py:1033
  21.0 4.6 %all-to-all-start = ((bf16[4,256,896]{2,1,0:T(8,128)(2,1)}), bf16[4,256,896]{2,1,0:T(8,128)(2,1)S(1)}, u32[]{:S(2)}, u32[]{:S(2)}) async-start(bf16[4,256,896]{2,1,0:T(8,128)(2,1)} %pad_maximum_fusion), calls=%async_computation | async-start | bytes 3670016 | tf_op jit(solution)/shard_map/all_to_all | solution.py:1127
  25.7 8.8 %collective-permute-done.1 = bf16[2,24,5120]{2,1,0:T(8,128)(2,1)S(1)} collective-permute-done((bf16[2,24,5120]{2,1,0:T(8,128)(2,1)S(1)}, bf16[2,24,5120]{2,1,0:T(8,128)(2,1)S(1)}, u32[]{:S(2)}, u32[]{:S(2)}) %collective-permute-start.1) | collective-permute-done | bytes 491552 | tf_op jit(solution)/shard_map/ppermute | solution.py:1033
  35.8 1.6 collective-permute-start.8
  37.5 1.9 collective-permute-start.5
  39.8 2.1 collective-permute-start.9
  46.0 8.6 %collective-permute-done.2 = bf16[4,24,1024]{2,1,0:T(8,128)(2,1)S(1)} collective-permute-done((bf16[4,24,1024]{2,1,0:T(8,128)(2,1)S(1)}, bf16[4,24,1024]{2,1,0:T(8,128)(2,1)S(1)}, u32[]{:S(2)}, u32[]{:S(2)}) %collective-permute-start.2) | collective-permute-done | bytes 196640 | tf_op jit(solution)/shard_map/ppermute | solution.py:1033
  58.6 4.0 %collective-permute-done.3 = bf16[2,4,24,1024]{3,2,1,0:T(8,128)(2,1)S(1)} collective-permute-done((bf16[2,4,24,1024]{3,2,1,0:T(8,128)(2,1)S(1)}, bf16[2,4,24,1024]{3,2,1,0:T(8,128)(2,1)S(1)}, u32[]{:S(2)}, u32[]{:S(2)}) %collective-permute-start.3) | collective-permute-done | bytes 393248 | tf_op jit(solution)/shard_map/ppermute | solution.py:1033
  69.7 5.8 %all-to-all-start.1 = ((bf16[4,256,640]{2,1,0:T(8,128)(2,1)}), bf16[4,256,640]{2,1,0:T(8,128)(2,1)S(1)}, u32[]{:S(2)}, u32[]{:S(2)}) async-start(bf16[4,256,640]{2,1,0:T(8,128)(2,1)} %slice.96), calls=%async_computation.1 | async-start | bytes 2621440 | tf_op jit(solution)/shard_map/all_to_all | solution.py:1127
  76.1 24.4 %shard_map.390 = (bf16[1024,768]{1,0:T(8,128)(2,1)}, f32[56,264,128]{2,1,0:T(8,128)}, f32[1024,128]{1,0:T(8,128)}, f32[1024,128]{1,0:T(8,128)}, f32[1024,1536]{1...) custom-call(s32[1]{0:T(128)} %bitcast.core_ref.edge_ref.start_ref.before_ref.next_ref._, ...), custom_call_target="tpu_custom_call" | custom-call | flops 1 | bytes 1 | tf_op jit(solution)/shard_map/pallas_call | solution.py:786
  108.5 25.5 %shard_map.391 = (bf16[1024,768]{1,0:T(8,128)(2,1)}, bf16[1024,1536]{1,0:T(8,128)(2,1)}, bf16[1024,1536]{1,0:T(8,128)(2,1)}, f32[8,1536]{1,0:T(8,128)}, bf16[4,1...) custom-call(s32[1]{0:T(128)} %bitcast.core_ref.edge_ref.start_ref.before_r, ...), custom_call_target="tpu_custom_call" | custom-call | flops 1 | bytes 1 | tf_op jit(solution)/shard_map/pallas_call | solution.py:851
  134.6 12.1 %shard_map.392 = (bf16[1024,1920]{1,0:T(8,128)(2,1)}, f32[8,1792]{1,0:T(8,128)}, f32[128,1536]{1,0:T(8,128)}, f32[14,8,128]{2,1,0:T(8,128)}) custom-call(f32[56,264,128]{2,1,0:T(8,128)} %get-tuple-element.116.ext_ref, f32[1024,128]{1,0:T(8,128)} %get-tuple-element.117.dtr_ref, f32[1024,128]{1,0:T(8,128)} %get-tuple-element.118.cum_ref, ...), custom_call_target="tpu_custom_call" | custom-call | flops 1 | bytes 1 | tf_op jit(solution)/shard_map/pallas_call | solution.py:910
  147.7 2.6 fusion.4
  153.3 5.5 %all-to-all-start.2 = ((bf16[4,256,768]{2,1,0:T(8,128)(2,1)}), bf16[4,256,768]{2,1,0:T(8,128)(2,1)S(1)}, u32[]{:S(2)}, u32[]{:S(2)}) async-start(bf16[4,256,768]{2,1,0:T(8,128)(2,1)} %bitcast.204), calls=%async_computation.2 | async-start | bytes 3145728 | tf_op jit(solution)/shard_map/all_to_all | solution.py:1143
  158.9 12.5 %shard_map.393 = (bf16[1024,1920]{1,0:T(8,128)(2,1)}, f32[8,1792]{1,0:T(8,128)}, f32[128,1536]{1,0:T(8,128)}, f32[14,8,128]{2,1,0:T(8,128)}) custom-call(f32[56,264,128]{2,1,0:T(8,128)} %get-tuple-element.116.ext_ref, f32[1024,128]{1,0:T(8,128)} %get-tuple-element.117.dtr_ref, ...), custom_call_target="tpu_custom_call", output_to_operand_aliasing={{0}: (14, {})} | custom-call | flops 1 | bytes 1 | tf_op jit(solution)/shard_map/pallas_call | solution.py:910
  177.1 21.9 %shard_map.394 = (bf16[1024,1920]{1,0:T(8,128)(2,1)}, f32[8,1792]{1,0:T(8,128)}, f32[128,1536]{1,0:T(8,128)}, f32[14,8,128]{2,1,0:T(8,128)}) custom-call(f32[56,264,128]{2,1,0:T(8,128)} %get-tuple-element.116.ext_ref, f32[1024,128]{1,0:T(8,128)} %get-tuple-element.117.dtr_ref, ...), custom_call_target="tpu_custom_call", output_to_operand_aliasing={{0}: (14, {})} | custom-call | flops 1 | bytes 1 | tf_op jit(solution)/shard_map/pallas_call | solution.py:910
  200.6 2.1 collective-permute-start.23
  202.7 2.4 collective-permute-start.24
  207.2 17.8 %shard_map.395 = (bf16[1024,768]{1,0:T(8,128)(2,1)}, f32[8,1792]{1,0:T(8,128)}, bf16[4,96,1024]{2,1,0:T(8,128)(2,1)}, f32[4,96,1024]{2,1,0:T(8,128)}, bf16[4,96,...) custom-call(s32[1]{0:T(128)} %bitcast.core_ref.edge_ref.start_ref.before_ref.next_ref._, bf16[1024,896]{1,0:T(8,128)(2,1)} %bitcast.179, ...), custom_call_target="tpu_custom_call" | custom-call | flops 1 | bytes 1 | tf_op jit(solution)/shard_map/pallas_call | solution.py:967
  225.9 4.5 %all-to-all-start.3 = ((bf16[4,256,768]{2,1,0:T(8,128)(2,1)}), bf16[4,256,768]{2,1,0:T(8,128)(2,1)}, u32[]{:S(2)}, u32[]{:S(2)}) async-start(bf16[4,256,768]{2,1,0:T(8,128)(2,1)} %bitcast.205), calls=%async_computation.3 | async-start | bytes 3145728 | tf_op jit(solution)/shard_map/all_to_all | solution.py:1143
  238.9 4.1 %collective-permute-done.36 = bf16[2,4,24,896]{3,2,1,0:T(8,128)(2,1)} collective-permute-done((bf16[2,4,24,896]{3,2,1,0:T(8,128)(2,1)S(1)}, bf16[2,4,24,896]{3,2,1,0:T(8,128)(2,1)}, u32[]{:S(2)}, u32[]{:S(2)}) %collective-permute-start.36) | collective-permute-done | bytes 344096 | tf_op jit(solution)/shard_map/ppermute | solution.py:1033
  245.4 2.4 collective-permute-done.33
  249.0 2.0 collective-permute-start.34
  251.1 3.7 %collective-permute-done.34 = bf16[4,24,1024]{2,1,0:T(8,128)(2,1)S(1)} collective-permute-done((bf16[4,24,1024]{2,1,0:T(8,128)(2,1)S(1)}, bf16[4,24,1024]{2,1,0:T(8,128)(2,1)S(1)}, u32[]{:S(2)}, u32[]{:S(2)}) %collective-permute-start.34) | collective-permute-done | bytes 196640 | tf_op jit(solution)/shard_map/ppermute | solution.py:1033
  255.5 12.3 %all-to-all-done.3 = bf16[4,256,768]{2,1,0:T(8,128)(2,1)} async-done(((bf16[4,256,768]{2,1,0:T(8,128)(2,1)}), bf16[4,256,768]{2,1,0:T(8,128)(2,1)}, u32[]{:S(2)}, u32[]{:S(2)}) %all-to-all-start.3) | async-done | bytes 1572896 | tf_op jit(solution)/shard_map/all_to_all | solution.py:1143
  269.9 2.0 collective-permute-start.39
  271.9 1.8 collective-permute-start.40
  277.4 2.5 collective-permute-start.31
  279.9 3.4 %convert_add_fusion = f32[4,256,768]{2,1,0:T(8,128)} fusion(bf16[4,256,768]{2,1,0:T(8,128)(2,1)} %all-to-all-done.3, bf16[4,256,768]{2,1,0:T(8,128)(2,1)S(1)} %copy-done.5), kind=kLoop, calls=%fused_computation | loop fusion | flops 2359296 | bytes 6291456 | tf_op jit(solution)/shard_map/add | solution.py:1371
  283.9 3.6 %shard_map.396 = (f32[1,24]{1,0:T(1,128)}, f32[1,24]{1,0:T(1,128)}, f32[1,24]{1,0:T(1,128)}, f32[24,3352]{1,0:T(8,128)}, f32[24,3352]{1,0:T(8,128)}, /*index=5*/...) custom-call(f32[8]{0:T(128)} %pad_maximum_fusion.16.rates_ref, ...), custom_call_target="tpu_custom_call" | custom-call | flops 1 | bytes 1 | tf_op jit(solution)/shard_map/pallas_call | solution.py:1012
  (231 shorter events, 67.2 us)
Async XLA Ops:
  4.8 15.3 %collective-permute-start = (bf16[24,5120]{1,0:T(8,128)(2,1)S(1)}, bf16[24,5120]{1,0:T(8,128)(2,1)S(1)}, u32[]{:S(2)}, u32[]{:S(2)}) collective-permute-start(bf16[24,5120]{1,0:T(8,128)(2,1)S(1)} %fusion.11), channel_id=1, source_target_pairs={{0,2},{1,3},{2,0},{3,1},{4,6},{5,7},{6,4},{7,5},{8,10},{9,11},{10,... | collective-permute-start | bytes 737288 | tf_op jit(solution)/shard_map/ppermute | solution.py:1033
  20.3 14.2 %collective-permute-start.1 = (bf16[2,24,5120]{2,1,0:T(8,128)(2,1)S(1)}, bf16[2,24,5120]{2,1,0:T(8,128)(2,1)S(1)}, u32[]{:S(2)}, u32[]{:S(2)}) collective-permute-start(bf16[2,24,5120]{2,1,0:T(8,128)(2,1)S(1)} %pad_maximum_fusion.9), channel_id=1, source_target_pairs={{0,1},{1,0},{2,3},{3,2},{4,5},{5,4},{6,7},{7,6},{8,9},{9,8},{10,11... | collective-permute-start | bytes 1474568 | tf_op jit(solution)/shard_map/ppermute | solution.py:1033
  21.0 47.2 %all-to-all-start = ((bf16[4,256,896]{2,1,0:T(8,128)(2,1)}), bf16[4,256,896]{2,1,0:T(8,128)(2,1)S(1)}, u32[]{:S(2)}, u32[]{:S(2)}) async-start(bf16[4,256,896]{2,1,0:T(8,128)(2,1)} %pad_maximum_fusion), calls=%async_computation | async-start | bytes 3670016 | tf_op jit(solution)/shard_map/all_to_all | solution.py:1127
  37.5 7.8 %collective-permute-start.5 = (bf16[4,24,896]{2,1,0:T(8,128)(2,1)S(1)}, bf16[4,24,896]{2,1,0:T(8,128)(2,1)S(1)}, u32[]{:S(2)}, u32[]{:S(2)}) collective-permute-start(bf16[4,24,896]{2,1,0:T(8,128)(2,1)S(1)} %slice.122), channel_id=1, source_target_pairs={{0,8},{4,12},{8,0},{12,4},{16,24},{20,28},{24,16},{28,20},{1,9},{5... | collective-permute-start | bytes 516104 | tf_op jit(solution)/shard_map/ppermute | solution.py:1033
  42.0 14.1 %collective-permute-start.12 = (bf16[4,48,768]{2,1,0:T(8,128)(2,1)S(1)}, bf16[4,48,768]{2,1,0:T(8,128)(2,1)S(1)}, u32[]{:S(2)}, u32[]{:S(2)}) collective-permute-start(bf16[4,48,768]{2,1,0:T(8,128)(2,1)S(1)} %bitcast.210), channel_id=1, source_target_pairs={{0,8},{4,12},{8,0},{12,4},{16,24},{20,28},{24,16},{28,20},{1,9},{5... | collective-permute-start | bytes 884744 | tf_op jit(solution)/shard_map/ppermute | solution.py:1033
  42.1 20.8 %collective-permute-start.11 = (bf16[4,24,1536]{2,1,0:T(8,128)(2,1)S(1)}, bf16[4,24,1536]{2,1,0:T(8,128)(2,1)S(1)}, u32[]{:S(2)}, u32[]{:S(2)}) collective-permute-start(bf16[4,24,1536]{2,1,0:T(8,128)(2,1)S(1)} %slice.135), channel_id=1, source_target_pairs={{0,16},{4,20},{8,24},{12,28},{16,0},{20,4},{24,8},{28,12},{1,17},{... | collective-permute-start | bytes 884744 | tf_op jit(solution)/shard_map/ppermute | solution.py:1033
  43.7 10.9 %collective-permute-start.2 = (bf16[4,24,1024]{2,1,0:T(8,128)(2,1)S(1)}, bf16[4,24,1024]{2,1,0:T(8,128)(2,1)S(1)}, u32[]{:S(2)}, u32[]{:S(2)}) collective-permute-start(bf16[4,24,1024]{2,1,0:T(8,128)(2,1)S(1)} %slice.121), channel_id=1, source_target_pairs={{0,16},{4,20},{8,24},{12,28},{16,0},{20,4},{24,8},{28,12},{1,17},{... | collective-permute-start | bytes 589832 | tf_op jit(solution)/shard_map/ppermute | solution.py:1033
  45.4 12.9 %collective-permute-start.6 = (bf16[2,4,24,896]{3,2,1,0:T(8,128)(2,1)S(1)}, bf16[2,4,24,896]{3,2,1,0:T(8,128)(2,1)S(1)}, u32[]{:S(2)}, u32[]{:S(2)}) collective-permute-start(bf16[2,4,24,896]{3,2,1,0:T(8,128)(2,1)S(1)} %pad_maximum_fusion.11), channel_id=1, source_target_pairs={{0,16},{4,20},{8,24},{12,28},{16,0},{20,4},{24,8},{28,12},{1,17},{... | collective-permute-start | bytes 1032200 | tf_op jit(solution)/shard_map/ppermute | solution.py:1033
  54.7 7.8 %collective-permute-start.3 = (bf16[2,4,24,1024]{3,2,1,0:T(8,128)(2,1)S(1)}, bf16[2,4,24,1024]{3,2,1,0:T(8,128)(2,1)S(1)}, u32[]{:S(2)}, u32[]{:S(2)}) collective-permute-start(bf16[2,4,24,1024]{3,2,1,0:T(8,128)(2,1)S(1)} %pad_maximum_fusion.10), channel_id=1, source_target_pairs={{0,8},{4,12},{8,0},{12,4},{16,24},{20,28},{24,16},{28,20},{1,9},{5... | collective-permute-start | bytes 1179656 | tf_op jit(solution)/shard_map/ppermute | solution.py:1033
  58.5 7.8 %collective-permute-start.7 = (bf16[4,96,896]{2,1,0:T(8,128)(2,1)S(1)}, bf16[4,96,896]{2,1,0:T(8,128)(2,1)S(1)}, u32[]{:S(2)}, u32[]{:S(2)}) collective-permute-start(bf16[4,96,896]{2,1,0:T(8,128)(2,1)S(1)} %bitcast.196), channel_id=1, source_target_pairs={{0,4},{4,0},{8,12},{12,8},{16,20},{20,16},{24,28},{28,24},{1,5},{5... | collective-permute-start | bytes 2064392 | tf_op jit(solution)/shard_map/ppermute | solution.py:1033
  64.9 35.6 %collective-permute-start.15 = (bf16[2,4,48,768]{3,2,1,0:T(8,128)(2,1)}, bf16[2,4,48,768]{3,2,1,0:T(8,128)(2,1)}, u32[]{:S(2)}, u32[]{:S(2)}) collective-permute-start(bf16[2,4,48,768]{3,2,1,0:T(8,128)(2,1)} %pad_maximum_fusion.8), channel_id=1, source_target_pairs={{0,16},{4,20},{8,24},{12,28},{16,0},{20,4},{24,8},{28,12},{1,17},{... | collective-permute-start | bytes 1769480 | tf_op jit(solution)/shard_map/ppermute | solution.py:1033
  68.2 33.9 %collective-permute-start.13 = (bf16[2,4,24,1536]{3,2,1,0:T(8,128)(2,1)}, bf16[2,4,24,1536]{3,2,1,0:T(8,128)(2,1)}, u32[]{:S(2)}, u32[]{:S(2)}) collective-permute-start(bf16[2,4,24,1536]{3,2,1,0:T(8,128)(2,1)} %pad_maximum_fusion.7), channel_id=1, source_target_pairs={{0,8},{4,12},{8,0},{12,4},{16,24},{20,28},{24,16},{28,20},{1,9},{5... | collective-permute-start | bytes 1769480 | tf_op jit(solution)/shard_map/ppermute | solution.py:1033
  69.7 37.7 %all-to-all-start.1 = ((bf16[4,256,640]{2,1,0:T(8,128)(2,1)}), bf16[4,256,640]{2,1,0:T(8,128)(2,1)S(1)}, u32[]{:S(2)}, u32[]{:S(2)}) async-start(bf16[4,256,640]{2,1,0:T(8,128)(2,1)} %slice.96), calls=%async_computation.1 | async-start | bytes 2621440 | tf_op jit(solution)/shard_map/all_to_all | solution.py:1127
  134.0 12.7 %collective-permute-start.17 = (bf16[4,192,768]{2,1,0:T(8,128)(2,1)}, bf16[4,192,768]{2,1,0:T(8,128)(2,1)S(1)}, u32[]{:S(2)}, u32[]{:S(2)}) collective-permute-start(bf16[4,192,768]{2,1,0:T(8,128)(2,1)} %get-tuple-element.124), channel_id=1, source_target_pairs={{0,4},{4,0},{8,12},{12,8},{16,20},{20,16},{24,28},{28,24},{1,5},{5... | collective-permute-start | bytes 3538952 | tf_op jit(solution)/shard_map/ppermute | solution.py:1033
  134.2 12.5 %collective-permute-start.18 = (bf16[4,96,1536]{2,1,0:T(8,128)(2,1)}, bf16[4,96,1536]{2,1,0:T(8,128)(2,1)S(1)}, u32[]{:S(2)}, u32[]{:S(2)}) collective-permute-start(bf16[4,96,1536]{2,1,0:T(8,128)(2,1)} %get-tuple-element.126), channel_id=1, source_target_pairs={{0,4},{4,0},{8,12},{12,8},{16,20},{20,16},{24,28},{28,24},{1,5},{5... | collective-permute-start | bytes 3538952 | tf_op jit(solution)/shard_map/ppermute | solution.py:1033
  150.2 21.2 %collective-permute-start.20 = (bf16[2,4,24,1536]{3,2,1,0:T(8,128)(2,1)}, bf16[2,4,24,1536]{3,2,1,0:T(8,128)(2,1)S(1)}, u32[]{:S(2)}, u32[]{:S(2)}) collective-permute-start(bf16[2,4,24,1536]{3,2,1,0:T(8,128)(2,1)} %get-tuple-element.188), channel_id=1, source_target_pairs={{0,16},{4,20},{8,24},{12,28},{16,0},{20,4},{24,8},{28,12},{1,17},{... | collective-permute-start | bytes 1769480 | tf_op jit(solution)/shard_map/ppermute | solution.py:1033
  152.2 19.2 %collective-permute-start.19 = (bf16[2,4,48,768]{3,2,1,0:T(8,128)(2,1)}, bf16[2,4,48,768]{3,2,1,0:T(8,128)(2,1)}, u32[]{:S(2)}, u32[]{:S(2)}) collective-permute-start(bf16[2,4,48,768]{3,2,1,0:T(8,128)(2,1)} %get-tuple-element.190), channel_id=1, source_target_pairs={{0,8},{4,12},{8,0},{12,4},{16,24},{20,28},{24,16},{28,20},{1,9},{5... | collective-permute-start | bytes 1769480 | tf_op jit(solution)/shard_map/ppermute | solution.py:1033
  153.3 53.9 %all-to-all-start.2 = ((bf16[4,256,768]{2,1,0:T(8,128)(2,1)}), bf16[4,256,768]{2,1,0:T(8,128)(2,1)S(1)}, u32[]{:S(2)}, u32[]{:S(2)}) async-start(bf16[4,256,768]{2,1,0:T(8,128)(2,1)} %bitcast.204), calls=%async_computation.2 | async-start | bytes 3145728 | tf_op jit(solution)/shard_map/all_to_all | solution.py:1143
  173.5 25.5 %collective-permute-start.21 = (bf16[4,48,768]{2,1,0:T(8,128)(2,1)}, bf16[4,48,768]{2,1,0:T(8,128)(2,1)}, u32[]{:S(2)}, u32[]{:S(2)}) collective-permute-start(bf16[4,48,768]{2,1,0:T(8,128)(2,1)} %fusion.9), channel_id=1, source_target_pairs={{0,16},{4,20},{8,24},{12,28},{16,0},{20,4},{24,8},{28,12},{1,17},{... | collective-permute-start | bytes 884744 | tf_op jit(solution)/shard_map/ppermute | solution.py:1033
  176.2 24.0 %collective-permute-start.22 = (bf16[4,24,1536]{2,1,0:T(8,128)(2,1)S(1)}, bf16[4,24,1536]{2,1,0:T(8,128)(2,1)S(1)}, u32[]{:S(2)}, u32[]{:S(2)}) collective-permute-start(bf16[4,24,1536]{2,1,0:T(8,128)(2,1)S(1)} %fusion.10), channel_id=1, source_target_pairs={{0,8},{4,12},{8,0},{12,4},{16,24},{20,28},{24,16},{28,20},{1,9},{5... | collective-permute-start | bytes 884744 | tf_op jit(solution)/shard_map/ppermute | solution.py:1033
  200.6 24.5 %collective-permute-start.23 = (bf16[24,3072]{1,0:T(8,128)(2,1)S(1)}, bf16[24,3072]{1,0:T(8,128)(2,1)S(1)}, u32[]{:S(2)}, u32[]{:S(2)}) collective-permute-start(bf16[24,3072]{1,0:T(8,128)(2,1)S(1)} %get-tuple-element.196), channel_id=1, source_target_pairs={{0,1},{1,2},{2,3},{3,0},{4,5},{5,6},{6,7},{7,4},{8,9},{9,10},{10,1... | collective-permute-start | bytes 442376 | tf_op jit(solution)/shard_map/ppermute | solution.py:1108
  202.7 22.4 %collective-permute-start.24 = (bf16[24,3072]{1,0:T(8,128)(2,1)S(1)}, bf16[24,3072]{1,0:T(8,128)(2,1)S(1)}, u32[]{:S(2)}, u32[]{:S(2)}) collective-permute-start(bf16[24,3072]{1,0:T(8,128)(2,1)S(1)} %get-tuple-element.195), channel_id=1, source_target_pairs={{0,2},{1,3},{2,0},{3,1},{4,6},{5,7},{6,4},{7,5},{8,10},{9,11},{10,... | collective-permute-start | bytes 442376 | tf_op jit(solution)/shard_map/ppermute | solution.py:1108
  205.1 20.1 %collective-permute-start.25 = (bf16[24,3072]{1,0:T(8,128)(2,1)S(1)}, bf16[24,3072]{1,0:T(8,128)(2,1)S(1)}, u32[]{:S(2)}, u32[]{:S(2)}) collective-permute-start(bf16[24,3072]{1,0:T(8,128)(2,1)S(1)} %get-tuple-element.194), channel_id=1, source_target_pairs={{0,3},{1,0},{2,1},{3,2},{4,7},{5,4},{6,5},{7,6},{8,11},{9,8},{10,9... | collective-permute-start | bytes 442376 | tf_op jit(solution)/shard_map/ppermute | solution.py:1108
  225.2 9.9 %collective-permute-start.32 = (bf16[4,96,1024]{2,1,0:T(8,128)(2,1)}, bf16[4,96,1024]{2,1,0:T(8,128)(2,1)}, u32[]{:S(2)}, u32[]{:S(2)}) collective-permute-start(bf16[4,96,1024]{2,1,0:T(8,128)(2,1)} %get-tuple-element.165), channel_id=1, source_target_pairs={{0,4},{4,0},{8,12},{12,8},{16,20},{20,16},{24,28},{28,24},{1,5},{5... | collective-permute-start | bytes 2359304 | tf_op jit(solution)/shard_map/ppermute | solution.py:1033
  225.9 41.9 %all-to-all-start.3 = ((bf16[4,256,768]{2,1,0:T(8,128)(2,1)}), bf16[4,256,768]{2,1,0:T(8,128)(2,1)}, u32[]{:S(2)}, u32[]{:S(2)}) async-start(bf16[4,256,768]{2,1,0:T(8,128)(2,1)} %bitcast.205), calls=%async_computation.3 | async-start | bytes 3145728 | tf_op jit(solution)/shard_map/all_to_all | solution.py:1143
  232.4 10.6 %collective-permute-start.36 = (bf16[2,4,24,896]{3,2,1,0:T(8,128)(2,1)S(1)}, bf16[2,4,24,896]{3,2,1,0:T(8,128)(2,1)}, u32[]{:S(2)}, u32[]{:S(2)}) collective-permute-start(bf16[2,4,24,896]{3,2,1,0:T(8,128)(2,1)S(1)} %fusion.8), channel_id=1, source_target_pairs={{0,16},{4,20},{8,24},{12,28},{16,0},{20,4},{24,8},{28,12},{1,17},{... | collective-permute-start | bytes 1032200 | tf_op jit(solution)/shard_map/ppermute | solution.py:1033
  236.2 11.6 %collective-permute-start.33 = (bf16[2,4,24,1024]{3,2,1,0:T(8,128)(2,1)S(1)}, bf16[2,4,24,1024]{3,2,1,0:T(8,128)(2,1)S(1)}, u32[]{:S(2)}, u32[]{:S(2)}) collective-permute-start(bf16[2,4,24,1024]{3,2,1,0:T(8,128)(2,1)S(1)} %fusion.7), channel_id=1, source_target_pairs={{0,8},{4,12},{8,0},{12,4},{16,24},{20,28},{24,16},{28,20},{1,9},{5... | collective-permute-start | bytes 1179656 | tf_op jit(solution)/shard_map/ppermute | solution.py:1033
  269.9 7.4 %collective-permute-start.38 = (bf16[24,1920]{1,0:T(8,128)(2,1)}, bf16[24,1920]{1,0:T(8,128)(2,1)S(1)}, u32[]{:S(2)}, u32[]{:S(2)}) collective-permute-start(bf16[24,1920]{1,0:T(8,128)(2,1)} %get-tuple-element.224), channel_id=1, source_target_pairs={{0,1},{1,2},{2,3},{3,0},{4,5},{5,6},{6,7},{7,4},{8,9},{9,10},{10,1... | collective-permute-start | bytes 276488 | tf_op jit(solution)/shard_map/ppermute | solution.py:1108
  269.9 13.3 %collective-permute-start.39 = (bf16[24,1920]{1,0:T(8,128)(2,1)}, bf16[24,1920]{1,0:T(8,128)(2,1)S(1)}, u32[]{:S(2)}, u32[]{:S(2)}) collective-permute-start(bf16[24,1920]{1,0:T(8,128)(2,1)} %get-tuple-element.225), channel_id=1, source_target_pairs={{0,2},{1,3},{2,0},{3,1},{4,6},{5,7},{6,4},{7,5},{8,10},{9,11},{10,... | collective-permute-start | bytes 276488 | tf_op jit(solution)/shard_map/ppermute | solution.py:1108
  271.9 11.3 %collective-permute-start.40 = (bf16[24,1920]{1,0:T(8,128)(2,1)}, bf16[24,1920]{1,0:T(8,128)(2,1)S(1)}, u32[]{:S(2)}, u32[]{:S(2)}) collective-permute-start(bf16[24,1920]{1,0:T(8,128)(2,1)} %get-tuple-element.223), channel_id=1, source_target_pairs={{0,3},{1,0},{2,1},{3,2},{4,7},{5,4},{6,5},{7,6},{8,11},{9,8},{10,9... | collective-permute-start | bytes 276488 | tf_op jit(solution)/shard_map/ppermute | solution.py:1108
  274.8 8.4 %collective-permute-start.29 = (f32[8,384]{1,0:T(8,128)S(1)}, f32[8,384]{1,0:T(8,128)S(1)}, u32[]{:S(2)}, u32[]{:S(2)}) collective-permute-start(f32[8,384]{1,0:T(8,128)S(1)} %fusion.30.refs_0_), channel_id=1, source_target_pairs={{0,1},{1,2},{2,3},{3,0},{4,5},{5,6},{6,7},{7,4},{8,9},{9,10},{10,1... | collective-permute-start | bytes 36872 | tf_op jit(solution)/shard_map/ppermute | solution.py:1394
  275.5 7.8 %collective-permute-start.30 = (f32[8,384]{1,0:T(8,128)S(1)}, f32[8,384]{1,0:T(8,128)S(1)}, u32[]{:S(2)}, u32[]{:S(2)}) collective-permute-start(f32[8,384]{1,0:T(8,128)S(1)} %fusion.30.refs_0_), channel_id=1, source_target_pairs={{0,2},{1,3},{2,0},{3,1},{4,6},{5,7},{6,4},{7,5},{8,10},{9,11},{10,... | collective-permute-start | bytes 36872 | tf_op jit(solution)/shard_map/ppermute | solution.py:1394
  (51 other events, 260.6 us)

commit v5 on v4

--- a/solution.py
+++ b/solution.py
@@ -1098,12 +1098,14 @@
     return give_half(block, "dp", bit, sum(1 for b in order[: len(order) - 1 - step] if b > bit))
 
 
-def scatter_seq(block):
+def scatter_seq(block, *others):
     extent = lax.axis_size("seq")
     place = lax.axis_index("seq")
     arrivals = [pick(block, place, 0)]
     for distance in range(1, extent):
         sent = pick(block, lax.rem(place + distance, extent), 0).astype(bf16)
+        if others and distance == extent - 1:
+            sent = after(sent, *others)
         route = [(i, (i + distance) % extent) for i in range(extent)]
         arrivals.append(lax.ppermute(sent, "seq", route))
     return arrivals
@@ -1362,6 +1364,7 @@
     g_b = core_sums(*handed[2:])
     g_a = core_and_next(*g_a, order_a)
     g_b = core_and_next(*g_b, order_b)
+    dsmall = after(dsmall, g_a[0], g_b[0])
     g_a = g_a[0] + g_a[1].astype(f32)
     g_b = g_b[0] + g_b[1].astype(f32)
     for step in range(2, last + 1):
@@ -1369,9 +1372,8 @@
         g_b = scatter_dp_bit(g_b, order_b, step)
     pieces = to_pieces(dx, part, size, piece)
     in_grad = out_grad.astype(f32) + pieces.astype(f32)
-    g_front = scatter_seq(jnp.concatenate([g_a, g_b], axis=2))
-    dsmall = sum_bits(dsmall, "dp", order_a[:0:-1])
-    dsmall = sum_bits(after(dsmall, pieces), "dp", order_a[:1])
+    g_front = scatter_seq(jnp.concatenate([g_a, g_b], axis=2), pieces)
+    dsmall = sum_bits(dsmall, "dp", order_a[::-1])
     slab_wide = -(-max(3 * lanes, seq_extent * max(conv_own, own_rows, gate_own)) // lanes) * lanes
     slab = [
         padded(

time: 294 us -> 287 us (0.976)
  waiting for transfers between devices: 56.4 us -> 51.4 us
    all_to_all x2, waiting for transfers between devices: 12.3 us -> 5.15 us  [to_pieces(): lax.all_to_all(block, 'seq', 0, 0, axis_index_groups=seq_groups(size), ti...]
    unnamed x75 -> x65, local copies, waits for them, and re-layouts: 8.09 us -> 7.92 us
  transfers between devices with their start and end apart: 45 -> 45, of which waited for: 16 -> 18; matrix products, arithmetic and copies ran while one was open for 11% -> 11% of each run, Pallas kernels for 31% -> 31%
where the time goes in v5:
time: 287 us; the launch traced here: 283 us
  Pallas kernels  118 us (41%)
  starting transfers between devices  64.6 us (23%)
  waiting for transfers between devices  51.4 us (18%)
  other arithmetic  32.8 us (11%)
  local copies, waits for them, and re-layouts  13.5 us (5%)
    pallas_call x3, Pallas kernels, mixer_backward(): pl.pallas_call(partial(mixer_backward_kernel, heads=heads, inner=inner, t...  46.5 us
    ppermute x32, waiting for transfers between devices, swap(): return lax.ppermute(block, axis, [(i, i ^ 1 << bit) for i in devices])  43.9 us
    ppermute x32, starting transfers between devices, swap(): return lax.ppermute(block, axis, [(i, i ^ 1 << bit) for i in devices])  31.1 us
    pallas_call x1, Pallas kernels, gate_step(): pl.pallas_call(partial(gate_kernel, gain_row=taps + 2), grid=(part, size)...  25.5 us
    pallas_call x1, Pallas kernels, mixer_forward(): pl.pallas_call(partial(mixer_forward_kernel, heads=heads, inner=inner, ta...  24.4 us
    pallas_call x1, Pallas kernels, input_grad(): pl.pallas_call(partial(input_grad_kernel, gain_row=taps + 1), grid=(part,...  17.8 us
    all_to_all x2, starting transfers between devices, to_sequences(): lax.all_to_all(block, 'seq', 0, 0, axis_index_groups=seq_groups(size), ti...  10.4 us
    all_to_all x2, starting transfers between devices, to_pieces(): lax.all_to_all(block, 'seq', 0, 0, axis_index_groups=seq_groups(size), ti...  10 us
  transfers between devices with their start and end apart: 45, of which 18 were waited for; matrix products, arithmetic and copies ran while one was open for 11% of the time, Pallas kernels for 31%

profile of v5, /device:TPU:0, one launch (start us, length us, event | category | flops | bytes accessed | tf_op | source)
XLA Modules:
  0.0 282.5 jit_solution(11267541539660955232)
XLA Ops:
  4.8 4.1 %collective-permute-start = (bf16[24,5120]{1,0:T(8,128)(2,1)S(1)}, bf16[24,5120]{1,0:T(8,128)(2,1)S(1)}, u32[]{:S(2)}, u32[]{:S(2)}) collective-permute-start(bf16[24,5120]{1,0:T(8,128)(2,1)S(1)} %fusion.10), channel_id=1, source_target_pairs={{0,2},{1,3},{2,0},{3,1},{4,6},{5,7},{6,4},{7,5},{8,10},{9,11},{10,... | collective-permute-start | bytes 737288 | tf_op jit(solution)/shard_map/ppermute | solution.py:1033
  11.4 2.8 pad_maximum_fusion
  14.2 5.9 %collective-permute-done = bf16[24,5120]{1,0:T(8,128)(2,1)S(1)} collective-permute-done((bf16[24,5120]{1,0:T(8,128)(2,1)S(1)}, bf16[24,5120]{1,0:T(8,128)(2,1)S(1)}, u32[]{:S(2)}, u32[]{:S(2)}) %collective-permute-start) | collective-permute-done | bytes 245792 | tf_op jit(solution)/shard_map/ppermute | solution.py:1033
  21.0 4.6 %all-to-all-start = ((bf16[4,256,896]{2,1,0:T(8,128)(2,1)}), bf16[4,256,896]{2,1,0:T(8,128)(2,1)S(1)}, u32[]{:S(2)}, u32[]{:S(2)}) async-start(bf16[4,256,896]{2,1,0:T(8,128)(2,1)} %pad_maximum_fusion), calls=%async_computation | async-start | bytes 3670016 | tf_op jit(solution)/shard_map/all_to_all | solution.py:1129
  25.7 8.8 %collective-permute-done.1 = bf16[2,24,5120]{2,1,0:T(8,128)(2,1)S(1)} collective-permute-done((bf16[2,24,5120]{2,1,0:T(8,128)(2,1)S(1)}, bf16[2,24,5120]{2,1,0:T(8,128)(2,1)S(1)}, u32[]{:S(2)}, u32[]{:S(2)}) %collective-permute-start.1) | collective-permute-done | bytes 491552 | tf_op jit(solution)/shard_map/ppermute | solution.py:1033
  37.5 1.9 collective-permute-start.5
  39.8 2.1 collective-permute-start.9
  46.0 8.6 %collective-permute-done.2 = bf16[4,24,1024]{2,1,0:T(8,128)(2,1)S(1)} collective-permute-done((bf16[4,24,1024]{2,1,0:T(8,128)(2,1)S(1)}, bf16[4,24,1024]{2,1,0:T(8,128)(2,1)S(1)}, u32[]{:S(2)}, u32[]{:S(2)}) %collective-permute-start.2) | collective-permute-done | bytes 196640 | tf_op jit(solution)/shard_map/ppermute | solution.py:1033
  58.6 4.0 %collective-permute-done.3 = bf16[2,4,24,1024]{3,2,1,0:T(8,128)(2,1)S(1)} collective-permute-done((bf16[2,4,24,1024]{3,2,1,0:T(8,128)(2,1)S(1)}, bf16[2,4,24,1024]{3,2,1,0:T(8,128)(2,1)S(1)}, u32[]{:S(2)}, u32[]{:S(2)}) %collective-permute-start.3) | collective-permute-done | bytes 393248 | tf_op jit(solution)/shard_map/ppermute | solution.py:1033
  69.7 5.8 %all-to-all-start.1 = ((bf16[4,256,640]{2,1,0:T(8,128)(2,1)}), bf16[4,256,640]{2,1,0:T(8,128)(2,1)S(1)}, u32[]{:S(2)}, u32[]{:S(2)}) async-start(bf16[4,256,640]{2,1,0:T(8,128)(2,1)} %slice.96), calls=%async_computation.1 | async-start | bytes 2621440 | tf_op jit(solution)/shard_map/all_to_all | solution.py:1129
  76.1 24.4 %shard_map.390 = (bf16[1024,768]{1,0:T(8,128)(2,1)}, f32[56,264,128]{2,1,0:T(8,128)}, f32[1024,128]{1,0:T(8,128)}, f32[1024,128]{1,0:T(8,128)}, f32[1024,1536]{1...) custom-call(s32[1]{0:T(128)} %bitcast.core_ref.edge_ref.start_ref.before_ref.next_ref._, ...), custom_call_target="tpu_custom_call" | custom-call | flops 1 | bytes 1 | tf_op jit(solution)/shard_map/pallas_call | solution.py:786
  108.5 25.5 %shard_map.391 = (bf16[1024,768]{1,0:T(8,128)(2,1)}, bf16[1024,1536]{1,0:T(8,128)(2,1)}, bf16[1024,1536]{1,0:T(8,128)(2,1)}, f32[8,1536]{1,0:T(8,128)}, bf16[4,1...) custom-call(s32[1]{0:T(128)} %bitcast.core_ref.edge_ref.start_ref.before_r, ...), custom_call_target="tpu_custom_call" | custom-call | flops 1 | bytes 1 | tf_op jit(solution)/shard_map/pallas_call | solution.py:851
  134.6 12.1 %shard_map.392 = (bf16[1024,1920]{1,0:T(8,128)(2,1)}, f32[8,1792]{1,0:T(8,128)}, f32[128,1536]{1,0:T(8,128)}, f32[14,8,128]{2,1,0:T(8,128)}) custom-call(f32[56,264,128]{2,1,0:T(8,128)} %get-tuple-element.117.ext_ref, f32[1024,128]{1,0:T(8,128)} %get-tuple-element.118.dtr_ref, f32[1024,128]{1,0:T(8,128)} %get-tuple-element.119.cum_ref, ...), custom_call_target="tpu_custom_call" | custom-call | flops 1 | bytes 1 | tf_op jit(solution)/shard_map/pallas_call | solution.py:910
  147.7 2.6 fusion.3
  153.3 5.5 %all-to-all-start.2 = ((bf16[4,256,768]{2,1,0:T(8,128)(2,1)}), bf16[4,256,768]{2,1,0:T(8,128)(2,1)S(1)}, u32[]{:S(2)}, u32[]{:S(2)}) async-start(bf16[4,256,768]{2,1,0:T(8,128)(2,1)} %bitcast.204), calls=%async_computation.2 | async-start | bytes 3145728 | tf_op jit(solution)/shard_map/all_to_all | solution.py:1145
  158.9 12.6 %shard_map.393 = (bf16[1024,1920]{1,0:T(8,128)(2,1)}, f32[8,1792]{1,0:T(8,128)}, f32[128,1536]{1,0:T(8,128)}, f32[14,8,128]{2,1,0:T(8,128)}) custom-call(f32[56,264,128]{2,1,0:T(8,128)} %get-tuple-element.117.ext_ref, f32[1024,128]{1,0:T(8,128)} %get-tuple-element.118.dtr_ref, ...), custom_call_target="tpu_custom_call", output_to_operand_aliasing={{0}: (14, {})} | custom-call | flops 1 | bytes 1 | tf_op jit(solution)/shard_map/pallas_call | solution.py:910
  177.1 21.9 %shard_map.394 = (bf16[1024,1920]{1,0:T(8,128)(2,1)}, f32[8,1792]{1,0:T(8,128)}, f32[128,1536]{1,0:T(8,128)}, f32[14,8,128]{2,1,0:T(8,128)}) custom-call(f32[56,264,128]{2,1,0:T(8,128)} %get-tuple-element.117.ext_ref, f32[1024,128]{1,0:T(8,128)} %get-tuple-element.118.dtr_ref, ...), custom_call_target="tpu_custom_call", output_to_operand_aliasing={{0}: (14, {})} | custom-call | flops 1 | bytes 1 | tf_op jit(solution)/shard_map/pallas_call | solution.py:910
  200.6 2.1 collective-permute-start.23
  202.7 2.4 collective-permute-start.24
  207.3 17.8 %shard_map.395 = (bf16[1024,768]{1,0:T(8,128)(2,1)}, f32[8,1792]{1,0:T(8,128)}, bf16[4,96,1024]{2,1,0:T(8,128)(2,1)}, f32[4,96,1024]{2,1,0:T(8,128)}, bf16[4,96,...) custom-call(s32[1]{0:T(128)} %bitcast.core_ref.edge_ref.start_ref.before_ref.next_ref._, bf16[1024,896]{1,0:T(8,128)(2,1)} %bitcast.179, ...), custom_call_target="tpu_custom_call" | custom-call | flops 1 | bytes 1 | tf_op jit(solution)/shard_map/pallas_call | solution.py:967
  226.4 4.5 %all-to-all-start.3 = ((bf16[4,256,768]{2,1,0:T(8,128)(2,1)}), bf16[4,256,768]{2,1,0:T(8,128)(2,1)}, u32[]{:S(2)}, u32[]{:S(2)}) async-start(bf16[4,256,768]{2,1,0:T(8,128)(2,1)} %bitcast.205), calls=%async_computation.3 | async-start | bytes 3145728 | tf_op jit(solution)/shard_map/all_to_all | solution.py:1145
  230.9 2.0 fusion.7
  233.5 1.8 fusion.6
  236.5 6.8 %collective-permute-done.36 = bf16[2,4,24,896]{3,2,1,0:T(8,128)(2,1)} collective-permute-done((bf16[2,4,24,896]{3,2,1,0:T(8,128)(2,1)}, bf16[2,4,24,896]{3,2,1,0:T(8,128)(2,1)}, u32[]{:S(2)}, u32[]{:S(2)}) %collective-permute-start.36) | collective-permute-done | bytes 344096 | tf_op jit(solution)/shard_map/ppermute | solution.py:1033
  250.0 2.1 collective-permute-start.35
  253.1 2.1 collective-permute-start.30
  255.3 3.0 %collective-permute-done.30 = f32[8,1792]{1,0:T(8,128)S(1)} collective-permute-done((f32[8,1792]{1,0:T(8,128)S(1)}, f32[8,1792]{1,0:T(8,128)S(1)}, u32[]{:S(2)}, u32[]{:S(2)}) %collective-permute-start.30) | collective-permute-done | bytes 57376 | tf_op jit(solution)/shard_map/ppermute | solution.py:1033
  258.5 2.1 collective-permute-start.31
  260.6 2.4 collective-permute-start.32
  267.0 5.1 %all-to-all-done.3 = bf16[4,256,768]{2,1,0:T(8,128)(2,1)} async-done(((bf16[4,256,768]{2,1,0:T(8,128)(2,1)}), bf16[4,256,768]{2,1,0:T(8,128)(2,1)}, u32[]{:S(2)}, u32[]{:S(2)}) %all-to-all-start.3) | async-done | bytes 1572896 | tf_op jit(solution)/shard_map/all_to_all | solution.py:1145
  272.3 3.4 %convert_add_fusion = f32[4,256,768]{2,1,0:T(8,128)} fusion(bf16[4,256,768]{2,1,0:T(8,128)(2,1)} %all-to-all-done.3, bf16[4,256,768]{2,1,0:T(8,128)(2,1)S(1)} %copy-done.5), kind=kLoop, calls=%fused_computation | loop fusion | flops 2359296 | bytes 6291456 | tf_op jit(solution)/shard_map/add | solution.py:1374
  277.6 3.5 %shard_map.396 = (f32[1,24]{1,0:T(1,128)}, f32[1,24]{1,0:T(1,128)}, f32[1,24]{1,0:T(1,128)}, f32[24,3352]{1,0:T(8,128)}, f32[24,3352]{1,0:T(8,128)}, /*index=5*/...) custom-call(f32[8]{0:T(128)} %pad_maximum_fusion.16.rates_ref, ...), custom_call_target="tpu_custom_call" | custom-call | flops 1 | bytes 1 | tf_op jit(solution)/shard_map/pallas_call | solution.py:1012
  (221 shorter events, 65.9 us)
Async XLA Ops:
  4.8 15.3 %collective-permute-start = (bf16[24,5120]{1,0:T(8,128)(2,1)S(1)}, bf16[24,5120]{1,0:T(8,128)(2,1)S(1)}, u32[]{:S(2)}, u32[]{:S(2)}) collective-permute-start(bf16[24,5120]{1,0:T(8,128)(2,1)S(1)} %fusion.10), channel_id=1, source_target_pairs={{0,2},{1,3},{2,0},{3,1},{4,6},{5,7},{6,4},{7,5},{8,10},{9,11},{10,... | collective-permute-start | bytes 737288 | tf_op jit(solution)/shard_map/ppermute | solution.py:1033
  20.3 14.2 %collective-permute-start.1 = (bf16[2,24,5120]{2,1,0:T(8,128)(2,1)S(1)}, bf16[2,24,5120]{2,1,0:T(8,128)(2,1)S(1)}, u32[]{:S(2)}, u32[]{:S(2)}) collective-permute-start(bf16[2,24,5120]{2,1,0:T(8,128)(2,1)S(1)} %pad_maximum_fusion.9), channel_id=1, source_target_pairs={{0,1},{1,0},{2,3},{3,2},{4,5},{5,4},{6,7},{7,6},{8,9},{9,8},{10,11... | collective-permute-start | bytes 1474568 | tf_op jit(solution)/shard_map/ppermute | solution.py:1033
  21.0 47.2 %all-to-all-start = ((bf16[4,256,896]{2,1,0:T(8,128)(2,1)}), bf16[4,256,896]{2,1,0:T(8,128)(2,1)S(1)}, u32[]{:S(2)}, u32[]{:S(2)}) async-start(bf16[4,256,896]{2,1,0:T(8,128)(2,1)} %pad_maximum_fusion), calls=%async_computation | async-start | bytes 3670016 | tf_op jit(solution)/shard_map/all_to_all | solution.py:1129
  42.0 14.1 %collective-permute-start.12 = (bf16[4,48,768]{2,1,0:T(8,128)(2,1)S(1)}, bf16[4,48,768]{2,1,0:T(8,128)(2,1)S(1)}, u32[]{:S(2)}, u32[]{:S(2)}) collective-permute-start(bf16[4,48,768]{2,1,0:T(8,128)(2,1)S(1)} %bitcast.210), channel_id=1, source_target_pairs={{0,8},{4,12},{8,0},{12,4},{16,24},{20,28},{24,16},{28,20},{1,9},{5... | collective-permute-start | bytes 884744 | tf_op jit(solution)/shard_map/ppermute | solution.py:1033
  42.1 20.8 %collective-permute-start.11 = (bf16[4,24,1536]{2,1,0:T(8,128)(2,1)S(1)}, bf16[4,24,1536]{2,1,0:T(8,128)(2,1)S(1)}, u32[]{:S(2)}, u32[]{:S(2)}) collective-permute-start(bf16[4,24,1536]{2,1,0:T(8,128)(2,1)S(1)} %slice.135), channel_id=1, source_target_pairs={{0,16},{4,20},{8,24},{12,28},{16,0},{20,4},{24,8},{28,12},{1,17},{... | collective-permute-start | bytes 884744 | tf_op jit(solution)/shard_map/ppermute | solution.py:1033
  43.7 10.9 %collective-permute-start.2 = (bf16[4,24,1024]{2,1,0:T(8,128)(2,1)S(1)}, bf16[4,24,1024]{2,1,0:T(8,128)(2,1)S(1)}, u32[]{:S(2)}, u32[]{:S(2)}) collective-permute-start(bf16[4,24,1024]{2,1,0:T(8,128)(2,1)S(1)} %slice.121), channel_id=1, source_target_pairs={{0,16},{4,20},{8,24},{12,28},{16,0},{20,4},{24,8},{28,12},{1,17},{... | collective-permute-start | bytes 589832 | tf_op jit(solution)/shard_map/ppermute | solution.py:1033
  45.4 12.9 %collective-permute-start.6 = (bf16[2,4,24,896]{3,2,1,0:T(8,128)(2,1)S(1)}, bf16[2,4,24,896]{3,2,1,0:T(8,128)(2,1)S(1)}, u32[]{:S(2)}, u32[]{:S(2)}) collective-permute-start(bf16[2,4,24,896]{3,2,1,0:T(8,128)(2,1)S(1)} %pad_maximum_fusion.11), channel_id=1, source_target_pairs={{0,16},{4,20},{8,24},{12,28},{16,0},{20,4},{24,8},{28,12},{1,17},{... | collective-permute-start | bytes 1032200 | tf_op jit(solution)/shard_map/ppermute | solution.py:1033
  54.7 7.8 %collective-permute-start.3 = (bf16[2,4,24,1024]{3,2,1,0:T(8,128)(2,1)S(1)}, bf16[2,4,24,1024]{3,2,1,0:T(8,128)(2,1)S(1)}, u32[]{:S(2)}, u32[]{:S(2)}) collective-permute-start(bf16[2,4,24,1024]{3,2,1,0:T(8,128)(2,1)S(1)} %pad_maximum_fusion.10), channel_id=1, source_target_pairs={{0,8},{4,12},{8,0},{12,4},{16,24},{20,28},{24,16},{28,20},{1,9},{5... | collective-permute-start | bytes 1179656 | tf_op jit(solution)/shard_map/ppermute | solution.py:1033
  64.9 35.6 %collective-permute-start.15 = (bf16[2,4,48,768]{3,2,1,0:T(8,128)(2,1)}, bf16[2,4,48,768]{3,2,1,0:T(8,128)(2,1)}, u32[]{:S(2)}, u32[]{:S(2)}) collective-permute-start(bf16[2,4,48,768]{3,2,1,0:T(8,128)(2,1)} %pad_maximum_fusion.8), channel_id=1, source_target_pairs={{0,16},{4,20},{8,24},{12,28},{16,0},{20,4},{24,8},{28,12},{1,17},{... | collective-permute-start | bytes 1769480 | tf_op jit(solution)/shard_map/ppermute | solution.py:1033
  68.2 33.9 %collective-permute-start.13 = (bf16[2,4,24,1536]{3,2,1,0:T(8,128)(2,1)}, bf16[2,4,24,1536]{3,2,1,0:T(8,128)(2,1)}, u32[]{:S(2)}, u32[]{:S(2)}) collective-permute-start(bf16[2,4,24,1536]{3,2,1,0:T(8,128)(2,1)} %pad_maximum_fusion.7), channel_id=1, source_target_pairs={{0,8},{4,12},{8,0},{12,4},{16,24},{20,28},{24,16},{28,20},{1,9},{5... | collective-permute-start | bytes 1769480 | tf_op jit(solution)/shard_map/ppermute | solution.py:1033
  69.7 37.7 %all-to-all-start.1 = ((bf16[4,256,640]{2,1,0:T(8,128)(2,1)}), bf16[4,256,640]{2,1,0:T(8,128)(2,1)S(1)}, u32[]{:S(2)}, u32[]{:S(2)}) async-start(bf16[4,256,640]{2,1,0:T(8,128)(2,1)} %slice.96), calls=%async_computation.1 | async-start | bytes 2621440 | tf_op jit(solution)/shard_map/all_to_all | solution.py:1129
  134.0 12.7 %collective-permute-start.17 = (bf16[4,192,768]{2,1,0:T(8,128)(2,1)}, bf16[4,192,768]{2,1,0:T(8,128)(2,1)S(1)}, u32[]{:S(2)}, u32[]{:S(2)}) collective-permute-start(bf16[4,192,768]{2,1,0:T(8,128)(2,1)} %get-tuple-element.125), channel_id=1, source_target_pairs={{0,4},{4,0},{8,12},{12,8},{16,20},{20,16},{24,28},{28,24},{1,5},{5... | collective-permute-start | bytes 3538952 | tf_op jit(solution)/shard_map/ppermute | solution.py:1033
  134.2 12.5 %collective-permute-start.18 = (bf16[4,96,1536]{2,1,0:T(8,128)(2,1)}, bf16[4,96,1536]{2,1,0:T(8,128)(2,1)S(1)}, u32[]{:S(2)}, u32[]{:S(2)}) collective-permute-start(bf16[4,96,1536]{2,1,0:T(8,128)(2,1)} %get-tuple-element.127), channel_id=1, source_target_pairs={{0,4},{4,0},{8,12},{12,8},{16,20},{20,16},{24,28},{28,24},{1,5},{5... | collective-permute-start | bytes 3538952 | tf_op jit(solution)/shard_map/ppermute | solution.py:1033
  150.3 21.2 %collective-permute-start.20 = (bf16[2,4,24,1536]{3,2,1,0:T(8,128)(2,1)}, bf16[2,4,24,1536]{3,2,1,0:T(8,128)(2,1)S(1)}, u32[]{:S(2)}, u32[]{:S(2)}) collective-permute-start(bf16[2,4,24,1536]{3,2,1,0:T(8,128)(2,1)} %get-tuple-element.194), channel_id=1, source_target_pairs={{0,16},{4,20},{8,24},{12,28},{16,0},{20,4},{24,8},{28,12},{1,17},{... | collective-permute-start | bytes 1769480 | tf_op jit(solution)/shard_map/ppermute | solution.py:1033
  152.3 19.2 %collective-permute-start.19 = (bf16[2,4,48,768]{3,2,1,0:T(8,128)(2,1)}, bf16[2,4,48,768]{3,2,1,0:T(8,128)(2,1)}, u32[]{:S(2)}, u32[]{:S(2)}) collective-permute-start(bf16[2,4,48,768]{3,2,1,0:T(8,128)(2,1)} %get-tuple-element.196), channel_id=1, source_target_pairs={{0,8},{4,12},{8,0},{12,4},{16,24},{20,28},{24,16},{28,20},{1,9},{5... | collective-permute-start | bytes 1769480 | tf_op jit(solution)/shard_map/ppermute | solution.py:1033
  153.3 53.9 %all-to-all-start.2 = ((bf16[4,256,768]{2,1,0:T(8,128)(2,1)}), bf16[4,256,768]{2,1,0:T(8,128)(2,1)S(1)}, u32[]{:S(2)}, u32[]{:S(2)}) async-start(bf16[4,256,768]{2,1,0:T(8,128)(2,1)} %bitcast.204), calls=%async_computation.2 | async-start | bytes 3145728 | tf_op jit(solution)/shard_map/all_to_all | solution.py:1145
  173.5 25.5 %collective-permute-start.21 = (bf16[4,48,768]{2,1,0:T(8,128)(2,1)}, bf16[4,48,768]{2,1,0:T(8,128)(2,1)}, u32[]{:S(2)}, u32[]{:S(2)}) collective-permute-start(bf16[4,48,768]{2,1,0:T(8,128)(2,1)} %fusion.8), channel_id=1, source_target_pairs={{0,16},{4,20},{8,24},{12,28},{16,0},{20,4},{24,8},{28,12},{1,17},{... | collective-permute-start | bytes 884744 | tf_op jit(solution)/shard_map/ppermute | solution.py:1033
  176.2 24.0 %collective-permute-start.22 = (bf16[4,24,1536]{2,1,0:T(8,128)(2,1)S(1)}, bf16[4,24,1536]{2,1,0:T(8,128)(2,1)S(1)}, u32[]{:S(2)}, u32[]{:S(2)}) collective-permute-start(bf16[4,24,1536]{2,1,0:T(8,128)(2,1)S(1)} %fusion.9), channel_id=1, source_target_pairs={{0,8},{4,12},{8,0},{12,4},{16,24},{20,28},{24,16},{28,20},{1,9},{5... | collective-permute-start | bytes 884744 | tf_op jit(solution)/shard_map/ppermute | solution.py:1033
  200.6 24.4 %collective-permute-start.23 = (bf16[24,3072]{1,0:T(8,128)(2,1)S(1)}, bf16[24,3072]{1,0:T(8,128)(2,1)S(1)}, u32[]{:S(2)}, u32[]{:S(2)}) collective-permute-start(bf16[24,3072]{1,0:T(8,128)(2,1)S(1)} %get-tuple-element.202), channel_id=1, source_target_pairs={{0,1},{1,2},{2,3},{3,0},{4,5},{5,6},{6,7},{7,4},{8,9},{9,10},{10,1... | collective-permute-start | bytes 442376 | tf_op jit(solution)/shard_map/ppermute | solution.py:1110
  202.7 22.4 %collective-permute-start.24 = (bf16[24,3072]{1,0:T(8,128)(2,1)S(1)}, bf16[24,3072]{1,0:T(8,128)(2,1)S(1)}, u32[]{:S(2)}, u32[]{:S(2)}) collective-permute-start(bf16[24,3072]{1,0:T(8,128)(2,1)S(1)} %get-tuple-element.201), channel_id=1, source_target_pairs={{0,2},{1,3},{2,0},{3,1},{4,6},{5,7},{6,4},{7,5},{8,10},{9,11},{10,... | collective-permute-start | bytes 442376 | tf_op jit(solution)/shard_map/ppermute | solution.py:1110
  205.1 20.0 %collective-permute-start.25 = (bf16[24,3072]{1,0:T(8,128)(2,1)S(1)}, bf16[24,3072]{1,0:T(8,128)(2,1)S(1)}, u32[]{:S(2)}, u32[]{:S(2)}) collective-permute-start(bf16[24,3072]{1,0:T(8,128)(2,1)S(1)} %get-tuple-element.200), channel_id=1, source_target_pairs={{0,3},{1,0},{2,1},{3,2},{4,7},{5,4},{6,5},{7,6},{8,11},{9,8},{10,9... | collective-permute-start | bytes 442376 | tf_op jit(solution)/shard_map/ppermute | solution.py:1110
  225.2 8.3 %collective-permute-start.26 = (bf16[4,96,1024]{2,1,0:T(8,128)(2,1)}, bf16[4,96,1024]{2,1,0:T(8,128)(2,1)}, u32[]{:S(2)}, u32[]{:S(2)}) collective-permute-start(bf16[4,96,1024]{2,1,0:T(8,128)(2,1)} %get-tuple-element.161), channel_id=1, source_target_pairs={{0,4},{4,0},{8,12},{12,8},{16,20},{20,16},{24,28},{28,24},{1,5},{5... | collective-permute-start | bytes 2359304 | tf_op jit(solution)/shard_map/ppermute | solution.py:1033
  226.4 45.7 %all-to-all-start.3 = ((bf16[4,256,768]{2,1,0:T(8,128)(2,1)}), bf16[4,256,768]{2,1,0:T(8,128)(2,1)}, u32[]{:S(2)}, u32[]{:S(2)}) async-start(bf16[4,256,768]{2,1,0:T(8,128)(2,1)} %bitcast.205), calls=%async_computation.3 | async-start | bytes 3145728 | tf_op jit(solution)/shard_map/all_to_all | solution.py:1145
  232.9 10.4 %collective-permute-start.36 = (bf16[2,4,24,896]{3,2,1,0:T(8,128)(2,1)}, bf16[2,4,24,896]{3,2,1,0:T(8,128)(2,1)}, u32[]{:S(2)}, u32[]{:S(2)}) collective-permute-start(bf16[2,4,24,896]{3,2,1,0:T(8,128)(2,1)} %fusion.7), channel_id=1, source_target_pairs={{0,16},{4,20},{8,24},{12,28},{16,0},{20,4},{24,8},{28,12},{1,17},{... | collective-permute-start | bytes 1032200 | tf_op jit(solution)/shard_map/ppermute | solution.py:1033
  235.3 11.0 %collective-permute-start.34 = (bf16[2,4,24,1024]{3,2,1,0:T(8,128)(2,1)}, bf16[2,4,24,1024]{3,2,1,0:T(8,128)(2,1)S(1)}, u32[]{:S(2)}, u32[]{:S(2)}) collective-permute-start(bf16[2,4,24,1024]{3,2,1,0:T(8,128)(2,1)} %fusion.6), channel_id=1, source_target_pairs={{0,8},{4,12},{8,0},{12,4},{16,24},{20,28},{24,16},{28,20},{1,9},{5... | collective-permute-start | bytes 1179656 | tf_op jit(solution)/shard_map/ppermute | solution.py:1033
  244.8 10.4 %collective-permute-start.37 = (bf16[4,24,896]{2,1,0:T(8,128)(2,1)S(1)}, bf16[4,24,896]{2,1,0:T(8,128)(2,1)S(1)}, u32[]{:S(2)}, u32[]{:S(2)}) collective-permute-start(bf16[4,24,896]{2,1,0:T(8,128)(2,1)S(1)} %fusion.22), channel_id=1, source_target_pairs={{0,8},{4,12},{8,0},{12,4},{16,24},{20,28},{24,16},{28,20},{1,9},{5... | collective-permute-start | bytes 516104 | tf_op jit(solution)/shard_map/ppermute | solution.py:1033
  250.0 14.4 %collective-permute-start.35 = (bf16[4,24,1024]{2,1,0:T(8,128)(2,1)S(1)}, bf16[4,24,1024]{2,1,0:T(8,128)(2,1)S(1)}, u32[]{:S(2)}, u32[]{:S(2)}) collective-permute-start(bf16[4,24,1024]{2,1,0:T(8,128)(2,1)S(1)} %fusion.13), channel_id=1, source_target_pairs={{0,16},{4,20},{8,24},{12,28},{16,0},{20,4},{24,8},{28,12},{1,17},{... | collective-permute-start | bytes 589832 | tf_op jit(solution)/shard_map/ppermute | solution.py:1033
  258.5 13.6 %collective-permute-start.31 = (f32[8,384]{1,0:T(8,128)S(1)}, f32[8,384]{1,0:T(8,128)S(1)}, u32[]{:S(2)}, u32[]{:S(2)}) collective-permute-start(f32[8,384]{1,0:T(8,128)S(1)} %fusion.29.refs_0_), channel_id=1, source_target_pairs={{0,1},{1,2},{2,3},{3,0},{4,5},{5,6},{6,7},{7,4},{8,9},{9,10},{10,1... | collective-permute-start | bytes 36872 | tf_op jit(solution)/shard_map/ppermute | solution.py:1396
  260.6 15.1 %collective-permute-start.32 = (f32[8,384]{1,0:T(8,128)S(1)}, f32[8,384]{1,0:T(8,128)}, u32[]{:S(2)}, u32[]{:S(2)}) collective-permute-start(f32[8,384]{1,0:T(8,128)S(1)} %fusion.29.refs_0_), channel_id=1, source_target_pairs={{0,2},{1,3},{2,0},{3,1},{4,6},{5,7},{6,4},{7,5},{8,10},{9,11},{10,... | collective-permute-start | bytes 36872 | tf_op jit(solution)/shard_map/ppermute | solution.py:1396
  263.0 12.8 %collective-permute-start.33 = (f32[8,384]{1,0:T(8,128)S(1)}, f32[8,384]{1,0:T(8,128)}, u32[]{:S(2)}, u32[]{:S(2)}) collective-permute-start(f32[8,384]{1,0:T(8,128)S(1)} %fusion.29.refs_0_), channel_id=1, source_target_pairs={{0,3},{1,0},{2,1},{3,2},{4,7},{5,4},{6,5},{7,6},{8,11},{9,8},{10,9... | collective-permute-start | bytes 36872 | tf_op jit(solution)/shard_map/ppermute | solution.py:1396
  265.9 9.8 %collective-permute-start.38 = (bf16[24,1920]{1,0:T(8,128)(2,1)}, bf16[24,1920]{1,0:T(8,128)(2,1)S(1)}, u32[]{:S(2)}, u32[]{:S(2)}) collective-permute-start(bf16[24,1920]{1,0:T(8,128)(2,1)} %get-tuple-element.230), channel_id=1, source_target_pairs={{0,1},{1,2},{2,3},{3,0},{4,5},{5,6},{6,7},{7,4},{8,9},{9,10},{10,1... | collective-permute-start | bytes 276488 | tf_op jit(solution)/shard_map/ppermute | solution.py:1110
  266.4 9.8 %collective-permute-start.39 = (bf16[24,1920]{1,0:T(8,128)(2,1)S(1)}, bf16[24,1920]{1,0:T(8,128)(2,1)S(1)}, u32[]{:S(2)}, u32[]{:S(2)}) collective-permute-start(bf16[24,1920]{1,0:T(8,128)(2,1)S(1)} %get-tuple-element.231), channel_id=1, source_target_pairs={{0,2},{1,3},{2,0},{3,1},{4,6},{5,7},{6,4},{7,5},{8,10},{9,11},{10,... | collective-permute-start | bytes 276488 | tf_op jit(solution)/shard_map/ppermute | solution.py:1110
  (46 other events, 217.0 us)

commit v6 on v5

--- a/solution.py
+++ b/solution.py
@@ -1213,26 +1213,28 @@
     skip = jnp.repeat(head_params[2], inner // heads)[None, :]
     summing = summing_matrix(inner, heads)
 
-    in_low = padded(in_weight.astype(bf16), own_rows, inner + conv_dim + lanes)
-    out_low_own = out_weight.astype(bf16).reshape(2, own_rows, width)
+    in_own = padded(in_weight, own_rows, inner + conv_dim + lanes)
+    out_own = out_weight.reshape(2, own_rows, width)
     own_small = jnp.concatenate(
         [
-            padded(conv_params.astype(bf16), tap_rows, lanes),
-            padded(norm_gain.astype(bf16)[None, :], 1, lanes),
-            padded(gate_gain.astype(bf16)[None, :], 1, lanes),
+            padded(conv_params, tap_rows, lanes),
+            padded(norm_gain[None, :], 1, lanes),
+            padded(gate_gain[None, :], 1, lanes),
         ]
     )
-    shard = jnp.concatenate([in_low, out_low_own[0], out_low_own[1]], axis=1)
+    shard = [in_own, out_own[0], out_own[1]]
     half = width // 6
     both = jnp.concatenate([layer_in, out_grad[:, :, :half]], axis=2)
     second = lax.optimization_barrier(out_grad[:, :, half:])
     if own_rows >= tap_rows + 2:
-        shard = jnp.concatenate([shard, padded(own_small, own_rows, lanes)], axis=1)
+        shard = shard + [padded(own_small, own_rows, lanes)]
+        shard = lax.optimization_barrier(jnp.concatenate(shard, axis=1)).astype(bf16)
         gathered = gather_seq(shard, both, second, head, skip)
         seq_small = gathered[:, : tap_rows + 2, -lanes:]
     else:
+        shard = lax.optimization_barrier(jnp.concatenate(shard, axis=1)).astype(bf16)
         gathered = gather_seq(shard)
-        seq_small = gather_seq(padded(own_small, 8, lanes))[:, : tap_rows + 2]
+        seq_small = gather_seq(padded(own_small, 8, lanes).astype(bf16))[:, : tap_rows + 2]
     tokens = to_sequences(after(both, shard), part, size)
     small = jnp.zeros((8, conv_dim), bf16)
     group = lax.axis_index("dp")

time: 287 us -> 286 us (level)
  other arithmetic: 32.8 us -> 29 us
  local copies, waits for them, and re-layouts: 13.5 us -> 16.5 us
  transfers between devices with their start and end apart: 45 -> 45, of which waited for: 18 -> 18; matrix products, arithmetic and copies ran while one was open for 11% -> 11% of each run, Pallas kernels for 31% -> 32%
where the time goes in v6:
time: 286 us; the launch traced here: 281 us
  Pallas kernels  118 us (41%)
  starting transfers between devices  64.6 us (23%)
  waiting for transfers between devices  50.8 us (18%)
  other arithmetic  29 us (10%)
  local copies, waits for them, and re-layouts  16.5 us (6%)
    pallas_call x3, Pallas kernels, mixer_backward(): pl.pallas_call(partial(mixer_backward_kernel, heads=heads, inner=inner, t...  46.5 us
    ppermute x32, waiting for transfers between devices, swap(): return lax.ppermute(block, axis, [(i, i ^ 1 << bit) for i in devices])  43.2 us
    ppermute x32, starting transfers between devices, swap(): return lax.ppermute(block, axis, [(i, i ^ 1 << bit) for i in devices])  31.1 us
    pallas_call x1, Pallas kernels, gate_step(): pl.pallas_call(partial(gate_kernel, gain_row=taps + 2), grid=(part, size)...  25.5 us
    pallas_call x1, Pallas kernels, mixer_forward(): pl.pallas_call(partial(mixer_forward_kernel, heads=heads, inner=inner, ta...  24.4 us
    pallas_call x1, Pallas kernels, input_grad(): pl.pallas_call(partial(input_grad_kernel, gain_row=taps + 1), grid=(part,...  17.8 us
    all_to_all x2, starting transfers between devices, to_sequences(): lax.all_to_all(block, 'seq', 0, 0, axis_index_groups=seq_groups(size), ti...  10.4 us
    all_to_all x2, starting transfers between devices, to_pieces(): lax.all_to_all(block, 'seq', 0, 0, axis_index_groups=seq_groups(size), ti...  10 us
  transfers between devices with their start and end apart: 45, of which 18 were waited for; matrix products, arithmetic and copies ran while one was open for 11% of the time, Pallas kernels for 32%

profile of v6, /device:TPU:0, one launch (start us, length us, event | category | flops | bytes accessed | tf_op | source)
XLA Modules:
  0.0 281.0 jit_solution(8861124284681433791)
XLA Ops:
  3.3 4.1 %collective-permute-start = (bf16[24,5120]{1,0:T(8,128)(2,1)S(1)}, bf16[24,5120]{1,0:T(8,128)(2,1)S(1)}, u32[]{:S(2)}, u32[]{:S(2)}) collective-permute-start(bf16[24,5120]{1,0:T(8,128)(2,1)S(1)} %select_maximum_fusion), channel_id=1, source_target_pairs={{0,2},{1,3},{2,0},{3,1},{4,6},{5,7},{6,4},{7,5},{8,10},{9,11},{10,... | collective-permute-start | bytes 737288 | tf_op jit(solution)/shard_map/ppermute | solution.py:1033
  8.1 2.6 slice.96
  13.5 5.2 %collective-permute-done = bf16[24,5120]{1,0:T(8,128)(2,1)S(1)} collective-permute-done((bf16[24,5120]{1,0:T(8,128)(2,1)S(1)}, bf16[24,5120]{1,0:T(8,128)(2,1)S(1)}, u32[]{:S(2)}, u32[]{:S(2)}) %collective-permute-start) | collective-permute-done | bytes 245792 | tf_op jit(solution)/shard_map/ppermute | solution.py:1033
  19.5 4.6 %all-to-all-start = ((bf16[4,256,896]{2,1,0:T(8,128)(2,1)}), bf16[4,256,896]{2,1,0:T(8,128)(2,1)S(1)}, u32[]{:S(2)}, u32[]{:S(2)}) async-start(bf16[4,256,896]{2,1,0:T(8,128)(2,1)} %pad_maximum_fusion), calls=%async_computation | async-start | bytes 3670016 | tf_op jit(solution)/shard_map/all_to_all | solution.py:1129
  24.2 8.8 %collective-permute-done.1 = bf16[2,24,5120]{2,1,0:T(8,128)(2,1)S(1)} collective-permute-done((bf16[2,24,5120]{2,1,0:T(8,128)(2,1)S(1)}, bf16[2,24,5120]{2,1,0:T(8,128)(2,1)S(1)}, u32[]{:S(2)}, u32[]{:S(2)}) %collective-permute-start.1) | collective-permute-done | bytes 491552 | tf_op jit(solution)/shard_map/ppermute | solution.py:1033
  36.0 1.9 collective-permute-start.5
  38.3 2.1 collective-permute-start.9
  44.5 8.6 %collective-permute-done.2 = bf16[4,24,1024]{2,1,0:T(8,128)(2,1)S(1)} collective-permute-done((bf16[4,24,1024]{2,1,0:T(8,128)(2,1)S(1)}, bf16[4,24,1024]{2,1,0:T(8,128)(2,1)S(1)}, u32[]{:S(2)}, u32[]{:S(2)}) %collective-permute-start.2) | collective-permute-done | bytes 196640 | tf_op jit(solution)/shard_map/ppermute | solution.py:1033
  57.0 4.0 %collective-permute-done.3 = bf16[2,4,24,1024]{3,2,1,0:T(8,128)(2,1)S(1)} collective-permute-done((bf16[2,4,24,1024]{3,2,1,0:T(8,128)(2,1)S(1)}, bf16[2,4,24,1024]{3,2,1,0:T(8,128)(2,1)S(1)}, u32[]{:S(2)}, u32[]{:S(2)}) %collective-permute-start.3) | collective-permute-done | bytes 393248 | tf_op jit(solution)/shard_map/ppermute | solution.py:1033
  68.2 5.8 %all-to-all-start.1 = ((bf16[4,256,640]{2,1,0:T(8,128)(2,1)}), bf16[4,256,640]{2,1,0:T(8,128)(2,1)S(1)}, u32[]{:S(2)}, u32[]{:S(2)}) async-start(bf16[4,256,640]{2,1,0:T(8,128)(2,1)} %slice.96), calls=%async_computation.1 | async-start | bytes 2621440 | tf_op jit(solution)/shard_map/all_to_all | solution.py:1129
  74.6 24.4 %shard_map.390 = (bf16[1024,768]{1,0:T(8,128)(2,1)}, f32[56,264,128]{2,1,0:T(8,128)}, f32[1024,128]{1,0:T(8,128)}, f32[1024,128]{1,0:T(8,128)}, f32[1024,1536]{1...) custom-call(s32[1]{0:T(128)} %bitcast.core_ref.edge_ref.start_ref.before_ref.next_ref._, ...), custom_call_target="tpu_custom_call" | custom-call | flops 1 | bytes 1 | tf_op jit(solution)/shard_map/pallas_call | solution.py:786
  107.0 25.5 %shard_map.391 = (bf16[1024,768]{1,0:T(8,128)(2,1)}, bf16[1024,1536]{1,0:T(8,128)(2,1)}, bf16[1024,1536]{1,0:T(8,128)(2,1)}, f32[8,1536]{1,0:T(8,128)}, bf16[4,1...) custom-call(s32[1]{0:T(128)} %bitcast.core_ref.edge_ref.start_ref.before_r, ...), custom_call_target="tpu_custom_call" | custom-call | flops 1 | bytes 1 | tf_op jit(solution)/shard_map/pallas_call | solution.py:851
  133.1 12.1 %shard_map.392 = (bf16[1024,1920]{1,0:T(8,128)(2,1)}, f32[8,1792]{1,0:T(8,128)}, f32[128,1536]{1,0:T(8,128)}, f32[14,8,128]{2,1,0:T(8,128)}) custom-call(f32[56,264,128]{2,1,0:T(8,128)} %get-tuple-element.117.ext_ref, f32[1024,128]{1,0:T(8,128)} %get-tuple-element.118.dtr_ref, f32[1024,128]{1,0:T(8,128)} %get-tuple-element.119.cum_ref, ...), custom_call_target="tpu_custom_call" | custom-call | flops 1 | bytes 1 | tf_op jit(solution)/shard_map/pallas_call | solution.py:910
  146.2 2.6 fusion.3
  151.8 5.6 %all-to-all-start.2 = ((bf16[4,256,768]{2,1,0:T(8,128)(2,1)}), bf16[4,256,768]{2,1,0:T(8,128)(2,1)S(1)}, u32[]{:S(2)}, u32[]{:S(2)}) async-start(bf16[4,256,768]{2,1,0:T(8,128)(2,1)} %bitcast.200), calls=%async_computation.2 | async-start | bytes 3145728 | tf_op jit(solution)/shard_map/all_to_all | solution.py:1145
  157.4 12.6 %shard_map.393 = (bf16[1024,1920]{1,0:T(8,128)(2,1)}, f32[8,1792]{1,0:T(8,128)}, f32[128,1536]{1,0:T(8,128)}, f32[14,8,128]{2,1,0:T(8,128)}) custom-call(f32[56,264,128]{2,1,0:T(8,128)} %get-tuple-element.117.ext_ref, f32[1024,128]{1,0:T(8,128)} %get-tuple-element.118.dtr_ref, ...), custom_call_target="tpu_custom_call", output_to_operand_aliasing={{0}: (14, {})} | custom-call | flops 1 | bytes 1 | tf_op jit(solution)/shard_map/pallas_call | solution.py:910
  175.6 21.9 %shard_map.394 = (bf16[1024,1920]{1,0:T(8,128)(2,1)}, f32[8,1792]{1,0:T(8,128)}, f32[128,1536]{1,0:T(8,128)}, f32[14,8,128]{2,1,0:T(8,128)}) custom-call(f32[56,264,128]{2,1,0:T(8,128)} %get-tuple-element.117.ext_ref, f32[1024,128]{1,0:T(8,128)} %get-tuple-element.118.dtr_ref, ...), custom_call_target="tpu_custom_call", output_to_operand_aliasing={{0}: (14, {})} | custom-call | flops 1 | bytes 1 | tf_op jit(solution)/shard_map/pallas_call | solution.py:910
  199.1 2.1 collective-permute-start.23
  201.2 2.4 collective-permute-start.24
  205.8 17.8 %shard_map.395 = (bf16[1024,768]{1,0:T(8,128)(2,1)}, f32[8,1792]{1,0:T(8,128)}, bf16[4,96,1024]{2,1,0:T(8,128)(2,1)}, f32[4,96,1024]{2,1,0:T(8,128)}, bf16[4,96,...) custom-call(s32[1]{0:T(128)} %bitcast.core_ref.edge_ref.start_ref.before_ref.next_ref._, bf16[1024,896]{1,0:T(8,128)(2,1)} %bitcast.175, ...), custom_call_target="tpu_custom_call" | custom-call | flops 1 | bytes 1 | tf_op jit(solution)/shard_map/pallas_call | solution.py:967
  224.9 4.5 %all-to-all-start.3 = ((bf16[4,256,768]{2,1,0:T(8,128)(2,1)}), bf16[4,256,768]{2,1,0:T(8,128)(2,1)}, u32[]{:S(2)}, u32[]{:S(2)}) async-start(bf16[4,256,768]{2,1,0:T(8,128)(2,1)} %bitcast.201), calls=%async_computation.3 | async-start | bytes 3145728 | tf_op jit(solution)/shard_map/all_to_all | solution.py:1145
  229.4 2.0 fusion.6
  232.0 1.8 fusion.5
  235.0 6.8 %collective-permute-done.36 = bf16[2,4,24,896]{3,2,1,0:T(8,128)(2,1)} collective-permute-done((bf16[2,4,24,896]{3,2,1,0:T(8,128)(2,1)}, bf16[2,4,24,896]{3,2,1,0:T(8,128)(2,1)}, u32[]{:S(2)}, u32[]{:S(2)}) %collective-permute-start.36) | collective-permute-done | bytes 344096 | tf_op jit(solution)/shard_map/ppermute | solution.py:1033
  248.5 2.1 collective-permute-start.35
  251.6 2.1 collective-permute-start.30
  253.8 3.0 %collective-permute-done.30 = f32[8,1792]{1,0:T(8,128)S(1)} collective-permute-done((f32[8,1792]{1,0:T(8,128)S(1)}, f32[8,1792]{1,0:T(8,128)S(1)}, u32[]{:S(2)}, u32[]{:S(2)}) %collective-permute-start.30) | collective-permute-done | bytes 57376 | tf_op jit(solution)/shard_map/ppermute | solution.py:1033
  257.0 2.1 collective-permute-start.31
  259.1 2.4 collective-permute-start.32
  265.5 5.2 %all-to-all-done.3 = bf16[4,256,768]{2,1,0:T(8,128)(2,1)} async-done(((bf16[4,256,768]{2,1,0:T(8,128)(2,1)}), bf16[4,256,768]{2,1,0:T(8,128)(2,1)}, u32[]{:S(2)}, u32[]{:S(2)}) %all-to-all-start.3) | async-done | bytes 1572896 | tf_op jit(solution)/shard_map/all_to_all | solution.py:1145
  270.8 3.4 %convert_add_fusion = f32[4,256,768]{2,1,0:T(8,128)} fusion(bf16[4,256,768]{2,1,0:T(8,128)(2,1)} %all-to-all-done.3, bf16[4,256,768]{2,1,0:T(8,128)(2,1)S(1)} %copy-done.4), kind=kLoop, calls=%fused_computation | loop fusion | flops 2359296 | bytes 6291456 | tf_op jit(solution)/shard_map/add | solution.py:1376
  276.1 3.5 %shard_map.396 = (f32[1,24]{1,0:T(1,128)}, f32[1,24]{1,0:T(1,128)}, f32[1,24]{1,0:T(1,128)}, f32[24,3352]{1,0:T(8,128)}, f32[24,3352]{1,0:T(8,128)}, /*index=5*/...) custom-call(f32[8]{0:T(128)} %pad_maximum_fusion.16.rates_ref, ...), custom_call_target="tpu_custom_call" | custom-call | flops 1 | bytes 1 | tf_op jit(solution)/shard_map/pallas_call | solution.py:1012
  (216 shorter events, 65.3 us)
Async XLA Ops:
  3.3 15.3 %collective-permute-start = (bf16[24,5120]{1,0:T(8,128)(2,1)S(1)}, bf16[24,5120]{1,0:T(8,128)(2,1)S(1)}, u32[]{:S(2)}, u32[]{:S(2)}) collective-permute-start(bf16[24,5120]{1,0:T(8,128)(2,1)S(1)} %select_maximum_fusion), channel_id=1, source_target_pairs={{0,2},{1,3},{2,0},{3,1},{4,6},{5,7},{6,4},{7,5},{8,10},{9,11},{10,... | collective-permute-start | bytes 737288 | tf_op jit(solution)/shard_map/ppermute | solution.py:1033
  18.8 14.2 %collective-permute-start.1 = (bf16[2,24,5120]{2,1,0:T(8,128)(2,1)S(1)}, bf16[2,24,5120]{2,1,0:T(8,128)(2,1)S(1)}, u32[]{:S(2)}, u32[]{:S(2)}) collective-permute-start(bf16[2,24,5120]{2,1,0:T(8,128)(2,1)S(1)} %pad_maximum_fusion.9), channel_id=1, source_target_pairs={{0,1},{1,0},{2,3},{3,2},{4,5},{5,4},{6,7},{7,6},{8,9},{9,8},{10,11... | collective-permute-start | bytes 1474568 | tf_op jit(solution)/shard_map/ppermute | solution.py:1033
  19.5 47.2 %all-to-all-start = ((bf16[4,256,896]{2,1,0:T(8,128)(2,1)}), bf16[4,256,896]{2,1,0:T(8,128)(2,1)S(1)}, u32[]{:S(2)}, u32[]{:S(2)}) async-start(bf16[4,256,896]{2,1,0:T(8,128)(2,1)} %pad_maximum_fusion), calls=%async_computation | async-start | bytes 3670016 | tf_op jit(solution)/shard_map/all_to_all | solution.py:1129
  40.4 14.1 %collective-permute-start.12 = (bf16[4,48,768]{2,1,0:T(8,128)(2,1)S(1)}, bf16[4,48,768]{2,1,0:T(8,128)(2,1)S(1)}, u32[]{:S(2)}, u32[]{:S(2)}) collective-permute-start(bf16[4,48,768]{2,1,0:T(8,128)(2,1)S(1)} %bitcast.206), channel_id=1, source_target_pairs={{0,8},{4,12},{8,0},{12,4},{16,24},{20,28},{24,16},{28,20},{1,9},{5... | collective-permute-start | bytes 884744 | tf_op jit(solution)/shard_map/ppermute | solution.py:1033
  40.5 20.8 %collective-permute-start.11 = (bf16[4,24,1536]{2,1,0:T(8,128)(2,1)S(1)}, bf16[4,24,1536]{2,1,0:T(8,128)(2,1)S(1)}, u32[]{:S(2)}, u32[]{:S(2)}) collective-permute-start(bf16[4,24,1536]{2,1,0:T(8,128)(2,1)S(1)} %slice.133), channel_id=1, source_target_pairs={{0,16},{4,20},{8,24},{12,28},{16,0},{20,4},{24,8},{28,12},{1,17},{... | collective-permute-start | bytes 884744 | tf_op jit(solution)/shard_map/ppermute | solution.py:1033
  42.2 10.9 %collective-permute-start.2 = (bf16[4,24,1024]{2,1,0:T(8,128)(2,1)S(1)}, bf16[4,24,1024]{2,1,0:T(8,128)(2,1)S(1)}, u32[]{:S(2)}, u32[]{:S(2)}) collective-permute-start(bf16[4,24,1024]{2,1,0:T(8,128)(2,1)S(1)} %slice.119), channel_id=1, source_target_pairs={{0,16},{4,20},{8,24},{12,28},{16,0},{20,4},{24,8},{28,12},{1,17},{... | collective-permute-start | bytes 589832 | tf_op jit(solution)/shard_map/ppermute | solution.py:1033
  43.8 12.9 %collective-permute-start.6 = (bf16[2,4,24,896]{3,2,1,0:T(8,128)(2,1)S(1)}, bf16[2,4,24,896]{3,2,1,0:T(8,128)(2,1)S(1)}, u32[]{:S(2)}, u32[]{:S(2)}) collective-permute-start(bf16[2,4,24,896]{3,2,1,0:T(8,128)(2,1)S(1)} %pad_maximum_fusion.11), channel_id=1, source_target_pairs={{0,16},{4,20},{8,24},{12,28},{16,0},{20,4},{24,8},{28,12},{1,17},{... | collective-permute-start | bytes 1032200 | tf_op jit(solution)/shard_map/ppermute | solution.py:1033
  53.2 7.8 %collective-permute-start.3 = (bf16[2,4,24,1024]{3,2,1,0:T(8,128)(2,1)S(1)}, bf16[2,4,24,1024]{3,2,1,0:T(8,128)(2,1)S(1)}, u32[]{:S(2)}, u32[]{:S(2)}) collective-permute-start(bf16[2,4,24,1024]{3,2,1,0:T(8,128)(2,1)S(1)} %pad_maximum_fusion.10), channel_id=1, source_target_pairs={{0,8},{4,12},{8,0},{12,4},{16,24},{20,28},{24,16},{28,20},{1,9},{5... | collective-permute-start | bytes 1179656 | tf_op jit(solution)/shard_map/ppermute | solution.py:1033
  63.4 35.6 %collective-permute-start.15 = (bf16[2,4,48,768]{3,2,1,0:T(8,128)(2,1)}, bf16[2,4,48,768]{3,2,1,0:T(8,128)(2,1)}, u32[]{:S(2)}, u32[]{:S(2)}) collective-permute-start(bf16[2,4,48,768]{3,2,1,0:T(8,128)(2,1)} %pad_maximum_fusion.8), channel_id=1, source_target_pairs={{0,16},{4,20},{8,24},{12,28},{16,0},{20,4},{24,8},{28,12},{1,17},{... | collective-permute-start | bytes 1769480 | tf_op jit(solution)/shard_map/ppermute | solution.py:1033
  66.7 33.9 %collective-permute-start.13 = (bf16[2,4,24,1536]{3,2,1,0:T(8,128)(2,1)}, bf16[2,4,24,1536]{3,2,1,0:T(8,128)(2,1)}, u32[]{:S(2)}, u32[]{:S(2)}) collective-permute-start(bf16[2,4,24,1536]{3,2,1,0:T(8,128)(2,1)} %pad_maximum_fusion.7), channel_id=1, source_target_pairs={{0,8},{4,12},{8,0},{12,4},{16,24},{20,28},{24,16},{28,20},{1,9},{5... | collective-permute-start | bytes 1769480 | tf_op jit(solution)/shard_map/ppermute | solution.py:1033
  68.2 37.7 %all-to-all-start.1 = ((bf16[4,256,640]{2,1,0:T(8,128)(2,1)}), bf16[4,256,640]{2,1,0:T(8,128)(2,1)S(1)}, u32[]{:S(2)}, u32[]{:S(2)}) async-start(bf16[4,256,640]{2,1,0:T(8,128)(2,1)} %slice.96), calls=%async_computation.1 | async-start | bytes 2621440 | tf_op jit(solution)/shard_map/all_to_all | solution.py:1129
  132.5 12.7 %collective-permute-start.17 = (bf16[4,192,768]{2,1,0:T(8,128)(2,1)}, bf16[4,192,768]{2,1,0:T(8,128)(2,1)S(1)}, u32[]{:S(2)}, u32[]{:S(2)}) collective-permute-start(bf16[4,192,768]{2,1,0:T(8,128)(2,1)} %get-tuple-element.125), channel_id=1, source_target_pairs={{0,4},{4,0},{8,12},{12,8},{16,20},{20,16},{24,28},{28,24},{1,5},{5... | collective-permute-start | bytes 3538952 | tf_op jit(solution)/shard_map/ppermute | solution.py:1033
  132.7 12.5 %collective-permute-start.18 = (bf16[4,96,1536]{2,1,0:T(8,128)(2,1)}, bf16[4,96,1536]{2,1,0:T(8,128)(2,1)S(1)}, u32[]{:S(2)}, u32[]{:S(2)}) collective-permute-start(bf16[4,96,1536]{2,1,0:T(8,128)(2,1)} %get-tuple-element.127), channel_id=1, source_target_pairs={{0,4},{4,0},{8,12},{12,8},{16,20},{20,16},{24,28},{28,24},{1,5},{5... | collective-permute-start | bytes 3538952 | tf_op jit(solution)/shard_map/ppermute | solution.py:1033
  148.8 21.2 %collective-permute-start.20 = (bf16[2,4,24,1536]{3,2,1,0:T(8,128)(2,1)}, bf16[2,4,24,1536]{3,2,1,0:T(8,128)(2,1)S(1)}, u32[]{:S(2)}, u32[]{:S(2)}) collective-permute-start(bf16[2,4,24,1536]{3,2,1,0:T(8,128)(2,1)} %get-tuple-element.194), channel_id=1, source_target_pairs={{0,16},{4,20},{8,24},{12,28},{16,0},{20,4},{24,8},{28,12},{1,17},{... | collective-permute-start | bytes 1769480 | tf_op jit(solution)/shard_map/ppermute | solution.py:1033
  150.8 19.2 %collective-permute-start.19 = (bf16[2,4,48,768]{3,2,1,0:T(8,128)(2,1)}, bf16[2,4,48,768]{3,2,1,0:T(8,128)(2,1)}, u32[]{:S(2)}, u32[]{:S(2)}) collective-permute-start(bf16[2,4,48,768]{3,2,1,0:T(8,128)(2,1)} %get-tuple-element.196), channel_id=1, source_target_pairs={{0,8},{4,12},{8,0},{12,4},{16,24},{20,28},{24,16},{28,20},{1,9},{5... | collective-permute-start | bytes 1769480 | tf_op jit(solution)/shard_map/ppermute | solution.py:1033
  151.8 53.9 %all-to-all-start.2 = ((bf16[4,256,768]{2,1,0:T(8,128)(2,1)}), bf16[4,256,768]{2,1,0:T(8,128)(2,1)S(1)}, u32[]{:S(2)}, u32[]{:S(2)}) async-start(bf16[4,256,768]{2,1,0:T(8,128)(2,1)} %bitcast.200), calls=%async_computation.2 | async-start | bytes 3145728 | tf_op jit(solution)/shard_map/all_to_all | solution.py:1145
  172.0 25.5 %collective-permute-start.21 = (bf16[4,48,768]{2,1,0:T(8,128)(2,1)}, bf16[4,48,768]{2,1,0:T(8,128)(2,1)}, u32[]{:S(2)}, u32[]{:S(2)}) collective-permute-start(bf16[4,48,768]{2,1,0:T(8,128)(2,1)} %fusion.7), channel_id=1, source_target_pairs={{0,16},{4,20},{8,24},{12,28},{16,0},{20,4},{24,8},{28,12},{1,17},{... | collective-permute-start | bytes 884744 | tf_op jit(solution)/shard_map/ppermute | solution.py:1033
  174.7 24.0 %collective-permute-start.22 = (bf16[4,24,1536]{2,1,0:T(8,128)(2,1)S(1)}, bf16[4,24,1536]{2,1,0:T(8,128)(2,1)S(1)}, u32[]{:S(2)}, u32[]{:S(2)}) collective-permute-start(bf16[4,24,1536]{2,1,0:T(8,128)(2,1)S(1)} %fusion.8), channel_id=1, source_target_pairs={{0,8},{4,12},{8,0},{12,4},{16,24},{20,28},{24,16},{28,20},{1,9},{5... | collective-permute-start | bytes 884744 | tf_op jit(solution)/shard_map/ppermute | solution.py:1033
  199.1 24.4 %collective-permute-start.23 = (bf16[24,3072]{1,0:T(8,128)(2,1)S(1)}, bf16[24,3072]{1,0:T(8,128)(2,1)S(1)}, u32[]{:S(2)}, u32[]{:S(2)}) collective-permute-start(bf16[24,3072]{1,0:T(8,128)(2,1)S(1)} %get-tuple-element.202), channel_id=1, source_target_pairs={{0,1},{1,2},{2,3},{3,0},{4,5},{5,6},{6,7},{7,4},{8,9},{9,10},{10,1... | collective-permute-start | bytes 442376 | tf_op jit(solution)/shard_map/ppermute | solution.py:1110
  201.2 22.4 %collective-permute-start.24 = (bf16[24,3072]{1,0:T(8,128)(2,1)S(1)}, bf16[24,3072]{1,0:T(8,128)(2,1)S(1)}, u32[]{:S(2)}, u32[]{:S(2)}) collective-permute-start(bf16[24,3072]{1,0:T(8,128)(2,1)S(1)} %get-tuple-element.201), channel_id=1, source_target_pairs={{0,2},{1,3},{2,0},{3,1},{4,6},{5,7},{6,4},{7,5},{8,10},{9,11},{10,... | collective-permute-start | bytes 442376 | tf_op jit(solution)/shard_map/ppermute | solution.py:1110
  203.6 20.0 %collective-permute-start.25 = (bf16[24,3072]{1,0:T(8,128)(2,1)S(1)}, bf16[24,3072]{1,0:T(8,128)(2,1)S(1)}, u32[]{:S(2)}, u32[]{:S(2)}) collective-permute-start(bf16[24,3072]{1,0:T(8,128)(2,1)S(1)} %get-tuple-element.200), channel_id=1, source_target_pairs={{0,3},{1,0},{2,1},{3,2},{4,7},{5,4},{6,5},{7,6},{8,11},{9,8},{10,9... | collective-permute-start | bytes 442376 | tf_op jit(solution)/shard_map/ppermute | solution.py:1110
  223.7 8.3 %collective-permute-start.26 = (bf16[4,96,1024]{2,1,0:T(8,128)(2,1)}, bf16[4,96,1024]{2,1,0:T(8,128)(2,1)}, u32[]{:S(2)}, u32[]{:S(2)}) collective-permute-start(bf16[4,96,1024]{2,1,0:T(8,128)(2,1)} %get-tuple-element.161), channel_id=1, source_target_pairs={{0,4},{4,0},{8,12},{12,8},{16,20},{20,16},{24,28},{28,24},{1,5},{5... | collective-permute-start | bytes 2359304 | tf_op jit(solution)/shard_map/ppermute | solution.py:1033
  224.9 45.8 %all-to-all-start.3 = ((bf16[4,256,768]{2,1,0:T(8,128)(2,1)}), bf16[4,256,768]{2,1,0:T(8,128)(2,1)}, u32[]{:S(2)}, u32[]{:S(2)}) async-start(bf16[4,256,768]{2,1,0:T(8,128)(2,1)} %bitcast.201), calls=%async_computation.3 | async-start | bytes 3145728 | tf_op jit(solution)/shard_map/all_to_all | solution.py:1145
  231.4 10.4 %collective-permute-start.36 = (bf16[2,4,24,896]{3,2,1,0:T(8,128)(2,1)}, bf16[2,4,24,896]{3,2,1,0:T(8,128)(2,1)}, u32[]{:S(2)}, u32[]{:S(2)}) collective-permute-start(bf16[2,4,24,896]{3,2,1,0:T(8,128)(2,1)} %fusion.6), channel_id=1, source_target_pairs={{0,16},{4,20},{8,24},{12,28},{16,0},{20,4},{24,8},{28,12},{1,17},{... | collective-permute-start | bytes 1032200 | tf_op jit(solution)/shard_map/ppermute | solution.py:1033
  233.8 11.0 %collective-permute-start.34 = (bf16[2,4,24,1024]{3,2,1,0:T(8,128)(2,1)}, bf16[2,4,24,1024]{3,2,1,0:T(8,128)(2,1)S(1)}, u32[]{:S(2)}, u32[]{:S(2)}) collective-permute-start(bf16[2,4,24,1024]{3,2,1,0:T(8,128)(2,1)} %fusion.5), channel_id=1, source_target_pairs={{0,8},{4,12},{8,0},{12,4},{16,24},{20,28},{24,16},{28,20},{1,9},{5... | collective-permute-start | bytes 1179656 | tf_op jit(solution)/shard_map/ppermute | solution.py:1033
  243.3 10.4 %collective-permute-start.37 = (bf16[4,24,896]{2,1,0:T(8,128)(2,1)S(1)}, bf16[4,24,896]{2,1,0:T(8,128)(2,1)S(1)}, u32[]{:S(2)}, u32[]{:S(2)}) collective-permute-start(bf16[4,24,896]{2,1,0:T(8,128)(2,1)S(1)} %fusion.18), channel_id=1, source_target_pairs={{0,8},{4,12},{8,0},{12,4},{16,24},{20,28},{24,16},{28,20},{1,9},{5... | collective-permute-start | bytes 516104 | tf_op jit(solution)/shard_map/ppermute | solution.py:1033
  248.5 14.4 %collective-permute-start.35 = (bf16[4,24,1024]{2,1,0:T(8,128)(2,1)S(1)}, bf16[4,24,1024]{2,1,0:T(8,128)(2,1)S(1)}, u32[]{:S(2)}, u32[]{:S(2)}) collective-permute-start(bf16[4,24,1024]{2,1,0:T(8,128)(2,1)S(1)} %fusion.9), channel_id=1, source_target_pairs={{0,16},{4,20},{8,24},{12,28},{16,0},{20,4},{24,8},{28,12},{1,17},{... | collective-permute-start | bytes 589832 | tf_op jit(solution)/shard_map/ppermute | solution.py:1033
  257.0 13.7 %collective-permute-start.31 = (f32[8,384]{1,0:T(8,128)S(1)}, f32[8,384]{1,0:T(8,128)S(1)}, u32[]{:S(2)}, u32[]{:S(2)}) collective-permute-start(f32[8,384]{1,0:T(8,128)S(1)} %fusion.25.refs_0_), channel_id=1, source_target_pairs={{0,1},{1,2},{2,3},{3,0},{4,5},{5,6},{6,7},{7,4},{8,9},{9,10},{10,1... | collective-permute-start | bytes 36872 | tf_op jit(solution)/shard_map/ppermute | solution.py:1398
  259.1 15.1 %collective-permute-start.32 = (f32[8,384]{1,0:T(8,128)S(1)}, f32[8,384]{1,0:T(8,128)}, u32[]{:S(2)}, u32[]{:S(2)}) collective-permute-start(f32[8,384]{1,0:T(8,128)S(1)} %fusion.25.refs_0_), channel_id=1, source_target_pairs={{0,2},{1,3},{2,0},{3,1},{4,6},{5,7},{6,4},{7,5},{8,10},{9,11},{10,... | collective-permute-start | bytes 36872 | tf_op jit(solution)/shard_map/ppermute | solution.py:1398
  261.5 12.8 %collective-permute-start.33 = (f32[8,384]{1,0:T(8,128)S(1)}, f32[8,384]{1,0:T(8,128)}, u32[]{:S(2)}, u32[]{:S(2)}) collective-permute-start(f32[8,384]{1,0:T(8,128)S(1)} %fusion.25.refs_0_), channel_id=1, source_target_pairs={{0,3},{1,0},{2,1},{3,2},{4,7},{5,4},{6,5},{7,6},{8,11},{9,8},{10,9... | collective-permute-start | bytes 36872 | tf_op jit(solution)/shard_map/ppermute | solution.py:1398
  264.4 9.9 %collective-permute-start.38 = (bf16[24,1920]{1,0:T(8,128)(2,1)}, bf16[24,1920]{1,0:T(8,128)(2,1)S(1)}, u32[]{:S(2)}, u32[]{:S(2)}) collective-permute-start(bf16[24,1920]{1,0:T(8,128)(2,1)} %get-tuple-element.230), channel_id=1, source_target_pairs={{0,1},{1,2},{2,3},{3,0},{4,5},{5,6},{6,7},{7,4},{8,9},{9,10},{10,1... | collective-permute-start | bytes 276488 | tf_op jit(solution)/shard_map/ppermute | solution.py:1110
  264.9 9.8 %collective-permute-start.39 = (bf16[24,1920]{1,0:T(8,128)(2,1)S(1)}, bf16[24,1920]{1,0:T(8,128)(2,1)S(1)}, u32[]{:S(2)}, u32[]{:S(2)}) collective-permute-start(bf16[24,1920]{1,0:T(8,128)(2,1)S(1)} %get-tuple-element.231), channel_id=1, source_target_pairs={{0,2},{1,3},{2,0},{3,1},{4,6},{5,7},{6,4},{7,5},{8,10},{9,11},{10,... | collective-permute-start | bytes 276488 | tf_op jit(solution)/shard_map/ppermute | solution.py:1110
  (46 other events, 209.3 us)
